TPU v7x, 256 devices: a whole 4x4x8 slice. The times are simulated.
256 devices in a mesh: tile: 64 (over x, z, core), lev: 4 (over y).
Axes of the slice: x: 4, y: 4, z: 8, core: 2. Of those that a mesh axis runs over, the one named last changes fastest.
Arguments:
- features: bfloat16 [8, 64, 12, 90, 192], P('lev', 'tile'), may hold values from -6 to 6
- attn_gain: float32 [192], replicated, may hold values from 0.5 to 1.5
- w_qkv: bfloat16 [192, 576], replicated, may hold values from -0.4375 to 0.4375
- w_proj: bfloat16 [192, 192], replicated, may hold values from -0.4375 to 0.4375
- window_bias: float32 [6, 144, 144], replicated, may hold values from -6 to 350, as said below
- patterns: int32 [8, 144], replicated, may hold values from 0 to 3
- window_pattern: int32 [4, 960], P(None, 'tile'), may hold values from 0 to 7
- mlp_gain: float32 [192], replicated, may hold values from 0.5 to 1.5
- w_expand: bfloat16 [192, 768], replicated, may hold values from -0.4375 to 0.4375
- w_reduce: bfloat16 [768, 192], replicated, may hold values from -0.21875 to 0.21875
- temp_head: bfloat16 [192], replicated, may hold values from -0.4375 to 0.4375
- temp_base: float32 [8], P('lev'), may hold values from 0.5 to 1.5
- thickness: float32 [8], P('lev'), may hold values from 0.2 to 1
- level_weight: float32 [8], P('lev'), may hold values from 0.5 to 2
- surface: float32 [64, 12, 90], P('tile'), may hold values from -6 to 6
- target: float32 [8, 64, 12, 90], P('lev', 'tile'), may hold values from -12 to 12
Outputs:
- height: float32 [8, 64, 12, 90], P('lev', 'tile')
- grad_features: bfloat16 [8, 64, 12, 90, 192], P('lev', 'tile')
Inputs may be any that keep to these rules, and one draw needn't show every extreme that they name: `window_bias`: the bias that a head adds to the score of a query and key position of a window.
All inputs are finite; a program needn't handle non-finite values.
Results may differ from a plain program's by a relative error of at most 0.023.
Values may be sent and summed in bfloat16 or wider, within the bound.
No kernel may reach another device: no remote copies, remote signals or barrier semaphores. Data moves between devices by JAX's collectives and lax.ppermute only.
A program may use at most 64 MiB of HBM per device.

v0:
```python
import jax
import jax.numpy as jnp
from jax import lax
from jax.sharding import PartitionSpec as P

LAT_DEV = 12
LON_BLOCKS = 4
GROUP = 3


epsilon = 1e-05


def shifted_2(value, axis, steps):
    count = lax.axis_size(axis)
    pairs = [(source, (source + steps) % count) for source in range(count)]
    return lax.ppermute(value, axis, pairs)


def carried_in(shard, axis, combine, identity, reverse):
    count, mine = (lax.axis_size(axis), lax.axis_index(axis))
    everything = lax.all_gather(shard, axis)
    start = jnp.broadcast_to(jnp.asarray(identity, shard.dtype), shard.shape)

    def lap(k, before):
        at = count - 1 - k if reverse else k
        reached = at > mine if reverse else at < mine
        new = combine(before, everything[at])
        return jnp.where(reached, new, before)

    return lax.fori_loop(0, count, lap, start)


def product(form, left, right):
    return jnp.einsum(form, left, right, preferred_element_type=jnp.float32)


def layer_norm(tokens, scale_gain):
    values = tokens.astype(jnp.float32)
    center = jnp.mean(values, axis=-1, keepdims=True)
    spread = jnp.mean(jnp.square(values - center), axis=-1, keepdims=True)
    return ((values - center) * lax.rsqrt(spread + epsilon) * scale_gain).astype(jnp.bfloat16)


def window_block(tokens, labels, weights):
    attn_gain, w_qkv, w_proj, window_bias, mlp_gain, w_expand, w_reduce = weights
    groups, length, channels = tokens.shape
    head_count = window_bias.shape[0]
    head_size = channels // head_count
    token_rows = tokens.reshape(groups * length, channels)
    normed = layer_norm(token_rows, attn_gain)
    projected = jnp.dot(normed, w_qkv, preferred_element_type=jnp.float32)
    queries = (
        (projected[:, :channels] * (1.0 / head_size**0.5))
        .astype(jnp.bfloat16)
        .reshape(groups, length, head_count, head_size)
    )
    key_rows = (
        projected[:, channels : 2 * channels]
        .astype(jnp.bfloat16)
        .reshape(groups, length, head_count, head_size)
    )
    value_rows = (
        projected[:, 2 * channels :]
        .astype(jnp.bfloat16)
        .reshape(groups, length, head_count, head_size)
    )
    scores = product("gqhd,gkhd->ghqk", queries, key_rows) + window_bias[None]
    allowed = labels[:, None, :, None] == labels[:, None, None, :]
    scores = jnp.where(allowed, scores, -1e30)
    scores = scores - jnp.max(scores, axis=-1, keepdims=True)
    raised = jnp.exp(scores)
    attn_weights = (raised / jnp.sum(raised, axis=-1, keepdims=True)).astype(jnp.bfloat16)
    context = (
        product("ghqk,gkhd->gqhd", attn_weights, value_rows)
        .astype(jnp.bfloat16)
        .reshape(groups * length, channels)
    )
    middle = (
        token_rows.astype(jnp.float32)
        + jnp.dot(context, w_proj, preferred_element_type=jnp.float32)
    ).astype(jnp.bfloat16)
    normed_two = layer_norm(middle, mlp_gain)
    expanded = jax.nn.gelu(
        jnp.dot(normed_two, w_expand, preferred_element_type=jnp.float32)
    ).astype(jnp.bfloat16)
    result = (
        middle.astype(jnp.float32) + jnp.dot(expanded, w_reduce, preferred_element_type=jnp.float32)
    ).astype(jnp.bfloat16)
    return result.reshape(groups, length, channels)


def windowed(shifted, window_ids, patterns, weights):
    levels_here, lat_rows, lon_cols, channels = shifted.shape
    level_pairs = levels_here // 2
    band_count = lat_rows // LAT_DEV
    lon_windows = lon_cols // 6
    windows = shifted.reshape(
        level_pairs, 2, band_count, LAT_DEV, lon_windows, 6, channels
    ).transpose(0, 2, 4, 1, 3, 5, 6)
    total_windows = level_pairs * band_count * lon_windows
    windows = windows.reshape(total_windows // GROUP, GROUP, 2 * LAT_DEV * 6, channels)
    choose = (
        window_ids.reshape(-1)[:, None] == jnp.arange(patterns.shape[0], dtype=jnp.int32)[None, :]
    ).astype(jnp.int32)
    labels = jnp.sum(choose[:, :, None] * patterns[None], axis=1).reshape(
        total_windows // GROUP, GROUP, -1
    )
    runner = jax.checkpoint(lambda packed: window_block(packed[0], packed[1], weights))
    outcome = lax.map(runner, (windows, labels))
    outcome = outcome.reshape(
        level_pairs, band_count, lon_windows, 2, LAT_DEV, 6, channels
    ).transpose(0, 3, 1, 4, 2, 5, 6)
    return outcome.reshape(levels_here, lat_rows, lon_cols, channels)


def edge_strips(field, direction, lat_move, next_move, wrap_move):
    half = field.shape[1] // 2
    if direction < 0:
        field = jnp.concatenate([field[:, half:], lat_move(field[:, :half])], axis=1)
        border = field[:, :, :3]
    else:
        field = jnp.concatenate([lat_move(field[:, half:]), field[:, :half]], axis=1)
        border = field[:, :, -3:]
    near = next_move(border)
    far = wrap_move(border)
    block = lax.axis_index("tile") % LON_BLOCKS
    edge = block == (LON_BLOCKS - 1 if direction < 0 else 0)
    arrived = jnp.where(edge, far, near)
    if direction < 0:
        return jnp.concatenate([field[:, :, 3:], arrived], axis=2)
    return jnp.concatenate([arrived, field[:, :, :-3]], axis=2)


def level_step(field, direction, level_move):
    outgoing = field[0] if direction < 0 else field[1]
    incoming = level_move(outgoing)
    if direction < 0:
        return jnp.stack([field[1], incoming])
    return jnp.stack([incoming, field[0]])


def rotate_tokens(tokens, direction):
    band_step = LON_BLOCKS * direction
    wrap_step = -(LON_BLOCKS - 1) * direction
    tokens = edge_strips(
        tokens,
        direction,
        lambda part: shifted_2(part, "tile", band_step),
        lambda part: shifted_2(part, "tile", direction),
        lambda part: shifted_2(part, "tile", wrap_step),
    )
    return level_step(tokens, direction, lambda part: shifted_2(part, "lev", direction))


def on_device(
    features,
    attn_gain,
    w_qkv,
    w_proj,
    window_bias,
    patterns,
    window_pattern,
    mlp_gain,
    w_expand,
    w_reduce,
    temp_head,
    temp_base,
    thickness,
    level_weight,
    surface,
    target,
):
    weights = (attn_gain, w_qkv, w_proj, window_bias, mlp_gain, w_expand, w_reduce)
    lev_index = lax.axis_index("lev")
    window_ids = lax.dynamic_slice_in_dim(window_pattern, lev_index, 1, 0)
    rolled = rotate_tokens(features[:, 0], -1)
    rolled_out, pullback = jax.vjp(
        lambda inputs: windowed(inputs, window_ids, patterns, weights), rolled
    )
    output = rotate_tokens(rolled_out, 1)
    temp_delta = jnp.dot(output, temp_head, preferred_element_type=jnp.float32)
    temps = temp_base[:, None, None] + temp_delta
    layer_thick = thickness[:, None, None] * temps
    zeros_plane = jnp.zeros(layer_thick.shape[1:], jnp.float32)
    below = carried_in(jnp.sum(layer_thick, axis=0), "lev", jnp.add, zeros_plane, False)
    height = surface[0][None] + below[None] + jnp.cumsum(layer_thick, axis=0)
    misfit = level_weight[:, None, None] * (height - target[:, 0])
    above = carried_in(jnp.sum(misfit, axis=0), "lev", jnp.add, zeros_plane, True)
    carried = above[None] + jnp.flip(jnp.cumsum(jnp.flip(misfit, 0), axis=0), 0)
    grad_temp = thickness[:, None, None] * carried
    grad_output = (grad_temp[..., None] * temp_head.astype(jnp.float32)).astype(jnp.bfloat16)
    grad_in = rotate_tokens(grad_output, -1)
    (grad_rolled,) = pullback(grad_in)
    return (height[:, None], rotate_tokens(grad_rolled, 1)[:, None])


def solution(mesh):
    placed = (
        P("lev", "tile", None, None, None),
        P(),
        P(),
        P(),
        P(),
        P(),
        P(None, "tile"),
        P(),
        P(),
        P(),
        P(),
        P("lev"),
        P("lev"),
        P("lev"),
        P("tile", None, None),
        P("lev", "tile", None, None),
    )
    return jax.shard_map(
        on_device,
        mesh=mesh,
        in_specs=placed,
        out_specs=(P("lev", "tile", None, None), P("lev", "tile", None, None, None)),
        check_vma=False,
    )
```

profile of v0, /device:TPU:1, one launch (start us, length us, event | category | flops | bytes accessed | tf_op | source)
XLA Modules:
  0.0 610.7 jit_solution(13608134303265864203)
XLA Ops:
  2.8 9.1 %collective-permute-start = (bf16[2,6,90,192]{3,0,2,1:T(2,128)(2,1)S(1)}, bf16[2,6,90,192]{3,0,2,1:T(2,128)(2,1)S(1)}, u32[]{:S(2)}, u32[]{:S(2)}) collective-permute-start(bf16[2,6,90,192]{3,0,2,1:T(2,128)(2,1)S(1)} %copy.308), channel_id=1, source_target_pairs={{0,240},{4,244},{8,248},{12,252},{16,0},{20,4},{24,8},{28,12},{32,... | collective-permute-start | bytes 1244168 | tf_op jit(solution)/shard_map/ppermute | solution.py:17
  11.9 23.4 %collective-permute-done = bf16[2,6,90,192]{3,0,2,1:T(2,128)(2,1)S(1)} collective-permute-done((bf16[2,6,90,192]{3,0,2,1:T(2,128)(2,1)S(1)}, bf16[2,6,90,192]{3,0,2,1:T(2,128)(2,1)S(1)}, u32[]{:S(2)}, u32[]{:S(2)}) %collective-permute-start) | collective-permute-done | bytes 414752 | tf_op jit(solution)/shard_map/ppermute | solution.py:17
  37.1 5.1 collective-permute-done.1
  43.4 2.9 collective-permute-start.3
  47.9 8.7 %collective-permute-done.3 = bf16[12,90,192]{2,1,0:T(8,128)(2,1)} collective-permute-done((bf16[12,90,192]{2,1,0:T(8,128)(2,1)}, bf16[12,90,192]{2,1,0:T(8,128)(2,1)}, u32[]{:S(2)}, u32[]{:S(2)}) %collective-permute-start.3) | collective-permute-done | bytes 414752 | tf_op jit(solution)/shard_map/ppermute | solution.py:17
  61.1 93.7 %while.56 = (s32[]{:T(128)}, bf16[5,3,144,192]{3,2,1,0:T(8,128)(2,1)}, bf16[5,3,144,192]{3,2,1,0:T(8,128)(2,1)}, f32[1,192]{1,0:T(1,128)}, bf16[192,576]{1,0:T(8...) while((s32[]{:T(128)}, ...), condition=%wide.region_8.9_spmd, body=%wide.region_1.8_spmd.sunk | while | flops 437758720 | bytes 18483904 | solution.py:110
  159.7 2.9 collective-permute-start.4
  162.6 22.4 %collective-permute-done.4 = bf16[2,6,90,192]{3,0,2,1:T(2,128)(2,1)S(1)} collective-permute-done((bf16[2,6,90,192]{3,0,2,1:T(2,128)(2,1)S(1)}, bf16[2,6,90,192]{3,0,2,1:T(2,128)(2,1)S(1)}, u32[]{:S(2)}, u32[]{:S(2)}) %collective-permute-start.4) | collective-permute-done | bytes 414752 | tf_op jit(solution)/shard_map/ppermute | solution.py:17
  185.0 7.0 %collective-permute-start.6 = (bf16[2,12,3,192]{3,0,2,1:T(2,128)(2,1)S(1)}, bf16[2,12,3,192]{3,0,2,1:T(2,128)(2,1)S(1)}, u32[]{:S(2)}, u32[]{:S(2)}) collective-permute-start(bf16[2,12,3,192]{3,0,2,1:T(2,128)(2,1)S(1)} %pad_maximum_fusion.8), channel_id=1, source_target_pairs={{0,4},{4,8},{8,12},{12,16},{16,20},{20,24},{24,28},{28,32},{32,36}... | collective-permute-start | bytes 82952 | tf_op jit(solution)/shard_map/ppermute | solution.py:17
  193.7 3.1 collective-permute-done.5
  201.2 16.6 %collective-permute-done.7 = bf16[12,90,192]{2,1,0:T(8,128)(2,1)} collective-permute-done((bf16[12,90,192]{2,1,0:T(8,128)(2,1)S(1)}, bf16[12,90,192]{2,1,0:T(8,128)(2,1)}, u32[]{:S(2)}, u32[]{:S(2)}) %collective-permute-start.7) | collective-permute-done | bytes 414752 | tf_op jit(solution)/shard_map/ppermute | solution.py:17
  219.7 2.7 pad_maximum_fusion.2
  223.2 9.0 %all-gather.2 = f32[4,12,90]{2,1,0:T(8,128)S(1)} all-gather(f32[1,12,90]{2,1,0:T(8,128)S(1)} %bitcast.223), channel_id=2, replica_groups=mesh['tile'=64,'lev'=4] {'lev'}, dimensions={0}, use_global_device_ids=true | all-gather | bytes 21600 | tf_op jit(solution)/shard_map/all_gather | solution.py:22
  233.0 9.0 %all-gather.3 = f32[4,12,90]{2,1,0:T(8,128)S(1)} all-gather(f32[1,12,90]{2,1,0:T(8,128)S(1)} %bitcast.222), channel_id=3, replica_groups=mesh['tile'=64,'lev'=4] {'lev'}, dimensions={0}, use_global_device_ids=true | all-gather | bytes 21600 | tf_op jit(solution)/shard_map/all_gather | solution.py:22
  244.2 15.6 %collective-permute-done.8 = bf16[2,6,90,192]{3,0,2,1:T(2,128)(2,1)S(1)} collective-permute-done((bf16[2,6,90,192]{3,0,2,1:T(2,128)(2,1)S(1)}, bf16[2,6,90,192]{3,0,2,1:T(2,128)(2,1)S(1)}, u32[]{:S(2)}, u32[]{:S(2)}) %collective-permute-start.8) | collective-permute-done | bytes 414752 | tf_op jit(solution)/shard_map/ppermute | solution.py:17
  259.9 10.6 %collective-permute-start.9 = (bf16[2,12,3,192]{3,2,1,0:T(4,128)(2,1)S(1)}, bf16[2,12,3,192]{3,2,1,0:T(4,128)(2,1)S(1)}, u32[]{:S(2)}, u32[]{:S(2)}) collective-permute-start(bf16[2,12,3,192]{3,2,1,0:T(4,128)(2,1)S(1)} %pad_maximum_fusion.5), channel_id=1, source_target_pairs={{0,12},{4,16},{8,20},{12,24},{16,28},{20,32},{24,36},{28,40},{32,4... | collective-permute-start | bytes 82952 | tf_op jit(solution)/shard_map/ppermute | solution.py:17
  271.8 7.3 %collective-permute-done.9 = bf16[2,12,3,192]{3,2,1,0:T(4,128)(2,1)S(1)} collective-permute-done((bf16[2,12,3,192]{3,2,1,0:T(4,128)(2,1)S(1)}, bf16[2,12,3,192]{3,2,1,0:T(4,128)(2,1)S(1)}, u32[]{:S(2)}, u32[]{:S(2)}) %collective-permute-start.9) | collective-permute-done | bytes 27680 | tf_op jit(solution)/shard_map/ppermute | solution.py:17
  281.2 13.1 %collective-permute-done.11 = bf16[12,90,192]{2,1,0:T(8,128)(2,1)} collective-permute-done((bf16[12,90,192]{2,1,0:T(8,128)(2,1)S(1)}, bf16[12,90,192]{2,1,0:T(8,128)(2,1)}, u32[]{:S(2)}, u32[]{:S(2)}) %collective-permute-start.11) | collective-permute-done | bytes 414752 | tf_op jit(solution)/shard_map/ppermute | solution.py:17
  298.9 251.7 %while.57 = (s32[]{:T(128)}, bf16[5,3,144,192]{3,2,1,0:T(8,128)(2,1)}, bf16[5,3,144,192]{3,2,1,0:T(8,128)(2,1)}, s32[5,3,144]{2,1,0:T(4,128)}, bf16[5,3,144,192]...) while((s32[]{:T(128)}, ...), condition=%wide.region_33.34_spmd, body=%wide.region_17.33_spmd.sunk | while | flops 807986752 | bytes 59676872 | solution.py:110
  313.5 2.7 convert_reduce_fusion.8
  323.3 4.3 multiply_reduce_fusion.23
  363.7 2.7 convert_reduce_fusion.8
  373.6 4.3 multiply_reduce_fusion.23
  414.0 2.7 convert_reduce_fusion.8
  423.9 4.3 multiply_reduce_fusion.23
  464.3 2.7 convert_reduce_fusion.8
  474.1 4.3 multiply_reduce_fusion.23
  514.6 2.7 convert_reduce_fusion.8
  524.4 4.3 multiply_reduce_fusion.23
  555.5 29.3 %collective-permute-done.12 = bf16[2,6,90,192]{3,0,2,1:T(2,128)(2,1)S(1)} collective-permute-done((bf16[2,6,90,192]{3,0,2,1:T(2,128)(2,1)S(1)}, bf16[2,6,90,192]{3,0,2,1:T(2,128)(2,1)S(1)}, u32[]{:S(2)}, u32[]{:S(2)}) %collective-permute-start.12) | collective-permute-done | bytes 414752 | tf_op jit(solution)/shard_map/ppermute | solution.py:17
  594.6 11.3 %collective-permute-done.15 = bf16[12,90,192]{2,1,0:T(8,128)(2,1)S(1)} collective-permute-done((bf16[12,90,192]{2,1,0:T(8,128)(2,1)S(1)}, bf16[12,90,192]{2,1,0:T(8,128)(2,1)S(1)}, u32[]{:S(2)}, u32[]{:S(2)}) %collective-permute-start.15) | collective-permute-done | bytes 414752 | tf_op jit(solution)/shard_map/ppermute | solution.py:17
  606.7 3.7 maximum_bitcast_fusion.2
  (923 shorter events, 358.3 us)
Async XLA Ops:
  0.6 45.7 %copy-start = (s32[4,15]{1,0:T(4,128)S(1)}, s32[4,15]{1,0:T(4,128)}, u32[]{:S(2)}) copy-start(s32[4,15]{1,0:T(4,128)} %param.30) | copy-start | bytes 724
  2.8 32.5 %collective-permute-start = (bf16[2,6,90,192]{3,0,2,1:T(2,128)(2,1)S(1)}, bf16[2,6,90,192]{3,0,2,1:T(2,128)(2,1)S(1)}, u32[]{:S(2)}, u32[]{:S(2)}) collective-permute-start(bf16[2,6,90,192]{3,0,2,1:T(2,128)(2,1)S(1)} %copy.308), channel_id=1, source_target_pairs={{0,240},{4,244},{8,248},{12,252},{16,0},{20,4},{24,8},{28,12},{32,... | collective-permute-start | bytes 1244168 | tf_op jit(solution)/shard_map/ppermute | solution.py:17
  35.4 6.9 %collective-permute-start.1 = (bf16[2,12,3,192]{3,2,1,0:T(4,128)(2,1)S(1)}, bf16[2,12,3,192]{3,2,1,0:T(4,128)(2,1)S(1)}, u32[]{:S(2)}, u32[]{:S(2)}) collective-permute-start(bf16[2,12,3,192]{3,2,1,0:T(4,128)(2,1)S(1)} %pad_maximum_fusion.6), channel_id=1, source_target_pairs={{0,12},{4,16},{8,20},{12,24},{16,28},{20,32},{24,36},{28,40},{32,4... | collective-permute-start | bytes 82952 | tf_op jit(solution)/shard_map/ppermute | solution.py:17
  36.3 6.0 collective-permute-start.2
  37.1 9.3 %copy-start.41 = (s32[8,144]{1,0:T(8,128)S(1)}, s32[8,144]{1,0:T(8,128)}, u32[]{:S(2)}) copy-start(s32[8,144]{1,0:T(8,128)} %param.29) | copy-start | bytes 13828
  37.1 10.0 %copy-start.29 = (f32[6,144,144]{2,1,0:T(8,128)S(1)}, f32[6,144,144]{2,1,0:T(8,128)}, u32[]{:S(2)}) copy-start(f32[6,144,144]{2,1,0:T(8,128)} %param.28) | copy-start | bytes 1492996
  43.4 13.1 %collective-permute-start.3 = (bf16[12,90,192]{2,1,0:T(8,128)(2,1)}, bf16[12,90,192]{2,1,0:T(8,128)(2,1)}, u32[]{:S(2)}, u32[]{:S(2)}) collective-permute-start(bf16[12,90,192]{2,1,0:T(8,128)(2,1)} %get-tuple-element.802), channel_id=1, source_target_pairs={{0,3},{1,0},{2,1},{3,2},{4,7},{5,4},{6,5},{7,6},{8,11},{9,8},{10,9... | collective-permute-start | bytes 1244168 | tf_op jit(solution)/shard_map/ppermute | solution.py:17
  159.7 25.2 %collective-permute-start.4 = (bf16[2,6,90,192]{3,0,2,1:T(2,128)(2,1)S(1)}, bf16[2,6,90,192]{3,0,2,1:T(2,128)(2,1)S(1)}, u32[]{:S(2)}, u32[]{:S(2)}) collective-permute-start(bf16[2,6,90,192]{3,0,2,1:T(2,128)(2,1)S(1)} %get-tuple-element.809), channel_id=1, source_target_pairs={{0,16},{4,20},{8,24},{12,28},{16,32},{20,36},{24,40},{28,44},{32,4... | collective-permute-start | bytes 1244168 | tf_op jit(solution)/shard_map/ppermute | solution.py:17
  185.0 8.7 %collective-permute-start.6 = (bf16[2,12,3,192]{3,0,2,1:T(2,128)(2,1)S(1)}, bf16[2,12,3,192]{3,0,2,1:T(2,128)(2,1)S(1)}, u32[]{:S(2)}, u32[]{:S(2)}) collective-permute-start(bf16[2,12,3,192]{3,0,2,1:T(2,128)(2,1)S(1)} %pad_maximum_fusion.8), channel_id=1, source_target_pairs={{0,4},{4,8},{8,12},{12,16},{16,20},{20,24},{24,28},{28,32},{32,36}... | collective-permute-start | bytes 82952 | tf_op jit(solution)/shard_map/ppermute | solution.py:17
  192.0 4.8 collective-permute-start.5
  200.4 17.3 %collective-permute-start.7 = (bf16[12,90,192]{2,1,0:T(8,128)(2,1)S(1)}, bf16[12,90,192]{2,1,0:T(8,128)(2,1)}, u32[]{:S(2)}, u32[]{:S(2)}) collective-permute-start(bf16[12,90,192]{2,1,0:T(8,128)(2,1)S(1)} %bitcast.219), channel_id=1, source_target_pairs={{0,1},{1,2},{2,3},{3,0},{4,5},{5,6},{6,7},{7,4},{8,9},{9,10},{10,1... | collective-permute-start | bytes 1244168 | tf_op jit(solution)/shard_map/ppermute | solution.py:17
  222.4 9.9 %copy-start.42 = (f32[1,12,90]{2,0,1:T(1,128)S(1)}, f32[1,12,90]{2,0,1:T(1,128)}, u32[]{:S(2)}) copy-start(f32[1,12,90]{2,0,1:T(1,128)} %param.38) | copy-start | bytes 12964
  222.5 9.9 %copy-start.40 = (f32[2,1,12,90]{3,1,2,0:T(1,128)S(1)}, f32[2,1,12,90]{3,1,2,0:T(1,128)}, u32[]{:S(2)}) copy-start(f32[2,1,12,90]{3,1,2,0:T(1,128)} %param.39) | copy-start | bytes 25924
  222.5 9.9 %copy-start.45 = (f32[2]{0:T(128)S(1)}, f32[2]{0:T(128)}, u32[]{:S(2)}) copy-start(f32[2]{0:T(128)} %param.37) | copy-start | bytes 28
  243.3 16.5 %collective-permute-start.8 = (bf16[2,6,90,192]{3,0,2,1:T(2,128)(2,1)S(1)}, bf16[2,6,90,192]{3,0,2,1:T(2,128)(2,1)S(1)}, u32[]{:S(2)}, u32[]{:S(2)}) collective-permute-start(bf16[2,6,90,192]{3,0,2,1:T(2,128)(2,1)S(1)} %copy.317), channel_id=1, source_target_pairs={{0,240},{4,244},{8,248},{12,252},{16,0},{20,4},{24,8},{28,12},{32,... | collective-permute-start | bytes 1244168 | tf_op jit(solution)/shard_map/ppermute | solution.py:17
  259.9 19.2 %collective-permute-start.9 = (bf16[2,12,3,192]{3,2,1,0:T(4,128)(2,1)S(1)}, bf16[2,12,3,192]{3,2,1,0:T(4,128)(2,1)S(1)}, u32[]{:S(2)}, u32[]{:S(2)}) collective-permute-start(bf16[2,12,3,192]{3,2,1,0:T(4,128)(2,1)S(1)} %pad_maximum_fusion.5), channel_id=1, source_target_pairs={{0,12},{4,16},{8,20},{12,24},{16,28},{20,32},{24,36},{28,40},{32,4... | collective-permute-start | bytes 82952 | tf_op jit(solution)/shard_map/ppermute | solution.py:17
  270.5 8.6 %collective-permute-start.10 = (bf16[2,12,3,192]{3,2,1,0:T(4,128)(2,1)S(1)}, bf16[2,12,3,192]{3,2,1,0:T(4,128)(2,1)S(1)}, u32[]{:S(2)}, u32[]{:S(2)}) collective-permute-start(bf16[2,12,3,192]{3,2,1,0:T(4,128)(2,1)S(1)} %pad_maximum_fusion.5), channel_id=1, source_target_pairs={{0,252},{4,0},{8,4},{12,8},{16,12},{20,16},{24,20},{28,24},{32,28}... | collective-permute-start | bytes 82952 | tf_op jit(solution)/shard_map/ppermute | solution.py:17
  279.4 15.0 %collective-permute-start.11 = (bf16[12,90,192]{2,1,0:T(8,128)(2,1)S(1)}, bf16[12,90,192]{2,1,0:T(8,128)(2,1)}, u32[]{:S(2)}, u32[]{:S(2)}) collective-permute-start(bf16[12,90,192]{2,1,0:T(8,128)(2,1)S(1)} %get-tuple-element.800), channel_id=1, source_target_pairs={{0,3},{1,0},{2,1},{3,2},{4,7},{5,4},{6,5},{7,6},{8,11},{9,8},{10,9... | collective-permute-start | bytes 1244168 | tf_op jit(solution)/shard_map/ppermute | solution.py:17
  299.0 6.5 %copy-start.16 = (bf16[192,576]{1,0:T(8,128)(2,1)}, bf16[192,576]{1,0:T(8,128)(2,1)S(1)}, u32[]{:S(2)}) copy-start(bf16[192,576]{1,0:T(8,128)(2,1)S(1)} %get-tuple-element.1048) | copy-start | bytes 663556 | tf_op jit(solution)/shard_map/transpose(jvp())/while
  301.1 5.6 copy-start.32
  349.3 6.5 %copy-start.16 = (bf16[192,576]{1,0:T(8,128)(2,1)}, bf16[192,576]{1,0:T(8,128)(2,1)S(1)}, u32[]{:S(2)}) copy-start(bf16[192,576]{1,0:T(8,128)(2,1)S(1)} %get-tuple-element.1048) | copy-start | bytes 663556 | tf_op jit(solution)/shard_map/transpose(jvp())/while
  351.4 5.6 copy-start.32
  399.6 6.5 %copy-start.16 = (bf16[192,576]{1,0:T(8,128)(2,1)}, bf16[192,576]{1,0:T(8,128)(2,1)S(1)}, u32[]{:S(2)}) copy-start(bf16[192,576]{1,0:T(8,128)(2,1)S(1)} %get-tuple-element.1048) | copy-start | bytes 663556 | tf_op jit(solution)/shard_map/transpose(jvp())/while
  401.6 5.6 copy-start.32
  449.9 6.5 %copy-start.16 = (bf16[192,576]{1,0:T(8,128)(2,1)}, bf16[192,576]{1,0:T(8,128)(2,1)S(1)}, u32[]{:S(2)}) copy-start(bf16[192,576]{1,0:T(8,128)(2,1)S(1)} %get-tuple-element.1048) | copy-start | bytes 663556 | tf_op jit(solution)/shard_map/transpose(jvp())/while
  451.9 5.6 copy-start.32
  500.1 6.5 %copy-start.16 = (bf16[192,576]{1,0:T(8,128)(2,1)}, bf16[192,576]{1,0:T(8,128)(2,1)S(1)}, u32[]{:S(2)}) copy-start(bf16[192,576]{1,0:T(8,128)(2,1)S(1)} %get-tuple-element.1048) | copy-start | bytes 663556 | tf_op jit(solution)/shard_map/transpose(jvp())/while
  502.2 5.6 copy-start.32
  555.4 29.4 %collective-permute-start.12 = (bf16[2,6,90,192]{3,0,2,1:T(2,128)(2,1)S(1)}, bf16[2,6,90,192]{3,0,2,1:T(2,128)(2,1)S(1)}, u32[]{:S(2)}, u32[]{:S(2)}) collective-permute-start(bf16[2,6,90,192]{3,0,2,1:T(2,128)(2,1)S(1)} %get-tuple-element.805), channel_id=1, source_target_pairs={{0,16},{4,20},{8,24},{12,28},{16,32},{20,36},{24,40},{28,44},{32,4... | collective-permute-start | bytes 1244168 | tf_op jit(solution)/shard_map/ppermute | solution.py:17
  584.9 2.8 collective-permute-start.14
  585.0 4.4 collective-permute-start.13
  593.1 12.8 %collective-permute-start.15 = (bf16[12,90,192]{2,1,0:T(8,128)(2,1)S(1)}, bf16[12,90,192]{2,1,0:T(8,128)(2,1)S(1)}, u32[]{:S(2)}, u32[]{:S(2)}) collective-permute-start(bf16[12,90,192]{2,1,0:T(8,128)(2,1)S(1)} %bitcast.220), channel_id=1, source_target_pairs={{0,1},{1,2},{2,3},{3,0},{4,5},{5,6},{6,7},{7,4},{8,9},{9,10},{10,1... | collective-permute-start | bytes 1244168 | tf_op jit(solution)/shard_map/ppermute | solution.py:17
  (164 other events, 306.1 us)
where the time goes:
time: 621 us; the launch traced here: 611 us
  waiting for transfers between devices  160 us (26%)
  local copies, waits for them, and re-layouts  156 us (25%)
  matrix products  139 us (22%)
  other arithmetic  92.1 us (15%)
  starting transfers between devices  40.9 us (7%)
  blocking collectives  18 us (3%)
    ppermute x16, waiting for transfers between devices, shifted_2(): return lax.ppermute(value, axis, pairs)  160 us
    dot_general x35, matrix products, product(): return jnp.einsum(form, left, right, preferred_element_type=jnp.float32)  48.8 us
    ppermute x16, starting transfers between devices, shifted_2(): return lax.ppermute(value, axis, pairs)  40.9 us
    dot_general x5, matrix products, window_block(): jnp.dot(normed_two, w_expand, preferred_element_type=jnp.float32)  21.7 us
    dot_general x10, matrix products, window_block(): jnp.dot(expanded, w_reduce, preferred_element_type=jnp.float32)  20.7 us
    while x340, local copies, waits for them, and re-layouts  20.6 us
    reshape x15, local copies, waits for them, and re-layouts, window_block(): context = product('ghqk,gkhd->gqhd', attn_weights, value_rows).astype(jnp...  20.2 us
    reduce_sum x10, other arithmetic, window_block(): scores = scores - jnp.max(scores, axis=-1, keepdims=True)  18.9 us
  transfers between devices with their start and end apart: 16, of which 13 were waited for; matrix products, arithmetic and copies ran while one was open for 1% of the time, Pallas kernels for 0%

commit v1 on v0

v1 whole, which is shorter than its diff:
```python
import jax
import jax.numpy as jnp
import numpy as np
from jax import lax
from jax.experimental import pallas as pl
from jax.experimental.pallas import tpu as pltpu
from jax.sharding import PartitionSpec as P

F32 = jnp.float32
BF16 = jnp.bfloat16
C = 192
HEADS = 6
HEAD = 32
FF = 768
WIN = 144
HALF = 72
QUARTER = 36
LONS = 90
SHIFT = 3
BLOCKS = 4
BANDS = 16
LEVS = 4
GROUP = 8
ROWS = 240
WIDE = 896
EPS = 1e-05
VMEM_LIMIT = 56 * 1024 * 1024


def source_rows():
    table = np.zeros((GROUP * HALF, 6 * 112), np.float32)
    for m in range(GROUP * HALF):
        w, r, o = m // QUARTER, (m % QUARTER) // 6, m % 6
        e = 6 * w + o
        if w < 15:
            lon = e + SHIFT
            table[m, 112 * r + (lon if lon < LONS else 96 + lon - LONS)] = 1.0
    return table


def target_rows():
    table = np.zeros((6 * 96, (GROUP + 1) * HALF), np.float32)
    for m in range(GROUP * HALF):
        w, r, o = m // QUARTER, (m % QUARTER) // 6, m % 6
        lon = 6 * w + o + SHIFT
        if w < 15 and lon < LONS:
            table[96 * r + lon, m] = 1.0
    for r in range(6):
        for o in range(3):
            table[96 * r + o, GROUP * HALF + 6 * r + o + 3] = 1.0
    return table


def window_rows():
    table = np.zeros((2 * WIN, 2 * WIN), np.float32)
    for part in range(4):
        for col in range(2):
            for i in range(QUARTER):
                table[col * WIN + part * QUARTER + i, (part * 2 + col) * QUARTER + i] = 1.0
    return table


def dot(a, b):
    return jnp.dot(a, b, preferred_element_type=F32)


def dot_nt(a, b):
    return lax.dot_general(a, b, (((1,), (1,)), ((), ())), preferred_element_type=F32)


def lanes(shape):
    return lax.broadcasted_iota(jnp.int32, shape, len(shape) - 1)


def split3(value):
    top = value.astype(BF16).astype(F32)
    rest = value - top
    middle = rest.astype(BF16).astype(F32)
    return top, middle, rest - middle


def roll(value, steps):
    return pltpu.roll(value, steps % 128, 1)


def pack_block(out_ref, at, first, second, spare):
    lane = lanes((HALF, 128))
    out_ref[at, 0:WIN, :] = jnp.concatenate(first, axis=0).astype(BF16)
    tail = jnp.where(lane < 64, second[0], roll(second[1], 64))
    tail = jnp.concatenate([tail, jnp.zeros((8, 128), F32)], axis=0)
    both = jnp.concatenate(second, axis=0)
    lane16 = lanes((16, 128))
    extra = spare
    for g in range(9):
        moved = roll(both[16 * g : 16 * g + 16], 8 * g - 64)
        extra = jnp.where((lane16 >= 8 * g) & (lane16 < 8 * g + 8), moved, extra)
    out_ref[at, WIN : WIN + 16, :] = extra.astype(BF16)
    out_ref[at, WIN + 16 : ROWS, :] = tail.astype(BF16)


def unpack_block(block):
    first = block[0:WIN].astype(F32)
    extra = block[WIN : WIN + 16].astype(F32)
    tail = block[WIN + 16 : ROWS].astype(F32)[0:HALF]
    lane16 = lanes((16, 128))
    keep = (lane16 >= 64) & (lane16 < 72)
    spread = [jnp.where(keep, roll(extra, 64 - 8 * g), 0.0) for g in range(9)]
    spread = jnp.concatenate(spread, axis=0)
    lane = lanes((HALF, 128))
    second = [
        jnp.where(lane < 64, tail, spread[0:HALF]),
        jnp.where(lane < 64, roll(tail, 64), spread[HALF:WIN]),
    ]
    return first, second, extra


def prep_kernel(
    start_ref, ids_ref, thick_ref, weight_ref, base_ref,
    f_ref, edge_ref, target_ref, surface_ref, perm_ref,
    out_ref, rows_ref, made_ref,
):
    start = start_ref[0]
    rows_ref[...] = jnp.zeros(rows_ref.shape, BF16)
    surf = jnp.where(start == 0, surface_ref[0:6, :], surface_ref[6:12, :])
    lane = lanes((LONS, 128))
    for lev in range(2):
        goal = jnp.where(start == 0, target_ref[lev, 0:6, :], target_ref[lev, 6:12, :])
        values = split3(goal) + split3(surf)
        stacked = []
        for r in range(6):
            stacked += [v[r : r + 1] for v in values]
            stacked.append(jnp.zeros((2, LONS), F32))
        stacked.append(jnp.zeros((128 - 48, LONS), F32))
        columns = jnp.concatenate(stacked, axis=0)
        columns = jnp.concatenate([columns, jnp.zeros((128, 128 - LONS), F32)], axis=1).T
        for r in range(6):
            row = f_ref[lev, start + r]
            second = jnp.concatenate(
                [row[:, 128:].astype(F32), jnp.zeros((LONS, 64), F32)], axis=1
            )
            extra = roll(columns, 64 - 8 * r)[0:LONS]
            second = jnp.where(lane < 64, second, jnp.where(lane < 72, extra, 0.0))
            rows_ref[112 * r : 112 * r + LONS, 0:128] = row[:, 0:128]
            rows_ref[112 * r : 112 * r + LONS, 128:256] = second.astype(BF16)
            rows_ref[112 * r + 96 : 112 * r + 104, :] = edge_ref[lev, start + r]
        made_ref[lev] = dot(perm_ref[...], rows_ref[...])
    lane16 = lanes((16, 128))
    row16 = lax.broadcasted_iota(jnp.int32, (16, 128), 0)
    scalars = jnp.zeros((16, 128), F32)
    for lev in range(2):
        for k, ref in enumerate((thick_ref, weight_ref, base_ref)):
            scalars = jnp.where((row16 == lev) & (lane16 == 72 + k), ref[lev], scalars)
    top, middle, low = split3(scalars)
    scalars = top + roll(middle, 3) + roll(low, 6)
    for d in range(GROUP):
        spare = scalars
        for p in range(4):
            for col in range(2):
                if 2 * d + col < 15:
                    ident = ids_ref[p, 2 * d + col].astype(F32)
                    spare = jnp.where((row16 == 2 + p) & (lane16 == 81 + col), ident, spare)
        at = slice(HALF * d, HALF * d + HALF)
        pack_block(
            out_ref, d,
            [made_ref[lev, at, 0:128] for lev in range(2)],
            [made_ref[lev, at, 128:256] for lev in range(2)],
            spare,
        )


def vmem():
    return pl.BlockSpec(memory_space=pltpu.VMEM)


def smem():
    return pl.BlockSpec(memory_space=pltpu.SMEM)


def prep(start, ids, thick, weight, base, feats, edge, target, surface, perm):
    return pl.pallas_call(
        prep_kernel,
        out_shape=jax.ShapeDtypeStruct((GROUP, ROWS, 128), BF16),
        in_specs=[smem()] * 5 + [vmem()] * 5,
        out_specs=vmem(),
        scratch_shapes=[
            pltpu.VMEM((6 * 112, 256), BF16),
            pltpu.VMEM((2, GROUP * HALF, 256), F32),
        ],
        compiler_params=pltpu.CompilerParams(vmem_limit_bytes=VMEM_LIMIT),
        cost_estimate=pl.CostEstimate(
            flops=3_000_000_000, bytes_accessed=2_500_000, transcendentals=0
        ),
        name="prep",
    )(start, ids, thick, weight, base, feats, edge, target, surface, perm)


def post_kernel(
    lower_ref, a_ref, b_ref, ea_ref, eb_ref, perm_ref, height_ref, grad_ref, rows_ref
):
    lower = lower_ref[0] == 1
    lane = lanes((96, 128))
    for half in range(2):
        for d in range(GROUP + 1):
            one = a_ref[d] if d < GROUP else ea_ref[...]
            two = b_ref[d] if d < GROUP else eb_ref[...]
            take = lower if half == 1 else jnp.logical_not(lower)
            block = jnp.where(take, one, two)
            first, second, _ = unpack_block(block)
            for lev in range(2):
                at = slice(HALF * d, HALF * d + HALF)
                rows_ref[lev, at, 0:128] = first[HALF * lev : HALF * lev + HALF]
                rows_ref[lev, at, 128:256] = second[lev]
        for lev in range(2):
            made = dot(perm_ref[...], rows_ref[lev].astype(BF16))
            columns = jnp.zeros((96, 128), F32)
            for r in range(6):
                grad_ref[lev, 6 * half + r] = made[96 * r : 96 * r + LONS, 0:C].astype(BF16)
                tile = made[96 * r : 96 * r + 96, 128:256]
                total = (tile + roll(tile, -1)) + roll(tile, -2)
                columns = jnp.where(lane == r, roll(total, r - 64), columns)
            columns = columns.T
            height_ref[lev, 6 * half : 6 * half + 6, :] = columns[0:6, 0:LONS]


def post(lower, a, b, ea, eb, perm):
    return pl.pallas_call(
        post_kernel,
        out_shape=(
            jax.ShapeDtypeStruct((2, 12, LONS), F32),
            jax.ShapeDtypeStruct((2, 12, LONS, C), BF16),
        ),
        in_specs=[smem()] + [vmem()] * 5,
        out_specs=(vmem(), vmem()),
        scratch_shapes=[pltpu.VMEM((2, (GROUP + 1) * HALF, 256), F32)],
        compiler_params=pltpu.CompilerParams(vmem_limit_bytes=VMEM_LIMIT),
        cost_estimate=pl.CostEstimate(
            flops=3_000_000_000, bytes_accessed=2_500_000, transcendentals=0
        ),
        name="post",
    )(lower, a, b, ea, eb, perm)


def norm_parts(x):
    center = jnp.sum(x, axis=-1, keepdims=True) * (1.0 / C)
    moved = x - center
    spread = jnp.sum(moved * moved, axis=-1, keepdims=True) * (1.0 / C)
    scale = lax.rsqrt(spread + EPS)
    return moved * scale, scale


def norm_back(cotangent, hat, scale):
    mean = jnp.sum(cotangent, axis=-1, keepdims=True) * (1.0 / C)
    along = jnp.sum(cotangent * hat, axis=-1, keepdims=True) * (1.0 / C)
    return scale * (cotangent - mean - hat * along)


def fill_diagonal(ref, turned):
    lane = lanes((HEAD, 128))
    for h in range(HEADS):
        rows = slice(HEAD * h, HEAD * h + HEAD)
        ref[rows, 128 * h : 128 * h + 128] = turned[rows, 0:128].astype(BF16)
        tail = jnp.concatenate([turned[rows, 128:WIN], jnp.zeros((HEAD, 112), F32)], axis=1)
        tail = roll(tail, 16 * h)
        tail = jnp.where((lane >= 16 * h) & (lane < 16 * h + 16), tail, 0.0)
        ref[rows, 768:WIDE] = tail.astype(BF16)


def gather_heads(turned, weights):
    main = [
        dot(turned[HEAD * h : HEAD * h + HEAD], weights[:, 128 * h : 128 * h + 128])
        for h in range(HEADS)
    ]
    main = jnp.concatenate(main, axis=0).T
    tail = dot(turned, weights[:, 768:WIDE]).T
    lane = lanes((16, C))
    last = jnp.zeros((16, C), F32)
    for h in range(HEADS):
        mine = (lane >= HEAD * h) & (lane < HEAD * h + HEAD)
        last = jnp.where(mine, tail[16 * h : 16 * h + 16], last)
    return jnp.concatenate([main, last], axis=0)


def head_rows(value):
    lane = lanes((WIN, C))
    parts, tails = [], []
    for h in range(HEADS):
        mine = jnp.where((lane >= HEAD * h) & (lane < HEAD * h + HEAD), value, 0.0).astype(BF16)
        parts.append(mine[0:128])
        tails.append(mine[128:WIN])
    return jnp.concatenate(parts + tails + [jnp.zeros((32, C), BF16)], axis=0)


def main_kernel(
    x_ref, order_ref, back_ref, w_ref, wt_ref, proj_ref, projt_ref, expand_ref, expandt_ref,
    reduce_ref, bias_ref, pat_q_ref, pat_k_ref, gains_ref,
    out_ref,
    tok_in, tok, diag_q, diag_n, probs, dscores, q_rows, n_rows, dq_rows, resid, hats, scales,
    deltas, source, heights, levels_ref, made,
):
    scale_q = 1.0 / HEAD**0.5
    lane72 = lanes((HALF, 128))
    for s in range(GROUP):
        first, second, extra = unpack_block(x_ref[s])
        tok_in[s, :, 0:128] = first
        tok_in[s, 0:HALF, 128:256] = second[0]
        tok_in[s, HALF:WIN, 128:256] = second[1]
        if s < 4:
            whole = (extra + roll(extra, -3)) + roll(extra, -6)
            lane16 = lanes((16, 128))
            levels_ref[s] = jnp.where(lane16 < 75, whole, extra)
    diag_q[...] = jnp.zeros(diag_q.shape, BF16)
    diag_n[...] = jnp.zeros(diag_n.shape, BF16)

    def place(p, part):
        a, beta = part // 2, part % 2
        return beta * 4 + (p + a) % 4, (HALF if a == 0 else 0)

    for p in range(4):
        pieces = []
        for part in range(4):
            s, at = place(p, part)
            pieces.append(tok_in[s, at : at + HALF, :])
        moved = dot(order_ref[...], jnp.concatenate(pieces, axis=0).astype(BF16))
        tok[2 * p] = moved[0:WIN]
        tok[2 * p + 1] = moved[WIN : 2 * WIN]

    gain_one = gains_ref[0:1, 0:C]
    gain_two = gains_ref[1:2, 0:C]
    head_row = gains_ref[2:3, 0:C]
    head_eight = jnp.broadcast_to(head_row, (8, C)).astype(BF16)
    u_row = dot_nt(head_eight, reduce_ref[...])[0:1]

    def forward(i, carry):
        p = i // 2
        col = i - 2 * p
        x = tok[i, :, 0:C]
        hat, scale = norm_parts(x)
        normed = (hat * gain_one).astype(BF16)
        hats[i] = hat
        scales[i] = jnp.broadcast_to(scale, (WIN, 128))
        turned = dot_nt(wt_ref[...], normed)
        queries = (dot(normed, w_ref[0]) * scale_q).astype(BF16)
        keys = dot(normed, w_ref[1]).astype(BF16)
        values = dot(normed, w_ref[2]).astype(BF16)
        q_rows[i] = queries
        fill_diagonal(diag_q, turned[0:C] * scale_q)
        keys_t = turned[C : 2 * C].astype(BF16)
        values_t = turned[2 * C : 3 * C].astype(BF16)
        scores = dot(keys, diag_q[...]) + bias_ref[...]
        idents = levels_ref[0]
        lane16 = lanes((16, 128))
        row16 = lax.broadcasted_iota(jnp.int32, (16, 128), 0)
        spot = (row16 == 2 + p) & (lane16 == 81 + col)
        ident = jnp.sum(jnp.where(spot, idents, 0.0), axis=0, keepdims=True)
        ident = jnp.sum(ident, axis=1, keepdims=True)
        row8 = lax.broadcasted_iota(jnp.int32, (8, 1), 0).astype(F32)
        label_q = jnp.sum(jnp.where(row8 == ident, pat_q_ref[...], 0.0), axis=0, keepdims=True)
        lane8 = lanes((1, 8)).astype(F32)
        label_k = jnp.sum(jnp.where(lane8 == ident, pat_k_ref[...], 0.0), axis=1, keepdims=True)
        scores = jnp.where(label_k == label_q, scores, -1e30)
        raised = jnp.exp(scores - jnp.max(scores, axis=0, keepdims=True))
        weights = (raised * (1.0 / jnp.sum(raised, axis=0, keepdims=True))).astype(BF16)
        probs[i] = weights
        context = gather_heads(values_t, weights).astype(BF16)
        middle = (x + dot(context, proj_ref[...])).astype(BF16).astype(F32)
        hat_two, scale_two = norm_parts(middle)
        normed_two = (hat_two * gain_two).astype(BF16)
        acc = jnp.zeros((WIN, 256), F32)
        back = jnp.zeros((WIN, C), F32)
        for f in range(3):
            at = slice(256 * f, 256 * f + 256)
            pre = dot(normed_two, expand_ref[:, at])
            u = u_row[:, at]
            square = pre * pre
            c0 = 0.7978845608028654
            wave = jnp.tanh(pre * (c0 + (c0 * 0.044715) * square))
            half = 0.5 * pre
            acc = acc + (half + half * wave) * u
            slope = (0.5 + 0.5 * wave) + half * (1.0 - wave * wave) * (
                c0 + (3.0 * c0 * 0.044715) * square
            )
            back = back + dot((slope * u).astype(BF16), expandt_ref[at, :])
        delta = jnp.sum(acc, axis=1, keepdims=True) + jnp.sum(
            middle * head_row, axis=1, keepdims=True
        )
        deltas[i] = jnp.broadcast_to(delta, (WIN, 128))
        kept = head_row + norm_back(back * gain_two, hat_two, scale_two)
        resid[i] = kept
        kept = kept.astype(BF16)
        fill_diagonal(diag_n, dot_nt(proj_ref[...], kept))
        n_rows[i] = dot(kept, projt_ref[...]).astype(BF16)
        dweights = dot(values, diag_n[...])
        weights = weights.astype(F32)
        inner = jnp.sum(weights * dweights, axis=0, keepdims=True)
        dscore = (weights * (dweights - inner)).astype(BF16)
        dscores[i] = dscore
        dq_rows[i] = gather_heads(keys_t, dscore)
        return carry

    lax.fori_loop(0, 8, forward, 0)

    def scalar(l, k):
        return levels_ref[l // 2, l % 2 : l % 2 + 1, 72 + k : 73 + k]

    for col in range(2):
        total = jnp.zeros((HALF, 128), F32)
        misfits, spots = [], []
        for l in range(8):
            a = 1 - l % 2
            i = 2 * ((l // 2 - a) % 4) + col
            rows = slice(HALF * a, HALF * a + HALF)
            spots.append((i, rows))
            extra = tok[i, rows, 128:256]
            goal = (extra[:, 64:65] + extra[:, 65:66]) + extra[:, 66:67]
            ground = (extra[:, 67:68] + extra[:, 68:69]) + extra[:, 69:70]
            temps = scalar(l, 2) + deltas[i, rows, :]
            total = total + scalar(l, 0) * temps
            height = ground + total
            misfits.append(scalar(l, 1) * (height - goal))
            top, middle, low = split3(height)
            heights[i, rows, :] = jnp.where(
                lane72 == 64, top, jnp.where(lane72 == 65, middle, low)
            )
        carried = jnp.zeros((HALF, 128), F32)
        for l in reversed(range(8)):
            i, rows = spots[l]
            carried = carried + misfits[l]
            source[i, rows, :] = scalar(l, 0) * carried

    def backward(i, carry):
        s = source[i, :, 0:1]
        dk = dot(dscores[i], head_rows(s * q_rows[i].astype(F32))).astype(BF16)
        dv = dot(probs[i], head_rows(s * n_rows[i].astype(F32))).astype(BF16)
        dq = ((s * scale_q) * dq_rows[i]).astype(BF16)
        dnormed = (
            dot(dq, wt_ref[0:C, :]) + dot(dk, wt_ref[C : 2 * C, :]) + dot(dv, wt_ref[2 * C :, :])
        )
        dx = norm_back(dnormed * gain_one, hats[i], scales[i, :, 0:1])
        grad = s * resid[i] + dx
        lane = lanes((WIN, 128))
        last = jnp.concatenate([grad[:, 128:C], jnp.zeros((WIN, 64), F32)], axis=1)
        last = jnp.where(lane < 64, last, jnp.where(lane < 67, heights[i], 0.0))
        made[i, :, 0:128] = grad[:, 0:128].astype(BF16)
        made[i, :, 128:256] = last.astype(BF16)
        return carry

    lax.fori_loop(0, 8, backward, 0)

    for p in range(4):
        moved = dot(back_ref[...], jnp.concatenate([made[2 * p], made[2 * p + 1]], axis=0))
        for part in range(4):
            s, at = place(p, part)
            tok_in[s, at : at + HALF, :] = moved[HALF * part : HALF * part + HALF]
    zero = jnp.zeros((16, 128), F32)
    for s in range(GROUP):
        pack_block(
            out_ref, s,
            [tok_in[s, HALF * k : HALF * k + HALF, 0:128] for k in range(2)],
            [tok_in[s, HALF * k : HALF * k + HALF, 128:256] for k in range(2)],
            zero,
        )


def layer(x, consts):
    return pl.pallas_call(
        main_kernel,
        out_shape=jax.ShapeDtypeStruct((GROUP, ROWS, 128), BF16),
        in_specs=[vmem()] * (1 + len(consts)),
        out_specs=vmem(),
        scratch_shapes=[
            pltpu.VMEM((GROUP, WIN, 256), F32),
            pltpu.VMEM((8, WIN, 256), F32),
            pltpu.VMEM((C, WIDE), BF16),
            pltpu.VMEM((C, WIDE), BF16),
            pltpu.VMEM((8, WIN, WIDE), BF16),
            pltpu.VMEM((8, WIN, WIDE), BF16),
            pltpu.VMEM((8, WIN, C), BF16),
            pltpu.VMEM((8, WIN, C), BF16),
            pltpu.VMEM((8, WIN, C), F32),
            pltpu.VMEM((8, WIN, C), F32),
            pltpu.VMEM((8, WIN, C), F32),
            pltpu.VMEM((8, WIN, 128), F32),
            pltpu.VMEM((8, WIN, 128), F32),
            pltpu.VMEM((8, WIN, 128), F32),
            pltpu.VMEM((8, WIN, 128), F32),
            pltpu.VMEM((4, 16, 128), F32),
            pltpu.VMEM((8, WIN, 256), BF16),
        ],
        compiler_params=pltpu.CompilerParams(vmem_limit_bytes=VMEM_LIMIT),
        cost_estimate=pl.CostEstimate(
            flops=20_000_000_000, bytes_accessed=4_000_000, transcendentals=3_000_000
        ),
        name="layer",
    )(x, *consts)


def pair_groups(odd):
    out = []
    for block in range(BLOCKS):
        for band in range(odd, BANDS, 2):
            members = (band, (band + 1) % BANDS)
            out.append(
                [(b * BLOCKS + block) * LEVS + lev for b in members for lev in range(LEVS)]
            )
    return out


def exchange(blocks, odd):
    return lax.all_to_all(
        blocks, ("tile", "lev"), 0, 0, axis_index_groups=pair_groups(odd)
    )


def block_step(value, steps):
    pairs = [
        (t, t - t % BLOCKS + (t + steps) % BLOCKS) for t in range(BANDS * BLOCKS)
    ]
    return lax.ppermute(value, "tile", pairs)


def exact_parts(value):
    top = lax.reduce_precision(value, 8, 7)
    middle = lax.reduce_precision(value - top, 8, 7)
    return [top, middle, value - top - middle]


def by_head_columns(value):
    main = value[:, :, 0:128].reshape(WIN, 768)
    tail = value[:, :, 128:WIN].reshape(WIN, 96)
    return jnp.pad(jnp.concatenate([main, tail], axis=1), ((0, 0), (0, 32)))


def on_device(
    features, attn_gain, w_qkv, w_proj, window_bias, patterns, window_pattern, mlp_gain,
    w_expand, w_reduce, temp_head, temp_base, thickness, level_weight, surface, target,
):
    feats = features[:, 0]
    goal = target[:, 0]
    ground = surface[0]
    rim = exact_parts(goal[:, :, 0:8]) + exact_parts(
        jnp.broadcast_to(ground[None, :, 0:8], (2, 12, 8))
    )
    rim = jnp.stack(rim + [jnp.zeros((2, 12, 8), F32)] * 2, axis=-1).astype(BF16)
    edge = jnp.concatenate(
        [feats[:, :, 0:8, :], rim, jnp.zeros((2, 12, 8, 56), BF16)], axis=-1
    )
    edge = block_step(edge, -1)

    band = lax.axis_index("tile") // BLOCKS
    even = (band % 2 == 0).astype(jnp.int32)
    perm = jnp.asarray(source_rows(), BF16)
    perm_back = jnp.asarray(target_rows(), BF16)
    order = jnp.asarray(window_rows(), BF16)
    order_back = jnp.asarray(window_rows().T, BF16)

    pat = patterns.astype(F32)
    pat_q = jnp.concatenate(
        [jnp.tile(pat[:, 0:128], (1, HEADS)), jnp.tile(pat[:, 128:WIN], (1, HEADS + 2))], axis=1
    )
    gains = jnp.pad(
        jnp.stack([attn_gain, mlp_gain, temp_head.astype(F32)]), ((0, 5), (0, 64))
    )
    consts = (
        order, order_back,
        jnp.stack([w_qkv[:, 0:C], w_qkv[:, C : 2 * C], w_qkv[:, 2 * C :]]),
        w_qkv.T, w_proj, w_proj.T, w_expand, w_expand.T, w_reduce,
        by_head_columns(window_bias.transpose(2, 0, 1)),
        pat_q, pat.T, gains,
    )

    made, back = [], []
    for odd in range(2):
        start = (6 * (even if odd == 0 else 1 - even)).reshape(1)
        made.append(
            prep(
                start, window_pattern, thickness, level_weight, temp_base,
                feats, edge, goal, ground, perm,
            )
        )
    for odd in range(2):
        got = exchange(made[odd], odd)
        back.append(exchange(layer(got, consts), odd))
    rims = [block_step(b[GROUP - 1], 1) for b in back]
    height, grad = post(even.reshape(1), back[0], back[1], rims[0], rims[1], perm_back)
    return height[:, None], grad[:, None]


def solution(mesh):
    placed = (
        P("lev", "tile", None, None, None),
        P(), P(), P(), P(), P(),
        P(None, "tile"),
        P(), P(), P(), P(),
        P("lev"), P("lev"), P("lev"),
        P("tile", None, None),
        P("lev", "tile", None, None),
    )
    return jax.shard_map(
        on_device,
        mesh=mesh,
        in_specs=placed,
        out_specs=(P("lev", "tile", None, None), P("lev", "tile", None, None, None)),
        check_vma=False,
    )
```

time: 621 us -> 154 us (0.25); the launches traced: 611 us -> 153 us
  waiting for transfers between devices: 160 us -> 14.9 us
  matrix products: 139 us -> 0 us
  local copies, waits for them, and re-layouts: 156 us -> 17.2 us
  other arithmetic: 92.1 us -> 4.23 us
  Pallas kernels: 0 us -> 75 us
  blocking collectives: 18 us -> 0 us
    ppermute x16 -> x3, waiting for transfers between devices: 160 us -> 1.29 us  [block_step(): return lax.ppermute(value, 'tile', pairs)]
    dot_general x81 -> x0, matrix products: 126 us -> none  [the longest x35 48.8 us: product(): return jnp.einsum(form, left, right, preferred_element_type=jnp.float32)]
    pallas_call x0 -> x5, Pallas kernels: none -> 75 us  [the longest x2 64.4 us: layer(): pl.pallas_call(main_kernel, out_shape=jax.ShapeDtypeStruct((GROUP, ROWS,...]
    reshape x55 -> x2, local copies, waits for them, and re-layouts: 57.9 us -> 0.32 us  [the longest x1 0.23 us: by_head_columns(): main = value[:, :, 0:128].reshape(WIN, 768)]
    reduce_sum x58 -> x0, other arithmetic: 44.4 us -> none  [the longest x10 18.9 us: window_block(): scores = scores - jnp.max(scores, axis=-1, keepdims=True)]
    ppermute x16 -> x3, starting transfers between devices: 40.9 us -> 12.4 us  [block_step(): return lax.ppermute(value, 'tile', pairs)]
    all_to_all x0 -> x4, starting transfers between devices: none -> 28.4 us  [exchange(): lax.all_to_all(blocks, ('tile', 'lev'), 0, 0, axis_index_groups=pair_grou...]
    convert_element_type x45 -> x0, local copies, waits for them, and re-layouts: 25.6 us -> none  [the longest x10 14.7 us: window_block(): value_rows = projected[:, 2 * channels:].astype(jnp.bfloat16).reshape(gro...]
  transfers between devices with their start and end apart: 16 -> 7, of which waited for: 13 -> 3; matrix products, arithmetic and copies ran while one was open for 1% -> 7% of each run, Pallas kernels for 0% -> 44%
where the time goes in v1:
time: 154 us; the launch traced here: 153 us
  Pallas kernels  75 us (49%)
  starting transfers between devices  40.7 us (26%)
  local copies, waits for them, and re-layouts  17.2 us (11%)
  waiting for transfers between devices  14.9 us (10%)
  other arithmetic  4.23 us (3%)
    pallas_call x2, Pallas kernels, layer(): pl.pallas_call(main_kernel, out_shape=jax.ShapeDtypeStruct((GROUP, ROWS,...  64.4 us
    all_to_all x4, starting transfers between devices, exchange(): lax.all_to_all(blocks, ('tile', 'lev'), 0, 0, axis_index_groups=pair_grou...  28.4 us
    all_to_all x4, waiting for transfers between devices, exchange(): lax.all_to_all(blocks, ('tile', 'lev'), 0, 0, axis_index_groups=pair_grou...  13.6 us
    unnamed x41, local copies, waits for them, and re-layouts  12.8 us
    ppermute x3, starting transfers between devices, block_step(): return lax.ppermute(value, 'tile', pairs)  12.4 us
    pallas_call x2, Pallas kernels, prep(): pl.pallas_call(prep_kernel, out_shape=jax.ShapeDtypeStruct((GROUP, ROWS,...  6.68 us
    pallas_call x1, Pallas kernels, post(): pl.pallas_call(post_kernel, out_shape=(jax.ShapeDtypeStruct((2, 12, LONS)...  3.93 us
  transfers between devices with their start and end apart: 7, of which 3 were waited for; matrix products, arithmetic and copies ran while one was open for 7% of the time, Pallas kernels for 44%

profile of v1, /device:TPU:1, one launch (start us, length us, event | category | flops | bytes accessed | tf_op | source)
XLA Modules:
  0.0 152.9 jit_solution(1278354071626582363)
XLA Ops:
  0.6 0.7 copy.148
  1.3 0.7 copy.147
  2.8 1.4 copy.146
  4.6 0.8 concatenate.10
  5.5 3.2 %collective-permute-start = (bf16[2,12,8,256]{3,2,1,0:T(8,128)(2,1)}, bf16[2,12,8,256]{3,2,1,0:T(8,128)(2,1)}, u32[]{:S(2)}, u32[]{:S(2)}) collective-permute-start(bf16[2,12,8,256]{3,2,1,0:T(8,128)(2,1)} %concatenate.10), channel_id=1, source_target_pairs={{0,12},{4,0},{8,4},{12,8},{16,28},{20,16},{24,20},{28,24},{32,44},... | collective-permute-start | bytes 294920 | tf_op jit(solution)/shard_map/ppermute | solution.py:518
  9.4 0.6 convert_bitcast_fusion
  10.8 0.8 stack.69
  11.6 0.8 copy.134
  12.6 1.7 %copy.128 = bf16[192,192]{0,1:T(8,128)(2,1)} copy(bf16[192,192]{1,0:T(8,128)(2,1)} %proj_ref.3) | data formatting | bytes 147456 | tf_op args[3]
  14.2 0.9 copy.127
  15.1 0.9 copy.135.reduce_ref
  16.0 0.9 copy.129
  17.2 0.6 pad_maximum_fusion.1.pat_q_ref
  17.8 3.3 %prep.2 = bf16[8,240,128]{2,1,0:T(8,128)(2,1)} custom-call(s32[1]{0:T(128)} %bitcast.1.start_ref, s32[4,15]{1,0:T(4,128)} %ids_ref.3, f32[2]{0:T(128)} %thick_ref.3, f32[2]{0:T(128)} %weight_ref.3, f32[2]{0:T(128)} %base_ref.3, bf16[2,12,90,192]{3,2,1,0:T(8,128)(2,1)} %bitcast.46, bf16[2,12,8,256]{3,2,1,0:T(8,128)(2,1)} %collective-permute-done.edge_ref, ...), custom_call_target="tpu_custom_call" | custom-call | flops 3000000000 | bytes 2500000 | tf_op jit(solution)/shard_map/prep/pallas_call | solution.py:180
  21.1 5.2 %all-to-all-start = ((bf16[8,240,128]{2,1,0:T(8,128)(2,1)}), bf16[8,240,128]{2,1,0:T(8,128)(2,1)S(1)}, u32[]{:S(2)}, u32[]{:S(2)}) async-start(bf16[8,240,128]{2,1,0:T(8,128)(2,1)} %prep.2), calls=%async_computation | async-start | bytes 983040 | tf_op jit(solution)/shard_map/all_to_all | solution.py:509
  27.0 0.8 pad_maximum_fusion.w_ref
  27.8 0.8 select_maximum_fusion.bias_ref
  28.6 3.3 %prep.3 = bf16[8,240,128]{2,1,0:T(8,128)(2,1)} custom-call(s32[1]{0:T(128)} %bitcast.21.start_ref, s32[4,15]{1,0:T(4,128)} %ids_ref.3, f32[2]{0:T(128)} %thick_ref.3, f32[2]{0:T(128)} %weight_ref.3, f32[2]{0:T(128)} %base_ref.3, bf16[2,12,90,192]{3,2,1,0:T(8,128)(2,1)} %bitcast.47, bf16[2,12,8,256]{3,2,1,0:T(8,128)(2,1)} %collective-permute-done.edge_ref, ...), custom_call_target="tpu_custom_call" | custom-call | flops 3000000000 | bytes 2500000 | tf_op jit(solution)/shard_map/prep/pallas_call | solution.py:180
  32.0 7.7 %all-to-all-done.x_ref = bf16[8,240,128]{2,1,0:T(8,128)(2,1)S(1)} async-done(((bf16[8,240,128]{2,1,0:T(8,128)(2,1)}), bf16[8,240,128]{2,1,0:T(8,128)(2,1)S(1)}, u32[]{:S(2)}, u32[]{:S(2)}) %all-to-all-start) | async-done | bytes 491552 | tf_op jit(solution)/shard_map/all_to_all | solution.py:509
  39.6 9.0 %all-to-all-start.2 = ((bf16[8,240,128]{2,1,0:T(8,128)(2,1)}), bf16[8,240,128]{2,1,0:T(8,128)(2,1)S(1)}, u32[]{:S(2)}, u32[]{:S(2)}) async-start(bf16[8,240,128]{2,1,0:T(8,128)(2,1)} %prep.3), calls=%async_computation.2 | async-start | bytes 983040 | tf_op jit(solution)/shard_map/all_to_all | solution.py:509
  48.6 32.2 %layer.2 = bf16[8,240,128]{2,1,0:T(8,128)(2,1)} custom-call(bf16[8,240,128]{2,1,0:T(8,128)(2,1)} %copy-done.5, bf16[288,288]{1,0:T(8,128)(2,1)} %constant.53.clone.order_ref, bf16[288,288]{1,0:T(8,128)(2,1)} %constant.54.clone.back_ref, bf16[3,192,192]{2,1,0:T(8,128)(2,1)} %pad_maximum_fusion.w_ref, bf16[576,192]{1,0:T(8,128)(2,1)} %bitcast.54, ...), custom_call_target="tpu_custom_call" | custom-call | flops 20000000000 | bytes 4000000 | tf_op jit(solution)/shard_map/layer/pallas_call | solution.py:465
  80.8 4.5 %all-to-all-start.1 = ((bf16[8,240,128]{2,1,0:T(8,128)(2,1)}), bf16[8,240,128]{2,1,0:T(8,128)(2,1)S(1)}, u32[]{:S(2)}, u32[]{:S(2)}) async-start(bf16[8,240,128]{2,1,0:T(8,128)(2,1)} %layer.2), calls=%async_computation.1 | async-start | bytes 983040 | tf_op jit(solution)/shard_map/all_to_all | solution.py:509
  85.3 32.2 %layer.3 = bf16[8,240,128]{2,1,0:T(8,128)(2,1)} custom-call(bf16[8,240,128]{2,1,0:T(8,128)(2,1)} %copy-done.6, bf16[288,288]{1,0:T(8,128)(2,1)} %constant.53.clone.order_ref, bf16[288,288]{1,0:T(8,128)(2,1)} %constant.54.clone.back_ref, bf16[3,192,192]{2,1,0:T(8,128)(2,1)} %pad_maximum_fusion.w_ref, bf16[576,192]{1,0:T(8,128)(2,1)} %bitcast.55, ...), custom_call_target="tpu_custom_call" | custom-call | flops 20000000000 | bytes 4000000 | tf_op jit(solution)/shard_map/layer/pallas_call | solution.py:465
  117.5 9.7 %all-to-all-start.3 = ((bf16[8,240,128]{2,1,0:T(8,128)(2,1)}), bf16[8,240,128]{2,1,0:T(8,128)(2,1)S(1)}, u32[]{:S(2)}, u32[]{:S(2)}) async-start(bf16[8,240,128]{2,1,0:T(8,128)(2,1)} %layer.3), calls=%async_computation.3 | async-start | bytes 983040 | tf_op jit(solution)/shard_map/all_to_all | solution.py:509
  127.2 4.2 %collective-permute-start.1 = (bf16[240,128]{1,0:T(8,128)(2,1)S(1)}, bf16[240,128]{1,0:T(8,128)(2,1)S(1)}, u32[]{:S(2)}, u32[]{:S(2)}) collective-permute-start(bf16[240,128]{1,0:T(8,128)(2,1)S(1)} %slice_bitcast_fusion.4), channel_id=1, source_target_pairs={{0,4},{4,8},{8,12},{12,0},{16,20},{20,24},{24,28},{28,16},{32,36},... | collective-permute-start | bytes 184328 | tf_op jit(solution)/shard_map/ppermute | solution.py:518
  131.5 5.9 %all-to-all-done.3.b_ref = bf16[8,240,128]{2,1,0:T(8,128)(2,1)S(1)} async-done(((bf16[8,240,128]{2,1,0:T(8,128)(2,1)}), bf16[8,240,128]{2,1,0:T(8,128)(2,1)S(1)}, u32[]{:S(2)}, u32[]{:S(2)}) %all-to-all-start.3) | async-done | bytes 491552 | tf_op jit(solution)/shard_map/all_to_all | solution.py:509
  137.4 4.9 %collective-permute-start.2 = (bf16[240,128]{1,0:T(8,128)(2,1)S(1)}, bf16[240,128]{1,0:T(8,128)(2,1)S(1)}, u32[]{:S(2)}, u32[]{:S(2)}) collective-permute-start(bf16[240,128]{1,0:T(8,128)(2,1)S(1)} %slice_bitcast_fusion.3), channel_id=1, source_target_pairs={{0,4},{4,8},{8,12},{12,0},{16,20},{20,24},{24,28},{28,16},{32,36},... | collective-permute-start | bytes 184328 | tf_op jit(solution)/shard_map/ppermute | solution.py:518
  142.3 1.3 collective-permute-done.2.eb_ref
  143.6 0.6 copy-done.14
  144.2 3.9 %post.1 = (f32[2,12,90]{2,1,0:T(8,128)}, bf16[2,12,90,192]{3,2,1,0:T(8,128)(2,1)}) custom-call(s32[1]{0:T(128)} %bitcast.lower_ref, bf16[8,240,128]{2,1,0:T(8,128)(2,1)} %copy-done.3, bf16[8,240,128]{2,1,0:T(8,128)(2,1)} %copy-done.4, bf16[240,128]{1,0:T(8,128)(2,1)} %copy-done.13, bf16[240,128]{1,0:T(8,128)(2,1)} %copy-done.14, ...), custom_call_target="tpu_custom_call" | custom-call | flops 3000000000 | bytes 2500000 | tf_op jit(solution)/shard_map/post/pallas_call | solution.py:226
  148.2 1.3 copy.138
  149.5 3.4 %copy.139 = bf16[2,1,12,90,192]{4,0,3,2,1:T(2,128)(2,1)} copy(bf16[2,1,12,90,192]{4,3,2,0,1:T(8,128)(2,1)} %bitcast.48) | data formatting | bytes 1658880
  (61 shorter events, 3.6 us)
Async XLA Ops:
  1.3 1.3 copy-start.9
  2.8 6.5 %copy-start.10 = (s32[8,144]{1,0:T(8,128)S(1)}, s32[8,144]{1,0:T(8,128)}, u32[]{:S(2)}) copy-start(s32[8,144]{1,0:T(8,128)} %param.25) | copy-start | bytes 13828
  4.3 6.5 %copy-start = (bf16[2,1,12,90,192]{4,3,2,0,1:T(8,128)(2,1)}, bf16[2,1,12,90,192]{4,3,2,0,1:T(8,128)(2,1)S(1)}, u32[]{:S(2)}) copy-start(bf16[2,1,12,90,192]{4,3,2,0,1:T(8,128)(2,1)S(1)} %copy.146) | copy-start | bytes 2488324
  4.3 6.3 %copy-start.2 = (f32[6,144,144]{2,1,0:T(8,128)S(1)}, f32[6,144,144]{2,1,0:T(8,128)}, u32[]{:S(2)}) copy-start(f32[6,144,144]{2,1,0:T(8,128)} %param.24) | copy-start | bytes 1492996
  5.5 12.3 %collective-permute-start = (bf16[2,12,8,256]{3,2,1,0:T(8,128)(2,1)}, bf16[2,12,8,256]{3,2,1,0:T(8,128)(2,1)}, u32[]{:S(2)}, u32[]{:S(2)}) collective-permute-start(bf16[2,12,8,256]{3,2,1,0:T(8,128)(2,1)} %concatenate.10), channel_id=1, source_target_pairs={{0,12},{4,0},{8,4},{12,8},{16,28},{20,16},{24,20},{28,24},{32,44},... | collective-permute-start | bytes 294920 | tf_op jit(solution)/shard_map/ppermute | solution.py:518
  10.6 3.6 %copy-start.1 = (bf16[192,576]{1,0:T(8,128)(2,1)S(1)}, bf16[192,576]{1,0:T(8,128)(2,1)}, u32[]{:S(2)}) copy-start(bf16[192,576]{1,0:T(8,128)(2,1)} %param.22) | copy-start | bytes 663556
  10.7 4.4 %copy-start.7 = (bf16[768,192]{0,1:T(8,128)(2,1)S(1)}, bf16[768,192]{0,1:T(8,128)(2,1)}, u32[]{:S(2)}) copy-start(bf16[768,192]{0,1:T(8,128)(2,1)} %param.29) | copy-start | bytes 884740
  10.7 5.3 %copy-start.8 = (bf16[192,768]{1,0:T(8,128)(2,1)S(1)}, bf16[192,768]{1,0:T(8,128)(2,1)}, u32[]{:S(2)}) copy-start(bf16[192,768]{1,0:T(8,128)(2,1)} %expand_ref.3) | copy-start | bytes 884740
  17.8 8.5 %copy-start.11 = (f32[192]{0:T(256)S(1)}, f32[192]{0:T(256)}, u32[]{:S(2)}) copy-start(f32[192]{0:T(256)} %param.27) | copy-start | bytes 2308
  17.8 8.5 %copy-start.12 = (f32[192]{0:T(256)S(1)}, f32[192]{0:T(256)}, u32[]{:S(2)}) copy-start(f32[192]{0:T(256)} %param.21) | copy-start | bytes 2308
  21.1 18.5 %all-to-all-start = ((bf16[8,240,128]{2,1,0:T(8,128)(2,1)}), bf16[8,240,128]{2,1,0:T(8,128)(2,1)S(1)}, u32[]{:S(2)}, u32[]{:S(2)}) async-start(bf16[8,240,128]{2,1,0:T(8,128)(2,1)} %prep.2), calls=%async_computation | async-start | bytes 983040 | tf_op jit(solution)/shard_map/all_to_all | solution.py:509
  39.6 9.0 %copy-start.5 = (bf16[8,240,128]{2,1,0:T(8,128)(2,1)}, bf16[8,240,128]{2,1,0:T(8,128)(2,1)S(1)}, u32[]{:S(2)}) copy-start(bf16[8,240,128]{2,1,0:T(8,128)(2,1)S(1)} %all-to-all-done.x_ref) | copy-start | bytes 1474564
  39.6 41.2 %all-to-all-start.2 = ((bf16[8,240,128]{2,1,0:T(8,128)(2,1)}), bf16[8,240,128]{2,1,0:T(8,128)(2,1)S(1)}, u32[]{:S(2)}, u32[]{:S(2)}) async-start(bf16[8,240,128]{2,1,0:T(8,128)(2,1)} %prep.3), calls=%async_computation.2 | async-start | bytes 983040 | tf_op jit(solution)/shard_map/all_to_all | solution.py:509
  80.8 4.5 %copy-start.6 = (bf16[8,240,128]{2,1,0:T(8,128)(2,1)}, bf16[8,240,128]{2,1,0:T(8,128)(2,1)S(1)}, u32[]{:S(2)}) copy-start(bf16[8,240,128]{2,1,0:T(8,128)(2,1)S(1)} %all-to-all-done.2.x_ref) | copy-start | bytes 1474564
  80.8 36.7 %all-to-all-start.1 = ((bf16[8,240,128]{2,1,0:T(8,128)(2,1)}), bf16[8,240,128]{2,1,0:T(8,128)(2,1)S(1)}, u32[]{:S(2)}, u32[]{:S(2)}) async-start(bf16[8,240,128]{2,1,0:T(8,128)(2,1)} %layer.2), calls=%async_computation.1 | async-start | bytes 983040 | tf_op jit(solution)/shard_map/all_to_all | solution.py:509
  117.5 26.1 %copy-start.3 = (bf16[8,240,128]{2,1,0:T(8,128)(2,1)}, bf16[8,240,128]{2,1,0:T(8,128)(2,1)S(1)}, u32[]{:S(2)}) copy-start(bf16[8,240,128]{2,1,0:T(8,128)(2,1)S(1)} %all-to-all-done.1.a_ref) | copy-start | bytes 1474564
  117.5 19.9 %all-to-all-start.3 = ((bf16[8,240,128]{2,1,0:T(8,128)(2,1)}), bf16[8,240,128]{2,1,0:T(8,128)(2,1)S(1)}, u32[]{:S(2)}, u32[]{:S(2)}) async-start(bf16[8,240,128]{2,1,0:T(8,128)(2,1)} %layer.3), calls=%async_computation.3 | async-start | bytes 983040 | tf_op jit(solution)/shard_map/all_to_all | solution.py:509
  127.2 15.1 %collective-permute-start.1 = (bf16[240,128]{1,0:T(8,128)(2,1)S(1)}, bf16[240,128]{1,0:T(8,128)(2,1)S(1)}, u32[]{:S(2)}, u32[]{:S(2)}) collective-permute-start(bf16[240,128]{1,0:T(8,128)(2,1)S(1)} %slice_bitcast_fusion.4), channel_id=1, source_target_pairs={{0,4},{4,8},{8,12},{12,0},{16,20},{20,24},{24,28},{28,16},{32,36},... | collective-permute-start | bytes 184328 | tf_op jit(solution)/shard_map/ppermute | solution.py:518
  137.4 6.2 %copy-start.4 = (bf16[8,240,128]{2,1,0:T(8,128)(2,1)}, bf16[8,240,128]{2,1,0:T(8,128)(2,1)S(1)}, u32[]{:S(2)}) copy-start(bf16[8,240,128]{2,1,0:T(8,128)(2,1)S(1)} %all-to-all-done.3.b_ref) | copy-start | bytes 1474564
  137.4 6.2 %collective-permute-start.2 = (bf16[240,128]{1,0:T(8,128)(2,1)S(1)}, bf16[240,128]{1,0:T(8,128)(2,1)S(1)}, u32[]{:S(2)}, u32[]{:S(2)}) collective-permute-start(bf16[240,128]{1,0:T(8,128)(2,1)S(1)} %slice_bitcast_fusion.3), channel_id=1, source_target_pairs={{0,4},{4,8},{8,12},{12,0},{16,20},{20,24},{24,28},{28,16},{32,36},... | collective-permute-start | bytes 184328 | tf_op jit(solution)/shard_map/ppermute | solution.py:518
  142.3 1.3 copy-start.13
  143.6 0.6 copy-start.14

commit v2 on v1

v2 whole, which is shorter than its diff:
```python
import jax
import jax.numpy as jnp
import numpy as np
from jax import lax
from jax.experimental import pallas as pl
from jax.experimental.pallas import tpu as pltpu
from jax.sharding import PartitionSpec as P

F32 = jnp.float32
BF16 = jnp.bfloat16
C = 192
HEADS = 6
HEAD = 32
FF = 768
WIN = 144
HALF = 72
QUARTER = 36
LONS = 90
SHIFT = 3
BLOCKS = 4
BANDS = 16
LEVS = 4
GROUP = 8
ROWS = 240
WIDE = 896
EPS = 1e-05
VMEM_LIMIT = 28 * 1024 * 1024
SMALL_VMEM = 12 * 1024 * 1024
VMEM_ALL = 60 * 1024 * 1024


def source_rows():
    table = np.zeros((2 * WIN, 6 * 64), np.float32)
    for q in range(2):
        for lev in range(2):
            for col in range(2):
                for i in range(QUARTER):
                    r, o = i // 6, i % 6
                    place = 2 * (12 * q + 6 * col + o + SHIFT) + lev
                    table[((q * 2 + lev) * 2 + col) * QUARTER + i, 64 * r + place] = 1.0
    return table


def target_rows():
    table = np.zeros((6 * 48, 3 * WIN), np.float32)
    for r in range(6):
        for x in range(48):
            e, lev = x // 2 + 9, x % 2
            d, col, o = e // 12, e % 12 // 6, e % 6
            table[48 * r + x, d * WIN + lev * HALF + col * QUARTER + 6 * r + o] = 1.0
    return table


def window_rows():
    table = np.zeros((WIN, WIN), np.float32)
    for col in range(2):
        for beta in range(2):
            for i in range(QUARTER):
                table[(col * 2 + beta) * QUARTER + i, (beta * 2 + col) * QUARTER + i] = 1.0
    return table


def dot(a, b):
    return jnp.dot(a, b, preferred_element_type=F32)


def dot_nt(a, b):
    return lax.dot_general(a, b, (((1,), (1,)), ((), ())), preferred_element_type=F32)


def lanes(shape):
    return lax.broadcasted_iota(jnp.int32, shape, len(shape) - 1)


def split3(value):
    top = value.astype(BF16).astype(F32)
    rest = value - top
    middle = rest.astype(BF16).astype(F32)
    return top, middle, rest - middle


def roll(value, steps):
    return pltpu.roll(value, steps % 128, 1)


def pack_block(out_ref, at, made, spare):
    lane = lanes((HALF, 128))
    out_ref[at, 0:WIN, :] = made[:, 0:128].astype(BF16)
    both = made[:, 128:256]
    tail = jnp.where(lane < 64, both[0:HALF], roll(both[HALF:WIN], 64))
    tail = jnp.concatenate([tail, jnp.zeros((8, 128), F32)], axis=0)
    lane16 = lanes((16, 128))
    extra = spare
    for g in range(9):
        moved = roll(both[16 * g : 16 * g + 16], 8 * g - 64)
        extra = jnp.where((lane16 >= 8 * g) & (lane16 < 8 * g + 8), moved, extra)
    out_ref[at, WIN : WIN + 16, :] = extra.astype(BF16)
    out_ref[at, WIN + 16 : ROWS, :] = tail.astype(BF16)


def unpack_block(block):
    first = block[0:WIN].astype(F32)
    extra = block[WIN : WIN + 16].astype(F32)
    tail = block[WIN + 16 : ROWS].astype(F32)[0:HALF]
    lane16 = lanes((16, 128))
    keep = (lane16 >= 64) & (lane16 < 72)
    spread = [jnp.where(keep, roll(extra, 64 - 8 * g), 0.0) for g in range(9)]
    spread = jnp.concatenate(spread, axis=0)
    lane = lanes((HALF, 128))
    second = [
        jnp.where(lane < 64, tail, spread[0:HALF]),
        jnp.where(lane < 64, roll(tail, 64), spread[HALF:WIN]),
    ]
    return first, second, extra


def vmem():
    return pl.BlockSpec(memory_space=pltpu.VMEM)


def smem():
    return pl.BlockSpec(memory_space=pltpu.SMEM)


def field_rows(targets, ground, count, padded):
    blank = jnp.zeros((count, 128 - LONS), F32)
    goal = [jnp.concatenate([t, blank], axis=1) for t in targets]
    ground = jnp.concatenate([ground, blank], axis=1)
    parts = split3(jnp.concatenate(goal, axis=1)) + split3(
        jnp.concatenate([ground, ground], axis=1)
    )
    if padded > count:
        more = jnp.zeros((padded - count, 256), F32)
        parts = [jnp.concatenate([v, more], axis=0) for v in parts]
    stacked = jnp.concatenate(parts, axis=0).astype(BF16)
    i = lax.broadcasted_iota(jnp.int32, (128, 6 * padded), 0)
    j = lanes((128, 6 * padded))
    hit = (j == padded * (i & 7) + (i >> 3)) & ((i & 7) < 6) & ((i >> 3) < count)
    return dot(jnp.where(hit, 1.0, 0.0).astype(BF16), stacked).astype(BF16)


def lon_pick(rows, first):
    x = lax.broadcasted_iota(jnp.int32, (rows, 256), 0)
    y = lanes((rows, 256))
    return jnp.where(y == 128 * (x & 1) + (x >> 1) + first, 1.0, 0.0).astype(BF16)


def rim_kernel(ids_ref, fa_ref, fb_ref, target_ref, surface_ref, next_ref, prev_ref):
    targets = [
        jnp.concatenate([target_ref[lev, r] for r in range(12)], axis=0) for lev in range(2)
    ]
    ground = jnp.concatenate([surface_ref[r] for r in range(12)], axis=0)
    fields = field_rows(targets, ground, 12, 16)
    spots = jnp.concatenate([lon_pick(8, 0), lon_pick(8, 86)], axis=0)
    values = dot_nt(spots, fields)
    lane = lanes((8, 128))
    idents = jnp.zeros((8, 128), F32)
    for p in range(4):
        idents = jnp.where(lane == 72 + p, ids_ref[p, 14].astype(F32), idents)
    for out_ref, f_ref, at, row, more in (
        (next_ref, fa_ref, 0, 0, 0.0), (prev_ref, fb_ref, 12, 8, idents)
    ):
        made = []
        for r in range(12):
            tokens = f_ref[r].reshape(20, C).astype(F32)[at : at + 8]
            second = jnp.concatenate([tokens[:, 128:C], jnp.zeros((8, 64), F32)], axis=1)
            extra = roll(values, 64 - 8 * r)[row : row + 8]
            second = jnp.where(lane < 64, second, jnp.where(lane < 72, extra, more))
            made.append(jnp.concatenate([tokens[:, 0:128], second], axis=1))
        out_ref[...] = jnp.concatenate(made, axis=0).astype(BF16)


def rim(ids, feats, target, surface):
    edge = jax.ShapeDtypeStruct((96, 256), BF16)
    return pl.pallas_call(
        rim_kernel,
        out_shape=(edge, edge),
        grid=(1,),
        in_specs=[
            smem(),
            pl.BlockSpec((12, 10, 2, C), lambda i: (0, 0, 0, 0)),
            pl.BlockSpec((12, 10, 2, C), lambda i: (0, 8, 0, 0)),
            pl.BlockSpec((2, 12, 1, LONS), lambda i: (0, 0, 0, 0)),
            pl.BlockSpec((12, 1, LONS), lambda i: (0, 0, 0)),
        ],
        out_specs=(
            pl.BlockSpec((96, 256), lambda i: (0, 0)),
            pl.BlockSpec((96, 256), lambda i: (0, 0)),
        ),
        compiler_params=pltpu.CompilerParams(vmem_limit_bytes=VMEM_ALL),
        name="rim",
    )(ids, feats, feats, target, surface)


def prep_kernel(
    half_ref, ids_ref, thick_ref, weight_ref, base_ref,
    f_ref, next_ref, prev_ref, target_ref, surface_ref, perm_ref,
    out_ref, rows_ref,
):
    targets = [
        jnp.concatenate([target_ref[lev, r] for r in range(6)], axis=0) for lev in range(2)
    ]
    ground = jnp.concatenate([surface_ref[r] for r in range(6)], axis=0)
    values = dot_nt(lon_pick(2 * LONS, 0), field_rows(targets, ground, 6, 8))
    after = next_ref[...].astype(F32)
    before = prev_ref[...].astype(F32)
    lane = lanes((2 * LONS, 128))
    for r in range(6):
        tokens = f_ref[r].reshape(2 * LONS, C).astype(F32)
        second = jnp.concatenate([tokens[:, 128:C], jnp.zeros((2 * LONS, 64), F32)], axis=1)
        extra = jnp.where(lane < 72, roll(values, 64 - 8 * r), 0.0)
        second = jnp.where(lane < 64, second, extra)
        for at, part in ((0, tokens[:, 0:128]), (128, second)):
            cut = slice(at, at + 128)
            rows_ref[208 * r : 208 * r + 176, cut] = part[0:176].astype(BF16)
            tail = [
                part[176:180],
                after[8 * r : 8 * r + 6, cut],
                before[8 * r + 2 : 8 * r + 8, cut],
                part[0:6],
                jnp.zeros((10, 128), F32),
            ]
            tail = jnp.concatenate(tail, axis=0).astype(BF16)
            rows_ref[208 * r + 176 : 208 * r + 208, cut] = tail
    lane16 = lanes((16, 128))
    row16 = lax.broadcasted_iota(jnp.int32, (16, 128), 0)
    scalars = jnp.zeros((16, 128), F32)
    for lev in range(2):
        for k, ref in enumerate((thick_ref, weight_ref, base_ref)):
            scalars = jnp.where((row16 == lev) & (lane16 == 72 + k), ref[lev], scalars)
    top, middle, low = split3(scalars)
    scalars = top + roll(middle, 3) + roll(low, 6)
    for m in range(4):
        source = [rows_ref[208 * r + 48 * m : 208 * r + 48 * m + 64, :] for r in range(6)]
        made = dot(perm_ref[...], jnp.concatenate(source, axis=0))
        for q in range(2):
            d = 2 * m + q
            spare = scalars
            for p in range(4):
                for col in range(2):
                    if 2 * d + col < 15:
                        ident = ids_ref[p, 2 * d + col].astype(F32)
                    else:
                        ident = before[0:1, 200 + p : 201 + p]
                    spare = jnp.where((row16 == 2 + p) & (lane16 == 81 + col), ident, spare)
            pack_block(out_ref, d, made[WIN * q : WIN * q + WIN], spare)


def prep(half, ids, thick, weight, base, feats, after, before, target, surface, perm):
    return pl.pallas_call(
        prep_kernel,
        out_shape=jax.ShapeDtypeStruct((GROUP, ROWS, 128), BF16),
        grid_spec=pltpu.PrefetchScalarGridSpec(
            num_scalar_prefetch=1,
            grid=(1,),
            in_specs=[smem()] * 4
            + [
                pl.BlockSpec((6, LONS, 2, C), lambda i, h: (h[0], 0, 0, 0)),
                pl.BlockSpec((48, 256), lambda i, h: (h[0], 0)),
                pl.BlockSpec((48, 256), lambda i, h: (h[0], 0)),
                pl.BlockSpec((2, 6, 1, LONS), lambda i, h: (0, h[0], 0, 0)),
                pl.BlockSpec((6, 1, LONS), lambda i, h: (h[0], 0, 0)),
                pl.BlockSpec((2 * WIN, 384), lambda i, h: (0, 0)),
            ],
            out_specs=pl.BlockSpec((GROUP, ROWS, 128), lambda i, h: (0, 0, 0)),
            scratch_shapes=[pltpu.VMEM((6 * 208, 256), BF16)],
        ),
        compiler_params=pltpu.CompilerParams(vmem_limit_bytes=SMALL_VMEM),
        cost_estimate=pl.CostEstimate(
            flops=1_000_000_000, bytes_accessed=2_500_000, transcendentals=0
        ),
        name="prep",
    )(half, ids, thick, weight, base, feats, after, before, target, surface, perm)


def post_kernel(half_ref, x_ref, perm_ref, *refs):
    height_ref, grad_ref, rows_ref = refs[-3:]
    for d in range(GROUP):
        first, second, _ = unpack_block(x_ref[d])
        rows_ref[d, :, 0:128] = first.astype(BF16)
        rows_ref[d, :, 128:256] = jnp.concatenate(second, axis=0).astype(BF16)
    lane = lanes((48, 128))
    columns = []
    for m in range(4):
        source = [rows_ref[(2 * m + k) % GROUP] for k in (-1, 0, 1)]
        made = dot(perm_ref[...], jnp.concatenate(source, axis=0))
        count = 24 if m < 3 else 18
        column = jnp.zeros((48, 128), F32)
        for r in range(6):
            tokens = made[48 * r : 48 * r + 2 * count, 0:C].astype(BF16)
            grad_ref[r, 24 * m : 24 * m + count] = tokens.reshape(count, 2, C)
            moved = roll(made[48 * r : 48 * r + 48, 128:256], 8 * r - 64)
            column = jnp.where((lane >= 8 * r) & (lane < 8 * r + 3), moved, column)
        columns.append(column)
    columns = jnp.concatenate(columns, axis=0).astype(BF16)
    rows = lax.dot_general(
        columns, lon_pick(192, 0), (((0,), (0,)), ((), ())), preferred_element_type=F32
    )
    for r in range(6):
        row = rows[8 * r : 8 * r + 1] + rows[8 * r + 1 : 8 * r + 2] + rows[8 * r + 2 : 8 * r + 3]
        for lev in range(2):
            height_ref[lev, r] = row[:, 128 * lev : 128 * lev + LONS]


def post(half, blocks, perm, earlier):
    kept = [] if earlier is None else list(earlier)
    return pl.pallas_call(
        post_kernel,
        out_shape=(
            jax.ShapeDtypeStruct((2, 12, 1, LONS), F32),
            jax.ShapeDtypeStruct((12, LONS, 2, C), BF16),
        ),
        grid_spec=pltpu.PrefetchScalarGridSpec(
            num_scalar_prefetch=1,
            grid=(1,),
            in_specs=[
                pl.BlockSpec((GROUP, ROWS, 128), lambda i, h: (0, 0, 0)),
                pl.BlockSpec((6 * 48, 3 * WIN), lambda i, h: (0, 0)),
            ]
            + [pl.BlockSpec(memory_space=pl.ANY) for _ in kept],
            out_specs=(
                pl.BlockSpec((2, 6, 1, LONS), lambda i, h: (0, h[0], 0, 0)),
                pl.BlockSpec((6, LONS, 2, C), lambda i, h: (h[0], 0, 0, 0)),
            ),
            scratch_shapes=[pltpu.VMEM((GROUP, WIN, 256), BF16)],
        ),
        input_output_aliases={3: 0, 4: 1} if kept else {},
        compiler_params=pltpu.CompilerParams(vmem_limit_bytes=SMALL_VMEM),
        cost_estimate=pl.CostEstimate(
            flops=1_000_000_000, bytes_accessed=2_500_000, transcendentals=0
        ),
        name="post",
    )(half, blocks, perm, *kept)


def norm_parts(x):
    center = jnp.sum(x, axis=-1, keepdims=True) * (1.0 / C)
    moved = x - center
    spread = jnp.sum(moved * moved, axis=-1, keepdims=True) * (1.0 / C)
    scale = lax.rsqrt(spread + EPS)
    return moved * scale, scale


def norm_back(cotangent, hat, scale):
    mean = jnp.sum(cotangent, axis=-1, keepdims=True) * (1.0 / C)
    along = jnp.sum(cotangent * hat, axis=-1, keepdims=True) * (1.0 / C)
    return scale * (cotangent - mean - hat * along)


def wide(value):
    return jnp.concatenate([value, value[:, 0:64]], axis=1)


def diagonal_tails(turned):
    lane = lanes((HEAD, 128))
    out = []
    for h in range(HEADS):
        rows = slice(HEAD * h, HEAD * h + HEAD)
        tail = jnp.concatenate([turned[rows, 128:WIN], jnp.zeros((HEAD, 112), F32)], axis=1)
        tail = roll(tail, 16 * h)
        out.append(jnp.where((lane >= 16 * h) & (lane < 16 * h + 16), tail, 0.0))
    return jnp.concatenate(out, axis=0)


def fill_diagonal(ref, turned, tails):
    for h in range(HEADS):
        rows = slice(HEAD * h, HEAD * h + HEAD)
        ref[rows, 128 * h : 128 * h + 128] = turned[rows, 0:128].astype(BF16)
    ref[0:C, 768:WIDE] = tails.astype(BF16)


def per_head(turned, weights):
    main = [
        dot(turned[HEAD * h : HEAD * h + HEAD], weights[:, 128 * h : 128 * h + 128])
        for h in range(HEADS)
    ]
    return jnp.concatenate(main, axis=0), dot(turned, weights[:, 768:WIDE])


def token_rows(main, tails):
    tails = tails.T
    lane = lanes((16, C))
    last = jnp.zeros((16, C), F32)
    for h in range(HEADS):
        mine = (lane >= HEAD * h) & (lane < HEAD * h + HEAD)
        last = jnp.where(mine, tails[16 * h : 16 * h + 16], last)
    return jnp.concatenate([main.T, last], axis=0)


def head_rows(value):
    lane = lanes((WIN, C))
    parts, tails = [], []
    for h in range(HEADS):
        mine = jnp.where((lane >= HEAD * h) & (lane < HEAD * h + HEAD), value, 0.0).astype(BF16)
        parts.append(mine[0:128])
        tails.append(mine[128:WIN])
    return jnp.concatenate(parts + tails + [jnp.zeros((32, C), BF16)], axis=0)


def setup_kernel(
    w_ref, bias_ref, pat_ref, attn_gain_ref, mlp_gain_ref, temp_head_ref,
    wt_ref, w3_ref, bias_out_ref, pat_q_ref, pat_k_ref, gains_ref,
):
    whole = w_ref[...].astype(F32)
    wt_ref[...] = whole.T.astype(BF16)
    for k in range(3):
        piece = whole[:, C * k : C * k + C]
        piece = jnp.concatenate([piece, jnp.zeros((C, 64), F32)], axis=1)
        w3_ref[k] = piece.astype(BF16)
    lane = lanes((WIN, 128))
    tails = jnp.zeros((WIN, 128), F32)
    for h in range(HEADS):
        turned = bias_ref[h].T
        bias_out_ref[:, 128 * h : 128 * h + 128] = turned[:, 0:128]
        tail = jnp.concatenate([turned[:, 128:WIN], jnp.zeros((WIN, 112), F32)], axis=1)
        tail = roll(tail, 16 * h)
        tails = jnp.where((lane >= 16 * h) & (lane < 16 * h + 16), tail, tails)
    bias_out_ref[:, 768:WIDE] = tails
    pat = pat_ref[...].astype(F32)
    for h in range(HEADS):
        pat_q_ref[:, 128 * h : 128 * h + 128] = pat[:, 0:128]
    tail = jnp.concatenate([pat[:, 128:WIN], jnp.zeros((8, 112), F32)], axis=1)
    tails = tail
    for h in range(1, 8):
        tails = tails + roll(tail, 16 * h)
    pat_q_ref[:, 768:WIDE] = tails
    pat_k_ref[...] = jnp.concatenate([pat, jnp.zeros((120, WIN), F32)], axis=0).T
    gains_ref[...] = jnp.zeros((8, 256), F32)
    gains_ref[0:1, 0:C] = attn_gain_ref[...]
    gains_ref[1:2, 0:C] = mlp_gain_ref[...]
    gains_ref[2:3, 0:C] = temp_head_ref[...].astype(F32)


def setup(w_qkv, window_bias, patterns, attn_gain, mlp_gain, temp_head):
    return pl.pallas_call(
        setup_kernel,
        out_shape=(
            jax.ShapeDtypeStruct((3 * C, C), BF16),
            jax.ShapeDtypeStruct((3, C, 256), BF16),
            jax.ShapeDtypeStruct((WIN, WIDE), F32),
            jax.ShapeDtypeStruct((8, WIDE), F32),
            jax.ShapeDtypeStruct((WIN, 128), F32),
            jax.ShapeDtypeStruct((8, 256), F32),
        ),
        in_specs=[vmem()] * 6,
        out_specs=(vmem(),) * 6,
        compiler_params=pltpu.CompilerParams(vmem_limit_bytes=VMEM_ALL),
        cost_estimate=pl.CostEstimate(
            flops=1_000_000_000, bytes_accessed=3_000_000, transcendentals=0
        ),
        name="setup",
    )(w_qkv, window_bias, patterns, attn_gain[None], mlp_gain[None], temp_head[None])


LOG2E = 1.4426950408889634


def interleave(runs, lag):
    live = list(runs)
    ahead = 0
    while live:
        for k, run in enumerate(list(live)):
            if run is runs[-1] and len(runs) > 1 and ahead < lag and runs[0] in live:
                continue
            try:
                next(run)
            except StopIteration:
                live.remove(run)
        ahead += 1


PER_COLUMN = (
    ((4, WIN, 256), F32),
    ((208, WIDE), BF16),
    ((208, WIDE), BF16),
    ((4, WIN, WIDE), BF16),
    ((4, WIN, WIDE), BF16),
    ((4, WIN, C), BF16),
    ((4, WIN, C), BF16),
    ((4, WIN, C), F32),
    ((4, WIN, C), F32),
    ((4, WIN, C), F32),
    ((4, WIN, 128), F32),
    ((4, WIN, 128), F32),
    ((4, WIN, 128), F32),
    ((4, WIN, 256), F32),
    ((4, WIN, 128), F32),
    ((4, WIN, 256), BF16),
)


def main_kernel(
    x_ref, order_ref, back_ref, wt_ref, w_ref, bias_ref, pat_q_ref, pat_k_ref, gains_ref,
    proj_ref, expand_ref, reduce_ref,
    out_ref, tok_in, levels_ref, *scratch,
):
    columns = (scratch[: len(PER_COLUMN)], scratch[len(PER_COLUMN) :])
    scale_q = 1.0 / HEAD**0.5
    lane72 = lanes((HALF, 128))
    lane16 = lanes((16, 128))
    row16 = lax.broadcasted_iota(jnp.int32, (16, 128), 0)
    for s in range(GROUP):
        first, second, extra = unpack_block(x_ref[s])
        tok_in[s, :, 0:128] = first
        tok_in[s, 0:HALF, 128:256] = second[0]
        tok_in[s, HALF:WIN, 128:256] = second[1]
        if s < 4:
            whole = (extra + roll(extra, -3)) + roll(extra, -6)
            levels_ref[s] = jnp.where(lane16 < 75, whole, extra)
    for col in range(2):
        for ref in columns[col][1:3]:
            ref[...] = jnp.zeros(ref.shape, BF16)

    def place(p, part):
        a, beta = part // 2, part % 2
        return beta * 4 + (p + a) % 4, (HALF if a == 0 else 0)

    pick_row = lax.broadcasted_iota(jnp.int32, (128, 256), 0)
    pick_lane = lanes((128, 256))
    pick = jnp.where(
        pick_lane < 128,
        jnp.where((pick_row >= 64) & (pick_row < 67), 1.0, 0.0),
        jnp.where((pick_row >= 67) & (pick_row < 70), 1.0, 0.0),
    ).astype(BF16)
    for p in range(4):
        for a in range(2):
            pieces = []
            for beta in range(2):
                s, at = place(p, 2 * a + beta)
                pieces.append(tok_in[s, at : at + HALF, :])
            moved = dot(order_ref[...], jnp.concatenate(pieces, axis=0).astype(BF16))
            fields = dot(moved[:, 128:256].astype(BF16), pick)
            for col in range(2):
                rows = slice(HALF * a, HALF * a + HALF)
                columns[col][0][p, rows, :] = moved[HALF * col : HALF * col + HALF]
                columns[col][13][p, rows, :] = fields[HALF * col : HALF * col + HALF]

    gain_one = gains_ref[0:1, 0:C]
    gain_two = gains_ref[1:2, 0:C]
    head_row = gains_ref[2:3, 0:C]
    head_eight = jnp.broadcast_to(head_row, (8, C)).astype(BF16)
    u_row = dot(head_eight, reduce_ref[...])[0:1]

    def forward(p, col):
        (tok, diag_q, diag_n, probs, dscores, q_rows, n_rows, dq_rows, resid, hats, scales,
         deltas, _, _, _, _) = columns[col]
        x = tok[p, :, 0:C]
        hat, scale = norm_parts(x)
        normed = (hat * gain_one).astype(BF16)
        hats[p] = hat
        scales[p] = jnp.broadcast_to(scale, (WIN, 128))
        spot = (row16 == 2 + p) & (lane16 == 81 + col)
        ident = jnp.sum(jnp.where(spot, levels_ref[0], 0.0), axis=0, keepdims=True)
        ident = jnp.sum(ident, axis=1, keepdims=True)
        row8 = lax.broadcasted_iota(jnp.int32, (8, 1), 0).astype(F32)
        label_q = jnp.sum(jnp.where(row8 == ident, pat_q_ref[...], 0.0), axis=0, keepdims=True)
        lane_row = lanes((1, 128)).astype(F32)
        label_k = jnp.sum(
            jnp.where(lane_row == ident, pat_k_ref[...], 0.0), axis=1, keepdims=True
        )
        yield
        turned = dot_nt(wt_ref[...], normed)
        q_turned = turned[0:C] * (scale_q * LOG2E)
        fill_diagonal(diag_q, q_turned, diagonal_tails(q_turned))
        apart = jnp.where(row8 == label_q, 0.0, -1e30)
        diag_q[C : C + 16, :] = jnp.concatenate(
            [apart, jnp.zeros((8, WIDE), F32)], axis=0
        ).astype(BF16)
        keys_t = turned[C : 2 * C].astype(BF16)
        values_t = turned[2 * C : 3 * C].astype(BF16)
        yield
        q_rows[p] = (dot(normed, w_ref[0])[:, 0:C] * scale_q).astype(BF16)
        keys = dot(normed, w_ref[1])
        marks = jnp.where(lanes((WIN, 128)).astype(F32) == label_k + 64.0, 1.0, keys[:, 128:256])
        keys = jnp.concatenate([keys[:, 0:128], marks], axis=1)[:, 0:208].astype(BF16)
        values = dot(normed, w_ref[2])
        lane_wide = lanes((1, 256))
        ones = jnp.where((lane_wide == C) | (lane_wide == C + 1), 1.0, 0.0)
        values = (values + ones)[:, 0:208].astype(BF16)
        yield
        scores = dot(keys, diag_q[...]) + bias_ref[...] * LOG2E
        yield
        raised = jnp.exp2(scores - jnp.max(scores, axis=0, keepdims=True))
        weights = (raised * (1.0 / jnp.sum(raised, axis=0, keepdims=True))).astype(BF16)
        probs[p] = weights
        yield
        main, tails = per_head(values_t, weights)
        context = token_rows(main, tails).astype(BF16)
        yield
        middle = (x + dot(context, proj_ref[...])).astype(BF16).astype(F32)
        hat_two, scale_two = norm_parts(middle)
        normed_two = (hat_two * gain_two).astype(BF16)
        yield
        acc = jnp.zeros((WIN, 256), F32)
        back = jnp.zeros((WIN, C), F32)
        c0 = 0.7978845608028654
        c1 = c0 * 0.044715
        for f in range(3):
            at = slice(256 * f, 256 * f + 256)
            pre = dot(normed_two, expand_ref[:, at])
            u = u_row[:, at]
            square = pre * pre
            gate = 0.5 + 0.5 * jnp.tanh(pre * (c0 + c1 * square))
            unit = pre * gate
            acc = acc + unit * u
            slope = gate * (1.0 + (pre - unit) * (2.0 * c0 + (6.0 * c1) * square))
            back = back + dot_nt((slope * u).astype(BF16), expand_ref[:, at])
            yield
        delta = jnp.sum(acc, axis=1, keepdims=True) + jnp.sum(
            middle * head_row, axis=1, keepdims=True
        )
        deltas[p] = jnp.broadcast_to(delta, (WIN, 128))
        kept = head_row + norm_back(back * gain_two, hat_two, scale_two)
        resid[p] = kept
        kept = kept.astype(BF16)
        yield
        n_turned = dot_nt(proj_ref[...], kept)
        n_tails = diagonal_tails(n_turned)
        fill_diagonal(diag_n, n_turned, n_tails)
        product = n_turned[:, 0:128] * main
        inner = [
            jnp.sum(product[HEAD * h : HEAD * h + HEAD], axis=0, keepdims=True)
            for h in range(HEADS)
        ]
        inner.append(jnp.sum(n_tails * tails, axis=0, keepdims=True))
        inner = jnp.concatenate(inner, axis=1)
        top = inner.astype(BF16).astype(F32)
        diag_n[C : C + 16, :] = jnp.concatenate(
            [-top, top - inner, jnp.zeros((14, WIDE), F32)], axis=0
        ).astype(BF16)
        n_rows[p] = dot_nt(kept, proj_ref[...]).astype(BF16)
        yield
        dweights = dot(values, diag_n[...])
        dscore = (probs[p].astype(F32) * dweights).astype(BF16)
        dscores[p] = dscore
        yield
        main, tails = per_head(keys_t, dscore)
        dq_rows[p] = token_rows(main, tails)

    def forward_step(p, carry):
        interleave([forward(p, 0), forward(p, 1)], LAG)
        return carry

    lax.fori_loop(0, 4, forward_step, 0)

    def scalar(l, k):
        return levels_ref[l // 2, l % 2 : l % 2 + 1, 72 + k : 73 + k]

    for col in range(2):
        deltas, source, fields, heights = (columns[col][k] for k in (11, 12, 13, 14))
        total = jnp.zeros((HALF, 128), F32)
        misfits, spots = [], []
        for l in range(8):
            a = 1 - l % 2
            p = (l // 2 - a) % 4
            rows = slice(HALF * a, HALF * a + HALF)
            spots.append((p, rows))
            temps = scalar(l, 2) + deltas[p, rows, :]
            total = total + scalar(l, 0) * temps
            height = fields[p, rows, 128:256] + total
            misfits.append(scalar(l, 1) * (height - fields[p, rows, 0:128]))
            top, middle, low = split3(height)
            heights[p, rows, :] = jnp.where(
                lane72 == 64, top, jnp.where(lane72 == 65, middle, low)
            )
        carried = jnp.zeros((HALF, 128), F32)
        for l in reversed(range(8)):
            p, rows = spots[l]
            carried = carried + misfits[l]
            source[p, rows, :] = scalar(l, 0) * carried

    def backward(p, col):
        (_, _, _, probs, dscores, q_rows, n_rows, dq_rows, resid, hats, scales,
         _, source, _, heights, made) = columns[col]
        s = wide(source[p])
        dk = dot(dscores[p], head_rows(s * q_rows[p].astype(F32))).astype(BF16)
        yield
        dv = dot(probs[p], head_rows(s * n_rows[p].astype(F32))).astype(BF16)
        yield
        dq = ((s * scale_q) * dq_rows[p]).astype(BF16)
        dnormed = (
            dot(dq, wt_ref[0:C, :]) + dot(dk, wt_ref[C : 2 * C, :]) + dot(dv, wt_ref[2 * C :, :])
        )
        yield
        dx = norm_back(dnormed * gain_one, hats[p], wide(scales[p]))
        grad = s * resid[p] + dx
        lane = lanes((WIN, 128))
        last = jnp.concatenate([grad[:, 128:C], jnp.zeros((WIN, 64), F32)], axis=1)
        last = jnp.where(lane < 64, last, jnp.where(lane < 67, heights[p], 0.0))
        made[p, :, 0:128] = grad[:, 0:128].astype(BF16)
        made[p, :, 128:256] = last.astype(BF16)

    def backward_step(p, carry):
        interleave([backward(p, 0), backward(p, 1)], 0)
        return carry

    lax.fori_loop(0, 4, backward_step, 0)

    for p in range(4):
        for a in range(2):
            rows = slice(HALF * a, HALF * a + HALF)
            pair = [columns[col][15][p].astype(F32)[rows] for col in range(2)]
            moved = dot(back_ref[...], jnp.concatenate(pair, axis=0).astype(BF16))
            for beta in range(2):
                s, at = place(p, 2 * a + beta)
                tok_in[s, at : at + HALF, :] = moved[HALF * beta : HALF * beta + HALF]
    zero = jnp.zeros((16, 128), F32)
    for s in range(GROUP):
        pack_block(out_ref, s, tok_in[s], zero)


LAG = 0


def layer(x, consts):
    return pl.pallas_call(
        main_kernel,
        out_shape=jax.ShapeDtypeStruct((GROUP, ROWS, 128), BF16),
        in_specs=[vmem()] * (1 + len(consts)),
        out_specs=vmem(),
        scratch_shapes=[
            pltpu.VMEM((GROUP, WIN, 256), F32),
            pltpu.VMEM((4, 16, 128), F32),
        ]
        + [pltpu.VMEM(shape, kind) for shape, kind in PER_COLUMN] * 2,
        compiler_params=pltpu.CompilerParams(vmem_limit_bytes=VMEM_LIMIT),
        cost_estimate=pl.CostEstimate(
            flops=20_000_000_000, bytes_accessed=4_000_000, transcendentals=3_000_000
        ),
        name="layer",
    )(x, *consts)


def pair_groups(odd):
    out = []
    for block in range(BLOCKS):
        for band in range(odd, BANDS, 2):
            members = (band, (band + 1) % BANDS)
            out.append(
                [(b * BLOCKS + block) * LEVS + lev for b in members for lev in range(LEVS)]
            )
    return out


def exchange(blocks, odd):
    return lax.all_to_all(
        blocks, ("tile", "lev"), 0, 0, axis_index_groups=pair_groups(odd)
    )


def block_step(value, steps):
    pairs = [
        (t, t - t % BLOCKS + (t + steps) % BLOCKS) for t in range(BANDS * BLOCKS)
    ]
    return lax.ppermute(value, "tile", pairs)


def on_device(
    features, attn_gain, w_qkv, w_proj, window_bias, patterns, window_pattern, mlp_gain,
    w_expand, w_reduce, temp_head, temp_base, thickness, level_weight, surface, target,
):
    feats = features[:, 0].transpose(1, 2, 0, 3)
    goal = target.transpose(0, 2, 1, 3)
    ground = surface.transpose(1, 0, 2)
    after, before = rim(window_pattern, feats, goal, ground)
    after = block_step(after, -1)
    before = block_step(before, 1)

    band = lax.axis_index("tile") // BLOCKS
    even = (band % 2 == 0).astype(jnp.int32)
    halves = [even.reshape(1), (1 - even).reshape(1)]
    perm = jnp.asarray(source_rows(), BF16)
    perm_back = jnp.asarray(target_rows(), BF16)
    order = jnp.asarray(window_rows(), BF16)
    order_back = jnp.asarray(window_rows().T, BF16)

    made = [
        prep(
            half, window_pattern, thickness, level_weight, temp_base,
            feats, after, before, goal, ground, perm,
        )
        for half in halves
    ]
    weights = (w_qkv, window_bias, patterns, attn_gain, mlp_gain, temp_head)
    weights, made[0] = lax.optimization_barrier((weights, made[0]))
    consts = (order, order_back) + tuple(setup(*weights)) + (w_proj, w_expand, w_reduce.T)
    done = None
    for odd in range(2):
        got = exchange(made[odd], odd)
        done = post(halves[odd], exchange(layer(got, consts), odd), perm_back, done)
    height, grad = done
    return height.transpose(0, 2, 1, 3), grad.transpose(2, 0, 1, 3)[:, None]


def solution(mesh):
    placed = (
        P("lev", "tile", None, None, None),
        P(), P(), P(), P(), P(),
        P(None, "tile"),
        P(), P(), P(), P(),
        P("lev"), P("lev"), P("lev"),
        P("tile", None, None),
        P("lev", "tile", None, None),
    )
    return jax.shard_map(
        on_device,
        mesh=mesh,
        in_specs=placed,
        out_specs=(P("lev", "tile", None, None), P("lev", "tile", None, None, None)),
        check_vma=False,
    )
```

time: 154 us -> 107 us (0.69)
  the two profiles are of different devices: /device:TPU:1 before, /device:TPU:32 now
where the time goes in v2:
time: 107 us
  Pallas kernels  48.7 us (46%)
  starting transfers between devices  35.4 us (33%)
  waiting for transfers between devices  17.5 us (16%)
  local copies, waits for them, and re-layouts  4.09 us (4%)
    pallas_call x2, Pallas kernels, layer(): pl.pallas_call(main_kernel, out_shape=jax.ShapeDtypeStruct((GROUP, ROWS,...  35.7 us
    all_to_all x4, starting transfers between devices, exchange(): lax.all_to_all(blocks, ('tile', 'lev'), 0, 0, axis_index_groups=pair_grou...  34.9 us
    all_to_all x4, waiting for transfers between devices, exchange(): lax.all_to_all(blocks, ('tile', 'lev'), 0, 0, axis_index_groups=pair_grou...  13.7 us
    pallas_call x2, Pallas kernels, prep(): pl.pallas_call(prep_kernel, out_shape=jax.ShapeDtypeStruct((GROUP, ROWS,...  4.85 us
    ppermute x2, waiting for transfers between devices, block_step(): return lax.ppermute(value, 'tile', pairs)  3.78 us
    unnamed x42, local copies, waits for them, and re-layouts  3.5 us
    pallas_call x2, Pallas kernels, post(): pl.pallas_call(post_kernel, out_shape=(jax.ShapeDtypeStruct((2, 12, 1, LO...  3.34 us
    pallas_call x1, Pallas kernels, setup(): pl.pallas_call(setup_kernel, out_shape=(jax.ShapeDtypeStruct((3 * C, C),...  2.75 us
  transfers between devices with their start and end apart: 6, of which 4 were waited for; matrix products, arithmetic and copies ran while one was open for 1% of the time, Pallas kernels for 40%

profile of v2, /device:TPU:32, one launch (start us, length us, event | category | flops | bytes accessed | tf_op | source)
XLA Modules:
  0.0 106.5 jit_solution(5631440403861452591)
XLA Ops:
  0.7 0.0 copy-start.11
  0.7 2.1 %rim.1 = (bf16[96,256]{1,0:T(8,128)(2,1)}, bf16[96,256]{1,0:T(8,128)(2,1)}) custom-call(s32[4,15]{1,0:T(4,128)} %ids_ref.5, bf16[12,90,2,192]{3,2,1,0:T(2,128)(2,1)} %bitcast.14, bf16[12,90,2,192]{3,2,1,0:T(2,128)(2,1)} %bitcast.15, f32[2,12,1,90]{3,2,1,0:T(1,128)} %bitcast.18, f32[12,1,90]{2,1,0:T(1,128)} %bitcast.21), custom_call_target="tpu_custom_call" | custom-call | tf_op jit(solution)/shard_map/rim/pallas_call | solution.py:175
  2.8 0.0 collective-permute-start
  2.8 0.5 collective-permute-start.1
  3.3 1.6 %collective-permute-done.next_ref = bf16[96,256]{1,0:T(8,128)(2,1)S(1)} collective-permute-done((bf16[96,256]{1,0:T(8,128)(2,1)}, bf16[96,256]{1,0:T(8,128)(2,1)S(1)}, u32[]{:S(2)}, u32[]{:S(2)}) %collective-permute-start) | collective-permute-done | bytes 49184 | tf_op jit(solution)/shard_map/ppermute | solution.py:755
  4.9 2.2 %collective-permute-done.1.prev_ref = bf16[96,256]{1,0:T(8,128)(2,1)S(1)} collective-permute-done((bf16[96,256]{1,0:T(8,128)(2,1)}, bf16[96,256]{1,0:T(8,128)(2,1)S(1)}, u32[]{:S(2)}, u32[]{:S(2)}) %collective-permute-start.1) | collective-permute-done | bytes 49184 | tf_op jit(solution)/shard_map/ppermute | solution.py:755
  7.1 0.0 copy-done
  7.1 0.0 copy-done.2
  7.1 0.0 copy-start.20
  7.2 2.4 %prep.3 = bf16[8,240,128]{2,1,0:T(8,128)(2,1)} custom-call(s32[1]{0:T(128)} %bitcast.6.half_ref, s32[4,15]{1,0:T(4,128)S(1)} %copy-done.3, f32[2]{0:T(128)S(1)} %copy-done.7, f32[2]{0:T(128)S(1)} %copy-done.8, f32[2]{0:T(128)S(1)} %copy-done.9, bf16[12,90,2,192]{3,2,1,0:T(2,128)(2,1)S(1)} %bitcast.16, bf16[96,256]{1,0:T(8,128)(2,1)S(1)} %collective-permute-done.next_ref, ...), custom_call_target="tpu_custom_call" | custom-call | flops 1000000000 | bytes 2500000 | tf_op jit(solution)/shard_map/prep/pallas_call | solution.py:250
  9.6 7.1 %all-to-all-start.2 = ((bf16[8,240,128]{2,1,0:T(8,128)(2,1)}), bf16[8,240,128]{2,1,0:T(8,128)(2,1)S(1)}, u32[]{:S(2)}, u32[]{:S(2)}) async-start(bf16[8,240,128]{2,1,0:T(8,128)(2,1)} %prep.3), calls=%async_computation.2 | async-start | bytes 983040 | tf_op jit(solution)/shard_map/all_to_all | solution.py:746
  16.7 0.6 broadcast_in_dim.14.temp_head_ref
  17.3 2.7 %setup.1 = (bf16[576,192]{1,0:T(8,128)(2,1)}, bf16[3,192,256]{2,1,0:T(8,128)(2,1)}, f32[144,896]{1,0:T(8,128)}, f32[8,896]{1,0:T(8,128)}, f32[144,128]{1,0:T(8,128)}, /*index=5*/f32[8,256]{1,0:T(8,128)}) custom-call(bf16[192,576]{1,0:T(8,128)(2,1)} %w_ref, f32[6,144,144]{2,1,0:T(8,128)} %bias_ref, s32[8,144]{1,0:T(8,128)} %pat_ref, f32[1,192]{1,0:T(1,128)} %bitcast.26, ...), custom_call_target="tpu_custom_call" | custom-call | flops 1000000000 | bytes 3000000 | tf_op jit(solution)/shard_map/setup/pallas_call | solution.py:435
  20.0 0.0 copy-start.6
  20.1 0.0 copy-start.12
  20.1 0.0 copy-start.13
  20.1 2.4 %prep.2 = bf16[8,240,128]{2,1,0:T(8,128)(2,1)} custom-call(s32[1]{0:T(128)} %bitcast.half_ref, s32[4,15]{1,0:T(4,128)S(1)} %copy-done.3, f32[2]{0:T(128)S(1)} %copy-done.7, f32[2]{0:T(128)S(1)} %copy-done.8, f32[2]{0:T(128)S(1)} %copy-done.9, bf16[12,90,2,192]{3,2,1,0:T(2,128)(2,1)S(1)} %bitcast.17, bf16[96,256]{1,0:T(8,128)(2,1)S(1)} %collective-permute-done.next_ref, ...), custom_call_target="tpu_custom_call" | custom-call | flops 1000000000 | bytes 2500000 | tf_op jit(solution)/shard_map/prep/pallas_call | solution.py:250
  22.5 4.5 %all-to-all-done.2.x_ref = bf16[8,240,128]{2,1,0:T(8,128)(2,1)S(1)} async-done(((bf16[8,240,128]{2,1,0:T(8,128)(2,1)}), bf16[8,240,128]{2,1,0:T(8,128)(2,1)S(1)}, u32[]{:S(2)}, u32[]{:S(2)}) %all-to-all-start.2) | async-done | bytes 491552 | tf_op jit(solution)/shard_map/all_to_all | solution.py:746
  27.1 13.1 %all-to-all-start = ((bf16[8,240,128]{2,1,0:T(8,128)(2,1)}), bf16[8,240,128]{2,1,0:T(8,128)(2,1)S(1)}, u32[]{:S(2)}, u32[]{:S(2)}) async-start(bf16[8,240,128]{2,1,0:T(8,128)(2,1)} %prep.2), calls=%async_computation | async-start | bytes 983040 | tf_op jit(solution)/shard_map/all_to_all | solution.py:746
  40.2 1.0 copy-done.15
  41.1 0.9 copy-done.16
  42.0 0.7 copy-done.19
  42.7 17.8 %layer.3 = bf16[8,240,128]{2,1,0:T(8,128)(2,1)} custom-call(bf16[8,240,128]{2,1,0:T(8,128)(2,1)S(1)} %all-to-all-done.2.x_ref, bf16[144,144]{1,0:T(8,128)(2,1)S(1)} %copy-done.12, bf16[144,144]{1,0:T(8,128)(2,1)S(1)} %copy-done.12, bf16[576,192]{1,0:T(8,128)(2,1)S(1)} %copy-done.14, bf16[3,192,256]{2,1,0:T(8,128)(2,1)S(1)} %copy-done.15, ...), custom_call_target="tpu_custom_call" | custom-call | flops 20000000000 | bytes 4000000 | tf_op jit(solution)/shard_map/layer/pallas_call | solution.py:716
  60.6 0.0 all-to-all-done.x_ref
  60.6 4.2 %all-to-all-start.3 = ((bf16[8,240,128]{2,1,0:T(8,128)(2,1)}), bf16[8,240,128]{2,1,0:T(8,128)(2,1)S(1)}, u32[]{:S(2)}, u32[]{:S(2)}) async-start(bf16[8,240,128]{2,1,0:T(8,128)(2,1)} %layer.3), calls=%async_computation.3 | async-start | bytes 983040 | tf_op jit(solution)/shard_map/all_to_all | solution.py:746
  64.8 0.9 copy-done.17
  65.7 17.8 %layer.2 = bf16[8,240,128]{2,1,0:T(8,128)(2,1)} custom-call(bf16[8,240,128]{2,1,0:T(8,128)(2,1)S(1)} %all-to-all-done.x_ref, bf16[144,144]{1,0:T(8,128)(2,1)S(1)} %copy-done.12, bf16[144,144]{1,0:T(8,128)(2,1)S(1)} %copy-done.12, bf16[576,192]{1,0:T(8,128)(2,1)S(1)} %copy-done.14, bf16[3,192,256]{2,1,0:T(8,128)(2,1)S(1)} %copy-done.15, ...), custom_call_target="tpu_custom_call" | custom-call | flops 20000000000 | bytes 4000000 | tf_op jit(solution)/shard_map/layer/pallas_call | solution.py:716
  83.5 0.0 all-to-all-done.3.x_ref
  83.5 10.5 %all-to-all-start.1 = ((bf16[8,240,128]{2,1,0:T(8,128)(2,1)}), bf16[8,240,128]{2,1,0:T(8,128)(2,1)S(1)}, u32[]{:S(2)}, u32[]{:S(2)}) async-start(bf16[8,240,128]{2,1,0:T(8,128)(2,1)} %layer.2), calls=%async_computation.1 | async-start | bytes 983040 | tf_op jit(solution)/shard_map/all_to_all | solution.py:746
  94.0 1.7 %post.2 = (f32[2,12,1,90]{3,2,1,0:T(1,128)}, bf16[12,90,2,192]{3,2,1,0:T(2,128)(2,1)}) custom-call(s32[1]{0:T(128)} %bitcast.6.half_ref, bf16[8,240,128]{2,1,0:T(8,128)(2,1)S(1)} %all-to-all-done.3.x_ref, bf16[288,432]{1,0:T(8,128)(2,1)S(1)} %copy-done.10), custom_call_target="tpu_custom_call" | custom-call | flops 1000000000 | bytes 2500000 | tf_op jit(solution)/shard_map/post/pallas_call | solution.py:307
  95.7 9.2 %all-to-all-done.1.x_ref = bf16[8,240,128]{2,1,0:T(8,128)(2,1)S(1)} async-done(((bf16[8,240,128]{2,1,0:T(8,128)(2,1)}), bf16[8,240,128]{2,1,0:T(8,128)(2,1)S(1)}, u32[]{:S(2)}, u32[]{:S(2)}) %all-to-all-start.1) | async-done | bytes 491552 | tf_op jit(solution)/shard_map/all_to_all | solution.py:746
  104.9 1.7 %post.3 = (f32[2,12,1,90]{3,2,1,0:T(1,128)}, bf16[12,90,2,192]{3,2,1,0:T(2,128)(2,1)}) custom-call(s32[1]{0:T(128)} %bitcast.half_ref, bf16[8,240,128]{2,1,0:T(8,128)(2,1)S(1)} %all-to-all-done.1.x_ref, bf16[288,432]{1,0:T(8,128)(2,1)S(1)} %copy-done.10, f32[2,12,1,90]{3,2,1,0:T(1,128)} %get-tuple-element.36.refs_0_, ...), custom_call_target="tpu_custom_call", output_to_operand_aliasing={{0}: (3, {}), {1}: (4, {})} | custom-call | flops 1000000000 | bytes 2500000 | tf_op jit(solution)/shard_map/post/pallas_call | solution.py:307
  (31 shorter events, 0.1 us)
Async XLA Ops:
  0.6 6.5 %copy-start = (bf16[2,1,12,90,192]{4,0,3,2,1:T(2,128)(2,1)S(1)}, bf16[2,1,12,90,192]{4,0,3,2,1:T(2,128)(2,1)}, u32[]{:S(2)}) copy-start(bf16[2,1,12,90,192]{4,0,3,2,1:T(2,128)(2,1)} %param.20) | copy-start | bytes 2488324
  0.6 6.4 %copy-start.1 = (f32[2,1,12,90]{3,1,2,0:T(1,128)S(1)}, f32[2,1,12,90]{3,1,2,0:T(1,128)}, u32[]{:S(2)}) copy-start(f32[2,1,12,90]{3,1,2,0:T(1,128)} %param.35) | copy-start | bytes 25924
  0.7 6.4 %copy-start.2 = (f32[1,12,90]{2,0,1:T(1,128)S(1)}, f32[1,12,90]{2,0,1:T(1,128)}, u32[]{:S(2)}) copy-start(f32[1,12,90]{2,0,1:T(1,128)} %param.34) | copy-start | bytes 12964
  0.7 6.4 %copy-start.3 = (s32[4,15]{1,0:T(4,128)S(1)}, s32[4,15]{1,0:T(4,128)}, u32[]{:S(2)}) copy-start(s32[4,15]{1,0:T(4,128)} %ids_ref.5) | copy-start | bytes 724
  0.7 6.4 %copy-start.7 = (f32[2]{0:T(128)S(1)}, f32[2]{0:T(128)}, u32[]{:S(2)}) copy-start(f32[2]{0:T(128)} %thick_ref.3) | copy-start | bytes 28
  0.7 6.4 %copy-start.8 = (f32[2]{0:T(128)S(1)}, f32[2]{0:T(128)}, u32[]{:S(2)}) copy-start(f32[2]{0:T(128)} %weight_ref.3) | copy-start | bytes 28
  0.7 6.4 %copy-start.9 = (f32[2]{0:T(128)S(1)}, f32[2]{0:T(128)}, u32[]{:S(2)}) copy-start(f32[2]{0:T(128)} %base_ref.3) | copy-start | bytes 28
  0.7 6.4 %copy-start.11 = (bf16[288,384]{1,0:T(8,128)(2,1)S(1)}, bf16[288,384]{1,0:T(8,128)(2,1)}, u32[]{:S(2)}) copy-start(bf16[288,384]{1,0:T(8,128)(2,1)} %constant.40.clone.perm_ref) | copy-start | bytes 663556
  2.8 2.1 %collective-permute-start = (bf16[96,256]{1,0:T(8,128)(2,1)}, bf16[96,256]{1,0:T(8,128)(2,1)S(1)}, u32[]{:S(2)}, u32[]{:S(2)}) collective-permute-start(bf16[96,256]{1,0:T(8,128)(2,1)} %get-tuple-element.21), channel_id=1, source_target_pairs={{0,12},{4,0},{8,4},{12,8},{16,28},{20,16},{24,20},{28,24},{32,44},... | collective-permute-start | bytes 147464 | tf_op jit(solution)/shard_map/ppermute | solution.py:755
  2.8 4.3 %collective-permute-start.1 = (bf16[96,256]{1,0:T(8,128)(2,1)}, bf16[96,256]{1,0:T(8,128)(2,1)S(1)}, u32[]{:S(2)}, u32[]{:S(2)}) collective-permute-start(bf16[96,256]{1,0:T(8,128)(2,1)} %get-tuple-element.22), channel_id=1, source_target_pairs={{0,4},{4,8},{8,12},{12,0},{16,20},{20,24},{24,28},{28,16},{32,36},... | collective-permute-start | bytes 147464 | tf_op jit(solution)/shard_map/ppermute | solution.py:755
  7.1 9.6 %copy-start.20 = (bf16[192]{0:T(256)(128)(2,1)S(1)}, bf16[192]{0:T(256)(128)(2,1)}, u32[]{:S(2)}) copy-start(bf16[192]{0:T(256)(128)(2,1)} %param.30) | copy-start | bytes 1156
  9.6 17.5 %all-to-all-start.2 = ((bf16[8,240,128]{2,1,0:T(8,128)(2,1)}), bf16[8,240,128]{2,1,0:T(8,128)(2,1)S(1)}, u32[]{:S(2)}, u32[]{:S(2)}) async-start(bf16[8,240,128]{2,1,0:T(8,128)(2,1)} %prep.3), calls=%async_computation.2 | async-start | bytes 983040 | tf_op jit(solution)/shard_map/all_to_all | solution.py:746
  20.0 20.1 %copy-start.4 = (bf16[192,768]{1,0:T(8,128)(2,1)S(1)}, bf16[192,768]{1,0:T(8,128)(2,1)}, u32[]{:S(2)}) copy-start(bf16[192,768]{1,0:T(8,128)(2,1)} %expand_ref.3) | copy-start | bytes 884740
  20.0 20.1 %copy-start.5 = (bf16[768,192]{0,1:T(8,128)(2,1)S(1)}, bf16[768,192]{0,1:T(8,128)(2,1)}, u32[]{:S(2)}) copy-start(bf16[768,192]{0,1:T(8,128)(2,1)} %param.29) | copy-start | bytes 884740
  20.0 20.1 %copy-start.6 = (bf16[192,192]{1,0:T(8,128)(2,1)S(1)}, bf16[192,192]{1,0:T(8,128)(2,1)}, u32[]{:S(2)}) copy-start(bf16[192,192]{1,0:T(8,128)(2,1)} %proj_ref.3) | copy-start | bytes 221188
  20.1 20.1 %copy-start.12 = (bf16[144,144]{1,0:T(8,128)(2,1)S(1)}, bf16[144,144]{1,0:T(8,128)(2,1)}, u32[]{:S(2)}) copy-start(bf16[144,144]{1,0:T(8,128)(2,1)} %constant.42.clone.order_ref.back_ref) | copy-start | bytes 124420
  20.1 20.1 %copy-start.13 = (f32[144,896]{1,0:T(8,128)S(1)}, f32[144,896]{1,0:T(8,128)}, u32[]{:S(2)}) copy-start(f32[144,896]{1,0:T(8,128)} %get-tuple-element.31.bias_ref) | copy-start | bytes 1548292
  20.1 20.1 %copy-start.14 = (bf16[576,192]{1,0:T(8,128)(2,1)S(1)}, bf16[576,192]{1,0:T(8,128)(2,1)}, u32[]{:S(2)}) copy-start(bf16[576,192]{1,0:T(8,128)(2,1)} %get-tuple-element.29.wt_ref) | copy-start | bytes 663556
  20.1 20.1 %copy-start.18 = (f32[8,896]{1,0:T(8,128)S(1)}, f32[8,896]{1,0:T(8,128)}, u32[]{:S(2)}) copy-start(f32[8,896]{1,0:T(8,128)} %get-tuple-element.32.pat_q_ref) | copy-start | bytes 86020
  27.1 33.5 %all-to-all-start = ((bf16[8,240,128]{2,1,0:T(8,128)(2,1)}), bf16[8,240,128]{2,1,0:T(8,128)(2,1)S(1)}, u32[]{:S(2)}, u32[]{:S(2)}) async-start(bf16[8,240,128]{2,1,0:T(8,128)(2,1)} %prep.2), calls=%async_computation | async-start | bytes 983040 | tf_op jit(solution)/shard_map/all_to_all | solution.py:746
  40.2 1.0 copy-start.15
  41.1 0.9 copy-start.16
  42.0 0.7 copy-start.19
  60.6 23.0 %all-to-all-start.3 = ((bf16[8,240,128]{2,1,0:T(8,128)(2,1)}), bf16[8,240,128]{2,1,0:T(8,128)(2,1)S(1)}, u32[]{:S(2)}, u32[]{:S(2)}) async-start(bf16[8,240,128]{2,1,0:T(8,128)(2,1)} %layer.3), calls=%async_computation.3 | async-start | bytes 983040 | tf_op jit(solution)/shard_map/all_to_all | solution.py:746
  64.8 0.9 copy-start.17
  65.7 28.3 %copy-start.10 = (bf16[288,432]{1,0:T(8,128)(2,1)S(1)}, bf16[288,432]{1,0:T(8,128)(2,1)}, u32[]{:S(2)}) copy-start(bf16[288,432]{1,0:T(8,128)(2,1)} %constant.41.clone.perm_ref) | copy-start | bytes 746500
  83.5 21.3 %all-to-all-start.1 = ((bf16[8,240,128]{2,1,0:T(8,128)(2,1)}), bf16[8,240,128]{2,1,0:T(8,128)(2,1)S(1)}, u32[]{:S(2)}, u32[]{:S(2)}) async-start(bf16[8,240,128]{2,1,0:T(8,128)(2,1)} %layer.2), calls=%async_computation.1 | async-start | bytes 983040 | tf_op jit(solution)/shard_map/all_to_all | solution.py:746

commit v3 on v2

--- a/solution.py
+++ b/solution.py
@@ -378,13 +378,13 @@
 
 
 def token_rows(main, tails):
-    tails = tails.T
+    tails = tails.astype(BF16).T
     lane = lanes((16, C))
-    last = jnp.zeros((16, C), F32)
+    last = jnp.zeros((16, C), BF16)
     for h in range(HEADS):
         mine = (lane >= HEAD * h) & (lane < HEAD * h + HEAD)
         last = jnp.where(mine, tails[16 * h : 16 * h + 16], last)
-    return jnp.concatenate([main.T, last], axis=0)
+    return jnp.concatenate([main.astype(BF16).T, last], axis=0)
 
 
 def head_rows(value):
@@ -411,11 +411,11 @@
     tails = jnp.zeros((WIN, 128), F32)
     for h in range(HEADS):
         turned = bias_ref[h].T
-        bias_out_ref[:, 128 * h : 128 * h + 128] = turned[:, 0:128]
+        bias_out_ref[:, 128 * h : 128 * h + 128] = turned[:, 0:128] * LOG2E
         tail = jnp.concatenate([turned[:, 128:WIN], jnp.zeros((WIN, 112), F32)], axis=1)
         tail = roll(tail, 16 * h)
         tails = jnp.where((lane >= 16 * h) & (lane < 16 * h + 16), tail, tails)
-    bias_out_ref[:, 768:WIDE] = tails
+    bias_out_ref[:, 768:WIDE] = tails * LOG2E
     pat = pat_ref[...].astype(F32)
     for h in range(HEADS):
         pat_q_ref[:, 128 * h : 128 * h + 128] = pat[:, 0:128]
@@ -455,18 +455,14 @@
 LOG2E = 1.4426950408889634
 
 
-def interleave(runs, lag):
+def interleave(*runs):
     live = list(runs)
-    ahead = 0
     while live:
-        for k, run in enumerate(list(live)):
-            if run is runs[-1] and len(runs) > 1 and ahead < lag and runs[0] in live:
-                continue
+        for run in list(live):
             try:
                 next(run)
             except StopIteration:
                 live.remove(run)
-        ahead += 1
 
 
 PER_COLUMN = (
@@ -477,7 +473,7 @@
     ((4, WIN, WIDE), BF16),
     ((4, WIN, C), BF16),
     ((4, WIN, C), BF16),
-    ((4, WIN, C), F32),
+    ((4, C, 256), F32),
     ((4, WIN, C), F32),
     ((4, WIN, C), F32),
     ((4, WIN, 128), F32),
@@ -490,10 +486,17 @@
 
 
 def main_kernel(
-    x_ref, order_ref, back_ref, wt_ref, w_ref, bias_ref, pat_q_ref, pat_k_ref, gains_ref,
-    proj_ref, expand_ref, reduce_ref,
-    out_ref, tok_in, levels_ref, *scratch,
+    x_ref, *refs
 ):
+    given, out_ref, held = refs[:N_CONST], refs[N_CONST], refs[N_CONST + 1 : 2 * N_CONST + 1]
+    tok_in, levels_ref, sems, *scratch = refs[2 * N_CONST + 1 :]
+    copies = [
+        pltpu.make_async_copy(a, b, sems.at[k]) for k, (a, b) in enumerate(zip(given, held))
+    ]
+    for copy in copies:
+        copy.start()
+    (order_ref, back_ref, wt_ref, w_ref, bias_ref, pat_q_ref, pat_k_ref, gains_ref, proj_ref,
+     expand_ref, reduce_ref) = held
     columns = (scratch[: len(PER_COLUMN)], scratch[len(PER_COLUMN) :])
     scale_q = 1.0 / HEAD**0.5
     lane72 = lanes((HALF, 128))
@@ -522,6 +525,7 @@
         jnp.where((pick_row >= 64) & (pick_row < 67), 1.0, 0.0),
         jnp.where((pick_row >= 67) & (pick_row < 70), 1.0, 0.0),
     ).astype(BF16)
+    copies[0].wait()
     for p in range(4):
         for a in range(2):
             pieces = []
@@ -535,6 +539,8 @@
                 columns[col][0][p, rows, :] = moved[HALF * col : HALF * col + HALF]
                 columns[col][13][p, rows, :] = fields[HALF * col : HALF * col + HALF]
 
+    for copy in copies[1:]:
+        copy.wait()
     gain_one = gains_ref[0:1, 0:C]
     gain_two = gains_ref[1:2, 0:C]
     head_row = gains_ref[2:3, 0:C]
@@ -578,14 +584,14 @@
         ones = jnp.where((lane_wide == C) | (lane_wide == C + 1), 1.0, 0.0)
         values = (values + ones)[:, 0:208].astype(BF16)
         yield
-        scores = dot(keys, diag_q[...]) + bias_ref[...] * LOG2E
+        scores = dot(keys, diag_q[...]) + bias_ref[...]
         yield
         raised = jnp.exp2(scores - jnp.max(scores, axis=0, keepdims=True))
         weights = (raised * (1.0 / jnp.sum(raised, axis=0, keepdims=True))).astype(BF16)
         probs[p] = weights
         yield
         main, tails = per_head(values_t, weights)
-        context = token_rows(main, tails).astype(BF16)
+        context = token_rows(main, tails)
         yield
         middle = (x + dot(context, proj_ref[...])).astype(BF16).astype(F32)
         hat_two, scale_two = norm_parts(middle)
@@ -599,12 +605,12 @@
             at = slice(256 * f, 256 * f + 256)
             pre = dot(normed_two, expand_ref[:, at])
             u = u_row[:, at]
-            square = pre * pre
-            gate = 0.5 + 0.5 * jnp.tanh(pre * (c0 + c1 * square))
+            gate = 0.5 + 0.5 * jnp.tanh(pre * (c0 + c1 * (pre * pre)))
             unit = pre * gate
             acc = acc + unit * u
-            slope = gate * (1.0 + (pre - unit) * (2.0 * c0 + (6.0 * c1) * square))
-            back = back + dot_nt((slope * u).astype(BF16), expand_ref[:, at])
+            pre, gate, unit = pre.astype(BF16), gate.astype(BF16), unit.astype(BF16)
+            slope = gate * (1.0 + (pre - unit) * (2.0 * c0 + (6.0 * c1) * (pre * pre)))
+            back = back + dot_nt(slope * u.astype(BF16), expand_ref[:, at])
             yield
         delta = jnp.sum(acc, axis=1, keepdims=True) + jnp.sum(
             middle * head_row, axis=1, keepdims=True
@@ -631,14 +637,15 @@
         n_rows[p] = dot_nt(kept, proj_ref[...]).astype(BF16)
         yield
         dweights = dot(values, diag_n[...])
-        dscore = (probs[p].astype(F32) * dweights).astype(BF16)
+        dscore = probs[p] * dweights.astype(BF16)
         dscores[p] = dscore
         yield
         main, tails = per_head(keys_t, dscore)
-        dq_rows[p] = token_rows(main, tails)
+        dq_rows[p, :, 0:128] = main
+        dq_rows[p, :, 128:256] = tails
 
     def forward_step(p, carry):
-        interleave([forward(p, 0), forward(p, 1)], LAG)
+        interleave(forward(p, 0), forward(p, 1))
         return carry
 
     lax.fori_loop(0, 4, forward_step, 0)
@@ -677,7 +684,8 @@
         yield
         dv = dot(probs[p], head_rows(s * n_rows[p].astype(F32))).astype(BF16)
         yield
-        dq = ((s * scale_q) * dq_rows[p]).astype(BF16)
+        dq = token_rows(dq_rows[p, :, 0:128], dq_rows[p, :, 128:256])
+        dq = ((s * scale_q) * dq.astype(F32)).astype(BF16)
         dnormed = (
             dot(dq, wt_ref[0:C, :]) + dot(dk, wt_ref[C : 2 * C, :]) + dot(dv, wt_ref[2 * C :, :])
         )
@@ -691,7 +699,7 @@
         made[p, :, 128:256] = last.astype(BF16)
 
     def backward_step(p, carry):
-        interleave([backward(p, 0), backward(p, 1)], 0)
+        interleave(backward(p, 0), backward(p, 1))
         return carry
 
     lax.fori_loop(0, 4, backward_step, 0)
@@ -709,21 +717,23 @@
         pack_block(out_ref, s, tok_in[s], zero)
 
 
-LAG = 0
+N_CONST = 11
 
 
 def layer(x, consts):
     return pl.pallas_call(
         main_kernel,
         out_shape=jax.ShapeDtypeStruct((GROUP, ROWS, 128), BF16),
-        in_specs=[vmem()] * (1 + len(consts)),
+        in_specs=[vmem()] + [pl.BlockSpec(memory_space=pltpu.HBM)] * N_CONST,
         out_specs=vmem(),
-        scratch_shapes=[
+        scratch_shapes=[pltpu.VMEM(c.shape, c.dtype) for c in consts]
+        + [
             pltpu.VMEM((GROUP, WIN, 256), F32),
             pltpu.VMEM((4, 16, 128), F32),
+            pltpu.SemaphoreType.DMA((N_CONST,)),
         ]
         + [pltpu.VMEM(shape, kind) for shape, kind in PER_COLUMN] * 2,
-        compiler_params=pltpu.CompilerParams(vmem_limit_bytes=VMEM_LIMIT),
+        compiler_params=pltpu.CompilerParams(vmem_limit_bytes=VMEM_ALL),
         cost_estimate=pl.CostEstimate(
             flops=20_000_000_000, bytes_accessed=4_000_000, transcendentals=3_000_000
         ),
@@ -734,7 +744,7 @@
 def pair_groups(odd):
     out = []
     for block in range(BLOCKS):
-        for band in range(odd, BANDS, 2):
+        for band in range((odd + block) % 2, BANDS, 2):
             members = (band, (band + 1) % BANDS)
             out.append(
                 [(b * BLOCKS + block) * LEVS + lev for b in members for lev in range(LEVS)]
@@ -767,7 +777,8 @@
     before = block_step(before, 1)
 
     band = lax.axis_index("tile") // BLOCKS
-    even = (band % 2 == 0).astype(jnp.int32)
+    block = lax.axis_index("tile") % BLOCKS
+    even = ((band + block) % 2 == 0).astype(jnp.int32)
     halves = [even.reshape(1), (1 - even).reshape(1)]
     perm = jnp.asarray(source_rows(), BF16)
     perm_back = jnp.asarray(target_rows(), BF16)

time: 107 us -> 100 us (0.935)
  the two profiles are of different devices: /device:TPU:32 before, /device:TPU:1 now
where the time goes in v3:
time: 100 us; the launch traced here: 99.3 us
  Pallas kernels  51.1 us (51%)
  starting transfers between devices  34.1 us (34%)
  waiting for transfers between devices  12.6 us (13%)
    pallas_call x2, Pallas kernels, layer(): pl.pallas_call(main_kernel, out_shape=jax.ShapeDtypeStruct((GROUP, ROWS,...  38.2 us
    all_to_all x4, starting transfers between devices, exchange(): lax.all_to_all(blocks, ('tile', 'lev'), 0, 0, axis_index_groups=pair_grou...  30.9 us
    all_to_all x4, waiting for transfers between devices, exchange(): lax.all_to_all(blocks, ('tile', 'lev'), 0, 0, axis_index_groups=pair_grou...  10.9 us
    pallas_call x2, Pallas kernels, prep(): pl.pallas_call(prep_kernel, out_shape=jax.ShapeDtypeStruct((GROUP, ROWS,...  4.83 us
    pallas_call x2, Pallas kernels, post(): pl.pallas_call(post_kernel, out_shape=(jax.ShapeDtypeStruct((2, 12, 1, LO...  3.34 us
    ppermute x2, starting transfers between devices, block_step(): return lax.ppermute(value, 'tile', pairs)  3.24 us
    pallas_call x1, Pallas kernels, setup(): pl.pallas_call(setup_kernel, out_shape=(jax.ShapeDtypeStruct((3 * C, C),...  2.74 us
    pallas_call x1, Pallas kernels, rim(): pl.pallas_call(rim_kernel, out_shape=(edge, edge), grid=(1,), in_specs=[s...  2.08 us
  transfers between devices with their start and end apart: 6, of which 3 were waited for; matrix products, arithmetic and copies ran while one was open for 1% of the time, Pallas kernels for 45%

profile of v3, /device:TPU:1, one launch (start us, length us, event | category | flops | bytes accessed | tf_op | source)
XLA Modules:
  0.0 99.3 jit_solution(7155166647384456953)
XLA Ops:
  0.6 0.0 copy-start
  0.6 0.0 copy-start.1
  0.7 0.0 copy-start.8
  0.7 2.1 %rim.1 = (bf16[96,256]{1,0:T(8,128)(2,1)}, bf16[96,256]{1,0:T(8,128)(2,1)}) custom-call(s32[4,15]{1,0:T(4,128)} %ids_ref.5, bf16[12,90,2,192]{3,2,1,0:T(2,128)(2,1)} %bitcast.14, bf16[12,90,2,192]{3,2,1,0:T(2,128)(2,1)} %bitcast.15, f32[2,12,1,90]{3,2,1,0:T(1,128)} %bitcast.18, f32[12,1,90]{2,1,0:T(1,128)} %bitcast.21), custom_call_target="tpu_custom_call" | custom-call | tf_op jit(solution)/shard_map/rim/pallas_call | solution.py:175
  2.8 3.2 %collective-permute-start = (bf16[96,256]{1,0:T(8,128)(2,1)}, bf16[96,256]{1,0:T(8,128)(2,1)S(1)}, u32[]{:S(2)}, u32[]{:S(2)}) collective-permute-start(bf16[96,256]{1,0:T(8,128)(2,1)} %get-tuple-element.21), channel_id=1, source_target_pairs={{0,12},{4,0},{8,4},{12,8},{16,28},{20,16},{24,20},{28,24},{32,44},... | collective-permute-start | bytes 147464 | tf_op jit(solution)/shard_map/ppermute | solution.py:765
  6.0 0.0 collective-permute-start.1
  6.0 1.8 %collective-permute-done.next_ref = bf16[96,256]{1,0:T(8,128)(2,1)S(1)} collective-permute-done((bf16[96,256]{1,0:T(8,128)(2,1)}, bf16[96,256]{1,0:T(8,128)(2,1)S(1)}, u32[]{:S(2)}, u32[]{:S(2)}) %collective-permute-start) | collective-permute-done | bytes 49184 | tf_op jit(solution)/shard_map/ppermute | solution.py:765
  7.8 0.0 collective-permute-done.1.prev_ref
  7.8 0.0 copy-done.1
  7.8 0.0 copy-done.2
  7.8 0.0 copy-done.3
  7.8 0.0 copy-done.4
  7.8 0.0 copy-done.5
  7.9 0.0 copy-done.6
  7.9 0.0 copy-done.8
  7.9 0.0 copy-start.11
  7.9 2.4 %prep.3 = bf16[8,240,128]{2,1,0:T(8,128)(2,1)} custom-call(s32[1]{0:T(128)} %bitcast.6.half_ref, s32[4,15]{1,0:T(4,128)S(1)} %copy-done.3, f32[2]{0:T(128)S(1)} %copy-done.4, f32[2]{0:T(128)S(1)} %copy-done.5, f32[2]{0:T(128)S(1)} %copy-done.6, bf16[12,90,2,192]{3,2,1,0:T(2,128)(2,1)S(1)} %bitcast.16, bf16[96,256]{1,0:T(8,128)(2,1)S(1)} %collective-permute-done.next_ref, ...), custom_call_target="tpu_custom_call" | custom-call | flops 1000000000 | bytes 2500000 | tf_op jit(solution)/shard_map/prep/pallas_call | solution.py:250
  10.3 12.4 %all-to-all-start.2 = ((bf16[8,240,128]{2,1,0:T(8,128)(2,1)}), bf16[8,240,128]{2,1,0:T(8,128)(2,1)S(1)}, u32[]{:S(2)}, u32[]{:S(2)}) async-start(bf16[8,240,128]{2,1,0:T(8,128)(2,1)} %prep.3), calls=%async_computation.2 | async-start | bytes 983040 | tf_op jit(solution)/shard_map/all_to_all | solution.py:756
  22.7 0.5 broadcast_in_dim.14.temp_head_ref
  23.3 2.7 %setup.1 = (bf16[576,192]{1,0:T(8,128)(2,1)}, bf16[3,192,256]{2,1,0:T(8,128)(2,1)}, f32[144,896]{1,0:T(8,128)}, f32[8,896]{1,0:T(8,128)}, f32[144,128]{1,0:T(8,128)}, /*index=5*/f32[8,256]{1,0:T(8,128)}) custom-call(bf16[192,576]{1,0:T(8,128)(2,1)} %w_ref, f32[6,144,144]{2,1,0:T(8,128)} %bias_ref, s32[8,144]{1,0:T(8,128)} %pat_ref, f32[1,192]{1,0:T(1,128)} %bitcast.26, ...), custom_call_target="tpu_custom_call" | custom-call | flops 1000000000 | bytes 3000000 | tf_op jit(solution)/shard_map/setup/pallas_call | solution.py:435
  26.0 2.4 %prep.2 = bf16[8,240,128]{2,1,0:T(8,128)(2,1)} custom-call(s32[1]{0:T(128)} %bitcast.half_ref, s32[4,15]{1,0:T(4,128)S(1)} %copy-done.3, f32[2]{0:T(128)S(1)} %copy-done.4, f32[2]{0:T(128)S(1)} %copy-done.5, f32[2]{0:T(128)S(1)} %copy-done.6, bf16[12,90,2,192]{3,2,1,0:T(2,128)(2,1)S(1)} %bitcast.17, bf16[96,256]{1,0:T(8,128)(2,1)S(1)} %collective-permute-done.next_ref, ...), custom_call_target="tpu_custom_call" | custom-call | flops 1000000000 | bytes 2500000 | tf_op jit(solution)/shard_map/prep/pallas_call | solution.py:250
  28.4 1.8 %all-to-all-done.2.x_ref = bf16[8,240,128]{2,1,0:T(8,128)(2,1)S(1)} async-done(((bf16[8,240,128]{2,1,0:T(8,128)(2,1)}), bf16[8,240,128]{2,1,0:T(8,128)(2,1)S(1)}, u32[]{:S(2)}, u32[]{:S(2)}) %all-to-all-start.2) | async-done | bytes 491552 | tf_op jit(solution)/shard_map/all_to_all | solution.py:756
  30.2 4.9 %all-to-all-start = ((bf16[8,240,128]{2,1,0:T(8,128)(2,1)}), bf16[8,240,128]{2,1,0:T(8,128)(2,1)S(1)}, u32[]{:S(2)}, u32[]{:S(2)}) async-start(bf16[8,240,128]{2,1,0:T(8,128)(2,1)} %prep.2), calls=%async_computation | async-start | bytes 983040 | tf_op jit(solution)/shard_map/all_to_all | solution.py:756
  35.1 19.1 %layer.3 = bf16[8,240,128]{2,1,0:T(8,128)(2,1)} custom-call(bf16[8,240,128]{2,1,0:T(8,128)(2,1)} %copy-done.9, bf16[144,144]{1,0:T(8,128)(2,1)} %constant.50.clone.refs_0_.refs_1_, bf16[144,144]{1,0:T(8,128)(2,1)} %constant.50.clone.refs_0_.refs_1_, bf16[576,192]{1,0:T(8,128)(2,1)} %get-tuple-element.29.refs_2_, ...), custom_call_target="tpu_custom_call" | custom-call | flops 20000000000 | bytes 4000000 | tf_op jit(solution)/shard_map/layer/pallas_call | solution.py:724
  54.2 0.0 all-to-all-done.x_ref
  54.2 9.6 %all-to-all-start.3 = ((bf16[8,240,128]{2,1,0:T(8,128)(2,1)}), bf16[8,240,128]{2,1,0:T(8,128)(2,1)S(1)}, u32[]{:S(2)}, u32[]{:S(2)}) async-start(bf16[8,240,128]{2,1,0:T(8,128)(2,1)} %layer.3), calls=%async_computation.3 | async-start | bytes 983040 | tf_op jit(solution)/shard_map/all_to_all | solution.py:756
  63.8 19.1 %layer.2 = bf16[8,240,128]{2,1,0:T(8,128)(2,1)} custom-call(bf16[8,240,128]{2,1,0:T(8,128)(2,1)} %copy-done.10, bf16[144,144]{1,0:T(8,128)(2,1)} %constant.50.clone.refs_0_.refs_1_, bf16[144,144]{1,0:T(8,128)(2,1)} %constant.50.clone.refs_0_.refs_1_, bf16[576,192]{1,0:T(8,128)(2,1)} %get-tuple-element.29.refs_2_, ...), custom_call_target="tpu_custom_call" | custom-call | flops 20000000000 | bytes 4000000 | tf_op jit(solution)/shard_map/layer/pallas_call | solution.py:724
  82.9 0.0 all-to-all-done.3.x_ref
  83.0 4.0 %all-to-all-start.1 = ((bf16[8,240,128]{2,1,0:T(8,128)(2,1)}), bf16[8,240,128]{2,1,0:T(8,128)(2,1)S(1)}, u32[]{:S(2)}, u32[]{:S(2)}) async-start(bf16[8,240,128]{2,1,0:T(8,128)(2,1)} %layer.2), calls=%async_computation.1 | async-start | bytes 983040 | tf_op jit(solution)/shard_map/all_to_all | solution.py:756
  86.9 1.7 %post.2 = (f32[2,12,1,90]{3,2,1,0:T(1,128)}, bf16[12,90,2,192]{3,2,1,0:T(2,128)(2,1)}) custom-call(s32[1]{0:T(128)} %bitcast.6.half_ref, bf16[8,240,128]{2,1,0:T(8,128)(2,1)S(1)} %all-to-all-done.3.x_ref, bf16[288,432]{1,0:T(8,128)(2,1)S(1)} %copy-done.7), custom_call_target="tpu_custom_call" | custom-call | flops 1000000000 | bytes 2500000 | tf_op jit(solution)/shard_map/post/pallas_call | solution.py:307
  88.6 9.1 %all-to-all-done.1.x_ref = bf16[8,240,128]{2,1,0:T(8,128)(2,1)S(1)} async-done(((bf16[8,240,128]{2,1,0:T(8,128)(2,1)}), bf16[8,240,128]{2,1,0:T(8,128)(2,1)S(1)}, u32[]{:S(2)}, u32[]{:S(2)}) %all-to-all-start.1) | async-done | bytes 491552 | tf_op jit(solution)/shard_map/all_to_all | solution.py:756
  97.7 1.7 %post.3 = (f32[2,12,1,90]{3,2,1,0:T(1,128)}, bf16[12,90,2,192]{3,2,1,0:T(2,128)(2,1)}) custom-call(s32[1]{0:T(128)} %bitcast.half_ref, bf16[8,240,128]{2,1,0:T(8,128)(2,1)S(1)} %all-to-all-done.1.x_ref, bf16[288,432]{1,0:T(8,128)(2,1)S(1)} %copy-done.7, f32[2,12,1,90]{3,2,1,0:T(1,128)} %get-tuple-element.36.refs_0_, ...), custom_call_target="tpu_custom_call", output_to_operand_aliasing={{0}: (3, {}), {1}: (4, {})} | custom-call | flops 1000000000 | bytes 2500000 | tf_op jit(solution)/shard_map/post/pallas_call | solution.py:307
  (13 shorter events, 0.0 us)
Async XLA Ops:
  0.6 7.2 %copy-start = (bf16[2,1,12,90,192]{4,0,3,2,1:T(2,128)(2,1)S(1)}, bf16[2,1,12,90,192]{4,0,3,2,1:T(2,128)(2,1)}, u32[]{:S(2)}) copy-start(bf16[2,1,12,90,192]{4,0,3,2,1:T(2,128)(2,1)} %param.20) | copy-start | bytes 2488324
  0.6 7.2 %copy-start.1 = (f32[2,1,12,90]{3,1,2,0:T(1,128)S(1)}, f32[2,1,12,90]{3,1,2,0:T(1,128)}, u32[]{:S(2)}) copy-start(f32[2,1,12,90]{3,1,2,0:T(1,128)} %param.35) | copy-start | bytes 25924
  0.7 7.2 %copy-start.2 = (f32[1,12,90]{2,0,1:T(1,128)S(1)}, f32[1,12,90]{2,0,1:T(1,128)}, u32[]{:S(2)}) copy-start(f32[1,12,90]{2,0,1:T(1,128)} %param.34) | copy-start | bytes 12964
  0.7 7.2 %copy-start.3 = (s32[4,15]{1,0:T(4,128)S(1)}, s32[4,15]{1,0:T(4,128)}, u32[]{:S(2)}) copy-start(s32[4,15]{1,0:T(4,128)} %ids_ref.5) | copy-start | bytes 724
  0.7 7.2 %copy-start.4 = (f32[2]{0:T(128)S(1)}, f32[2]{0:T(128)}, u32[]{:S(2)}) copy-start(f32[2]{0:T(128)} %thick_ref.3) | copy-start | bytes 28
  0.7 7.2 %copy-start.5 = (f32[2]{0:T(128)S(1)}, f32[2]{0:T(128)}, u32[]{:S(2)}) copy-start(f32[2]{0:T(128)} %weight_ref.3) | copy-start | bytes 28
  0.7 7.2 %copy-start.6 = (f32[2]{0:T(128)S(1)}, f32[2]{0:T(128)}, u32[]{:S(2)}) copy-start(f32[2]{0:T(128)} %base_ref.3) | copy-start | bytes 28
  0.7 7.2 %copy-start.8 = (bf16[288,384]{1,0:T(8,128)(2,1)S(1)}, bf16[288,384]{1,0:T(8,128)(2,1)}, u32[]{:S(2)}) copy-start(bf16[288,384]{1,0:T(8,128)(2,1)} %constant.48.clone.perm_ref) | copy-start | bytes 663556
  2.8 5.0 %collective-permute-start = (bf16[96,256]{1,0:T(8,128)(2,1)}, bf16[96,256]{1,0:T(8,128)(2,1)S(1)}, u32[]{:S(2)}, u32[]{:S(2)}) collective-permute-start(bf16[96,256]{1,0:T(8,128)(2,1)} %get-tuple-element.21), channel_id=1, source_target_pairs={{0,12},{4,0},{8,4},{12,8},{16,28},{20,16},{24,20},{28,24},{32,44},... | collective-permute-start | bytes 147464 | tf_op jit(solution)/shard_map/ppermute | solution.py:765
  6.0 1.8 %collective-permute-start.1 = (bf16[96,256]{1,0:T(8,128)(2,1)}, bf16[96,256]{1,0:T(8,128)(2,1)S(1)}, u32[]{:S(2)}, u32[]{:S(2)}) collective-permute-start(bf16[96,256]{1,0:T(8,128)(2,1)} %get-tuple-element.22), channel_id=1, source_target_pairs={{0,4},{4,8},{8,12},{12,0},{16,20},{20,24},{24,28},{28,16},{32,36},... | collective-permute-start | bytes 147464 | tf_op jit(solution)/shard_map/ppermute | solution.py:765
  7.9 14.8 %copy-start.11 = (bf16[192]{0:T(256)(128)(2,1)S(1)}, bf16[192]{0:T(256)(128)(2,1)}, u32[]{:S(2)}) copy-start(bf16[192]{0:T(256)(128)(2,1)} %param.30) | copy-start | bytes 1156
  10.3 19.9 %all-to-all-start.2 = ((bf16[8,240,128]{2,1,0:T(8,128)(2,1)}), bf16[8,240,128]{2,1,0:T(8,128)(2,1)S(1)}, u32[]{:S(2)}, u32[]{:S(2)}) async-start(bf16[8,240,128]{2,1,0:T(8,128)(2,1)} %prep.3), calls=%async_computation.2 | async-start | bytes 983040 | tf_op jit(solution)/shard_map/all_to_all | solution.py:756
  30.2 4.9 %copy-start.9 = (bf16[8,240,128]{2,1,0:T(8,128)(2,1)}, bf16[8,240,128]{2,1,0:T(8,128)(2,1)S(1)}, u32[]{:S(2)}) copy-start(bf16[8,240,128]{2,1,0:T(8,128)(2,1)S(1)} %all-to-all-done.2.x_ref) | copy-start | bytes 1474564
  30.2 24.0 %all-to-all-start = ((bf16[8,240,128]{2,1,0:T(8,128)(2,1)}), bf16[8,240,128]{2,1,0:T(8,128)(2,1)S(1)}, u32[]{:S(2)}, u32[]{:S(2)}) async-start(bf16[8,240,128]{2,1,0:T(8,128)(2,1)} %prep.2), calls=%async_computation | async-start | bytes 983040 | tf_op jit(solution)/shard_map/all_to_all | solution.py:756
  54.2 9.7 %copy-start.10 = (bf16[8,240,128]{2,1,0:T(8,128)(2,1)}, bf16[8,240,128]{2,1,0:T(8,128)(2,1)S(1)}, u32[]{:S(2)}) copy-start(bf16[8,240,128]{2,1,0:T(8,128)(2,1)S(1)} %all-to-all-done.x_ref) | copy-start | bytes 1474564
  54.2 28.8 %all-to-all-start.3 = ((bf16[8,240,128]{2,1,0:T(8,128)(2,1)}), bf16[8,240,128]{2,1,0:T(8,128)(2,1)S(1)}, u32[]{:S(2)}, u32[]{:S(2)}) async-start(bf16[8,240,128]{2,1,0:T(8,128)(2,1)} %layer.3), calls=%async_computation.3 | async-start | bytes 983040 | tf_op jit(solution)/shard_map/all_to_all | solution.py:756
  63.8 23.1 %copy-start.7 = (bf16[288,432]{1,0:T(8,128)(2,1)S(1)}, bf16[288,432]{1,0:T(8,128)(2,1)}, u32[]{:S(2)}) copy-start(bf16[288,432]{1,0:T(8,128)(2,1)} %constant.49.clone.perm_ref) | copy-start | bytes 746500
  83.0 14.7 %all-to-all-start.1 = ((bf16[8,240,128]{2,1,0:T(8,128)(2,1)}), bf16[8,240,128]{2,1,0:T(8,128)(2,1)S(1)}, u32[]{:S(2)}, u32[]{:S(2)}) async-start(bf16[8,240,128]{2,1,0:T(8,128)(2,1)} %layer.2), calls=%async_computation.1 | async-start | bytes 983040 | tf_op jit(solution)/shard_map/all_to_all | solution.py:756

commit v4 on v3

--- a/solution.py
+++ b/solution.py
@@ -195,18 +195,23 @@
 def prep_kernel(
     half_ref, ids_ref, thick_ref, weight_ref, base_ref,
     f_ref, next_ref, prev_ref, target_ref, surface_ref, perm_ref,
-    out_ref, rows_ref,
+    out_ref, rows_ref, packed, sems,
 ):
+    upper = half_ref[0] == 1
+    start = 6 * half_ref[0]
     targets = [
-        jnp.concatenate([target_ref[lev, r] for r in range(6)], axis=0) for lev in range(2)
+        jnp.concatenate([target_ref[lev, start + r] for r in range(6)], axis=0)
+        for lev in range(2)
     ]
-    ground = jnp.concatenate([surface_ref[r] for r in range(6)], axis=0)
+    ground = jnp.concatenate([surface_ref[start + r] for r in range(6)], axis=0)
     values = dot_nt(lon_pick(2 * LONS, 0), field_rows(targets, ground, 6, 8))
-    after = next_ref[...].astype(F32)
-    before = prev_ref[...].astype(F32)
+    after, before = (
+        jnp.where(upper, ref[48:96].astype(F32), ref[0:48].astype(F32))
+        for ref in (next_ref, prev_ref)
+    )
     lane = lanes((2 * LONS, 128))
     for r in range(6):
-        tokens = f_ref[r].reshape(2 * LONS, C).astype(F32)
+        tokens = f_ref[start + r].reshape(2 * LONS, C).astype(F32)
         second = jnp.concatenate([tokens[:, 128:C], jnp.zeros((2 * LONS, 64), F32)], axis=1)
         extra = jnp.where(lane < 72, roll(values, 64 - 8 * r), 0.0)
         second = jnp.where(lane < 64, second, extra)
@@ -243,28 +248,23 @@
                     else:
                         ident = before[0:1, 200 + p : 201 + p]
                     spare = jnp.where((row16 == 2 + p) & (lane16 == 81 + col), ident, spare)
-            pack_block(out_ref, d, made[WIN * q : WIN * q + WIN], spare)
+            pack_block(packed, d, made[WIN * q : WIN * q + WIN], spare)
+            pltpu.make_async_copy(packed.at[d], out_ref.at[d], sems.at[d]).start()
+    for d in range(GROUP):
+        pltpu.make_async_copy(packed.at[d], out_ref.at[d], sems.at[d]).wait()
 
 
 def prep(half, ids, thick, weight, base, feats, after, before, target, surface, perm):
     return pl.pallas_call(
         prep_kernel,
         out_shape=jax.ShapeDtypeStruct((GROUP, ROWS, 128), BF16),
-        grid_spec=pltpu.PrefetchScalarGridSpec(
-            num_scalar_prefetch=1,
-            grid=(1,),
-            in_specs=[smem()] * 4
-            + [
-                pl.BlockSpec((6, LONS, 2, C), lambda i, h: (h[0], 0, 0, 0)),
-                pl.BlockSpec((48, 256), lambda i, h: (h[0], 0)),
-                pl.BlockSpec((48, 256), lambda i, h: (h[0], 0)),
-                pl.BlockSpec((2, 6, 1, LONS), lambda i, h: (0, h[0], 0, 0)),
-                pl.BlockSpec((6, 1, LONS), lambda i, h: (h[0], 0, 0)),
-                pl.BlockSpec((2 * WIN, 384), lambda i, h: (0, 0)),
-            ],
-            out_specs=pl.BlockSpec((GROUP, ROWS, 128), lambda i, h: (0, 0, 0)),
-            scratch_shapes=[pltpu.VMEM((6 * 208, 256), BF16)],
-        ),
+        in_specs=[smem()] * 5 + [vmem()] * 6,
+        out_specs=pl.BlockSpec(memory_space=pl.ANY),
+        scratch_shapes=[
+            pltpu.VMEM((6 * 208, 256), BF16),
+            pltpu.VMEM((GROUP, ROWS, 128), BF16),
+            pltpu.SemaphoreType.DMA((GROUP,)),
+        ],
         compiler_params=pltpu.CompilerParams(vmem_limit_bytes=SMALL_VMEM),
         cost_estimate=pl.CostEstimate(
             flops=1_000_000_000, bytes_accessed=2_500_000, transcendentals=0
@@ -274,7 +274,12 @@
 
 
 def post_kernel(half_ref, x_ref, perm_ref, *refs):
-    height_ref, grad_ref, rows_ref = refs[-3:]
+    height_out, grad_out, rows_ref, height_ref, grad_ref, sems = refs[-6:]
+    start = 6 * half_ref[0]
+    copies = [
+        pltpu.make_async_copy(grad_ref, grad_out.at[pl.ds(start, 6)], sems.at[0]),
+        pltpu.make_async_copy(height_ref, height_out.at[:, pl.ds(start, 6)], sems.at[1]),
+    ]
     for d in range(GROUP):
         first, second, _ = unpack_block(x_ref[d])
         rows_ref[d, :, 0:128] = first.astype(BF16)
@@ -292,6 +297,7 @@
             moved = roll(made[48 * r : 48 * r + 48, 128:256], 8 * r - 64)
             column = jnp.where((lane >= 8 * r) & (lane < 8 * r + 3), moved, column)
         columns.append(column)
+    copies[0].start()
     columns = jnp.concatenate(columns, axis=0).astype(BF16)
     rows = lax.dot_general(
         columns, lon_pick(192, 0), (((0,), (0,)), ((), ())), preferred_element_type=F32
@@ -300,6 +306,9 @@
         row = rows[8 * r : 8 * r + 1] + rows[8 * r + 1 : 8 * r + 2] + rows[8 * r + 2 : 8 * r + 3]
         for lev in range(2):
             height_ref[lev, r] = row[:, 128 * lev : 128 * lev + LONS]
+    copies[1].start()
+    for copy in copies:
+        copy.wait()
 
 
 def post(half, blocks, perm, earlier):
@@ -310,20 +319,14 @@
             jax.ShapeDtypeStruct((2, 12, 1, LONS), F32),
             jax.ShapeDtypeStruct((12, LONS, 2, C), BF16),
         ),
-        grid_spec=pltpu.PrefetchScalarGridSpec(
-            num_scalar_prefetch=1,
-            grid=(1,),
-            in_specs=[
-                pl.BlockSpec((GROUP, ROWS, 128), lambda i, h: (0, 0, 0)),
-                pl.BlockSpec((6 * 48, 3 * WIN), lambda i, h: (0, 0)),
-            ]
-            + [pl.BlockSpec(memory_space=pl.ANY) for _ in kept],
-            out_specs=(
-                pl.BlockSpec((2, 6, 1, LONS), lambda i, h: (0, h[0], 0, 0)),
-                pl.BlockSpec((6, LONS, 2, C), lambda i, h: (h[0], 0, 0, 0)),
-            ),
-            scratch_shapes=[pltpu.VMEM((GROUP, WIN, 256), BF16)],
-        ),
+        in_specs=[smem(), vmem(), vmem()] + [pl.BlockSpec(memory_space=pl.ANY) for _ in kept],
+        out_specs=(pl.BlockSpec(memory_space=pl.ANY), pl.BlockSpec(memory_space=pl.ANY)),
+        scratch_shapes=[
+            pltpu.VMEM((GROUP, WIN, 256), BF16),
+            pltpu.VMEM((2, 6, 1, LONS), F32),
+            pltpu.VMEM((6, LONS, 2, C), BF16),
+            pltpu.SemaphoreType.DMA((2,)),
+        ],
         input_output_aliases={3: 0, 4: 1} if kept else {},
         compiler_params=pltpu.CompilerParams(vmem_limit_bytes=SMALL_VMEM),
         cost_estimate=pl.CostEstimate(
@@ -370,10 +373,10 @@
 
 
 def per_head(turned, weights):
-    main = [
-        dot(turned[HEAD * h : HEAD * h + HEAD], weights[:, 128 * h : 128 * h + 128])
-        for h in range(HEADS)
-    ]
+    main = []
+    for c in range(3):
+        two = dot(turned[64 * c : 64 * c + 64], weights[:, 256 * c : 256 * c + 256])
+        main += [two[0:HEAD, 0:128], two[HEAD:64, 128:256]]
     return jnp.concatenate(main, axis=0), dot(turned, weights[:, 768:WIDE])
 
 
@@ -398,15 +401,10 @@
 
 
 def setup_kernel(
-    w_ref, bias_ref, pat_ref, attn_gain_ref, mlp_gain_ref, temp_head_ref,
-    wt_ref, w3_ref, bias_out_ref, pat_q_ref, pat_k_ref, gains_ref,
+    w_ref, bias_ref, pat_ref, attn_gain_ref, mlp_gain_ref, temp_head_ref, reduce_ref,
+    wt_ref, bias_out_ref, pat_q_ref, pat_k_ref, gains_ref, u_ref,
 ):
-    whole = w_ref[...].astype(F32)
-    wt_ref[...] = whole.T.astype(BF16)
-    for k in range(3):
-        piece = whole[:, C * k : C * k + C]
-        piece = jnp.concatenate([piece, jnp.zeros((C, 64), F32)], axis=1)
-        w3_ref[k] = piece.astype(BF16)
+    wt_ref[...] = w_ref[...].astype(F32).T.astype(BF16)
     lane = lanes((WIN, 128))
     tails = jnp.zeros((WIN, 128), F32)
     for h in range(HEADS):
@@ -428,28 +426,30 @@
     gains_ref[...] = jnp.zeros((8, 256), F32)
     gains_ref[0:1, 0:C] = attn_gain_ref[...]
     gains_ref[1:2, 0:C] = mlp_gain_ref[...]
-    gains_ref[2:3, 0:C] = temp_head_ref[...].astype(F32)
-
-
-def setup(w_qkv, window_bias, patterns, attn_gain, mlp_gain, temp_head):
+    head_row = temp_head_ref[...].astype(F32)
+    gains_ref[2:3, 0:C] = head_row
+    u_ref[...] = dot(jnp.broadcast_to(head_row, (8, C)).astype(BF16), reduce_ref[...])
+
+
+def setup(w_qkv, window_bias, patterns, attn_gain, mlp_gain, temp_head, reduce_t):
     return pl.pallas_call(
         setup_kernel,
         out_shape=(
             jax.ShapeDtypeStruct((3 * C, C), BF16),
-            jax.ShapeDtypeStruct((3, C, 256), BF16),
             jax.ShapeDtypeStruct((WIN, WIDE), F32),
             jax.ShapeDtypeStruct((8, WIDE), F32),
             jax.ShapeDtypeStruct((WIN, 128), F32),
             jax.ShapeDtypeStruct((8, 256), F32),
+            jax.ShapeDtypeStruct((8, FF), F32),
         ),
-        in_specs=[vmem()] * 6,
+        in_specs=[vmem()] * 7,
         out_specs=(vmem(),) * 6,
-        compiler_params=pltpu.CompilerParams(vmem_limit_bytes=VMEM_ALL),
+        compiler_params=pltpu.CompilerParams(vmem_limit_bytes=SMALL_VMEM),
         cost_estimate=pl.CostEstimate(
             flops=1_000_000_000, bytes_accessed=3_000_000, transcendentals=0
         ),
         name="setup",
-    )(w_qkv, window_bias, patterns, attn_gain[None], mlp_gain[None], temp_head[None])
+    )(w_qkv, window_bias, patterns, attn_gain[None], mlp_gain[None], temp_head[None], reduce_t)
 
 
 LOG2E = 1.4426950408889634
@@ -486,17 +486,10 @@
 
 
 def main_kernel(
-    x_ref, *refs
+    x_ref, order_ref, back_ref, wt_ref, bias_ref, pat_q_ref, pat_k_ref, gains_ref, u_ref,
+    proj_ref, expand_ref,
+    out_ref, tok_in, levels_ref, packed, sems, *scratch,
 ):
-    given, out_ref, held = refs[:N_CONST], refs[N_CONST], refs[N_CONST + 1 : 2 * N_CONST + 1]
-    tok_in, levels_ref, sems, *scratch = refs[2 * N_CONST + 1 :]
-    copies = [
-        pltpu.make_async_copy(a, b, sems.at[k]) for k, (a, b) in enumerate(zip(given, held))
-    ]
-    for copy in copies:
-        copy.start()
-    (order_ref, back_ref, wt_ref, w_ref, bias_ref, pat_q_ref, pat_k_ref, gains_ref, proj_ref,
-     expand_ref, reduce_ref) = held
     columns = (scratch[: len(PER_COLUMN)], scratch[len(PER_COLUMN) :])
     scale_q = 1.0 / HEAD**0.5
     lane72 = lanes((HALF, 128))
@@ -525,7 +518,6 @@
         jnp.where((pick_row >= 64) & (pick_row < 67), 1.0, 0.0),
         jnp.where((pick_row >= 67) & (pick_row < 70), 1.0, 0.0),
     ).astype(BF16)
-    copies[0].wait()
     for p in range(4):
         for a in range(2):
             pieces = []
@@ -539,13 +531,10 @@
                 columns[col][0][p, rows, :] = moved[HALF * col : HALF * col + HALF]
                 columns[col][13][p, rows, :] = fields[HALF * col : HALF * col + HALF]
 
-    for copy in copies[1:]:
-        copy.wait()
     gain_one = gains_ref[0:1, 0:C]
     gain_two = gains_ref[1:2, 0:C]
     head_row = gains_ref[2:3, 0:C]
-    head_eight = jnp.broadcast_to(head_row, (8, C)).astype(BF16)
-    u_row = dot(head_eight, reduce_ref[...])[0:1]
+    u_row = u_ref[0:1, :]
 
     def forward(p, col):
         (tok, diag_q, diag_n, probs, dscores, q_rows, n_rows, dq_rows, resid, hats, scales,
@@ -575,14 +564,14 @@
         keys_t = turned[C : 2 * C].astype(BF16)
         values_t = turned[2 * C : 3 * C].astype(BF16)
         yield
-        q_rows[p] = (dot(normed, w_ref[0])[:, 0:C] * scale_q).astype(BF16)
-        keys = dot(normed, w_ref[1])
-        marks = jnp.where(lanes((WIN, 128)).astype(F32) == label_k + 64.0, 1.0, keys[:, 128:256])
-        keys = jnp.concatenate([keys[:, 0:128], marks], axis=1)[:, 0:208].astype(BF16)
-        values = dot(normed, w_ref[2])
-        lane_wide = lanes((1, 256))
-        ones = jnp.where((lane_wide == C) | (lane_wide == C + 1), 1.0, 0.0)
-        values = (values + ones)[:, 0:208].astype(BF16)
+        q_rows[p] = (dot_nt(normed, wt_ref[0:C, :]) * scale_q).astype(BF16)
+        keys = dot_nt(normed, wt_ref[C : 2 * C, :])
+        lane16w = lanes((WIN, 16))
+        marks = jnp.where(lane16w.astype(F32) == label_k, 1.0, 0.0)
+        keys = jnp.concatenate([keys, marks], axis=1).astype(BF16)
+        values = dot_nt(normed, wt_ref[2 * C : 3 * C, :])
+        ones = jnp.where(lane16w < 2, 1.0, 0.0)
+        values = jnp.concatenate([values, ones], axis=1).astype(BF16)
         yield
         scores = dot(keys, diag_q[...]) + bias_ref[...]
         yield
@@ -714,26 +703,26 @@
                 tok_in[s, at : at + HALF, :] = moved[HALF * beta : HALF * beta + HALF]
     zero = jnp.zeros((16, 128), F32)
     for s in range(GROUP):
-        pack_block(out_ref, s, tok_in[s], zero)
-
-
-N_CONST = 11
+        pack_block(packed, s, tok_in[s], zero)
+        pltpu.make_async_copy(packed.at[s], out_ref.at[s], sems.at[s]).start()
+    for s in range(GROUP):
+        pltpu.make_async_copy(packed.at[s], out_ref.at[s], sems.at[s]).wait()
 
 
 def layer(x, consts):
     return pl.pallas_call(
         main_kernel,
         out_shape=jax.ShapeDtypeStruct((GROUP, ROWS, 128), BF16),
-        in_specs=[vmem()] + [pl.BlockSpec(memory_space=pltpu.HBM)] * N_CONST,
-        out_specs=vmem(),
-        scratch_shapes=[pltpu.VMEM(c.shape, c.dtype) for c in consts]
-        + [
+        in_specs=[vmem()] * (1 + len(consts)),
+        out_specs=pl.BlockSpec(memory_space=pl.ANY),
+        scratch_shapes=[
             pltpu.VMEM((GROUP, WIN, 256), F32),
             pltpu.VMEM((4, 16, 128), F32),
-            pltpu.SemaphoreType.DMA((N_CONST,)),
+            pltpu.VMEM((GROUP, ROWS, 128), BF16),
+            pltpu.SemaphoreType.DMA((GROUP,)),
         ]
         + [pltpu.VMEM(shape, kind) for shape, kind in PER_COLUMN] * 2,
-        compiler_params=pltpu.CompilerParams(vmem_limit_bytes=VMEM_ALL),
+        compiler_params=pltpu.CompilerParams(vmem_limit_bytes=VMEM_LIMIT),
         cost_estimate=pl.CostEstimate(
             flops=20_000_000_000, bytes_accessed=4_000_000, transcendentals=3_000_000
         ),
@@ -792,9 +781,9 @@
         )
         for half in halves
     ]
-    weights = (w_qkv, window_bias, patterns, attn_gain, mlp_gain, temp_head)
+    weights = (w_qkv, window_bias, patterns, attn_gain, mlp_gain, temp_head, w_reduce.T)
     weights, made[0] = lax.optimization_barrier((weights, made[0]))
-    consts = (order, order_back) + tuple(setup(*weights)) + (w_proj, w_expand, w_reduce.T)
+    consts = (order, order_back) + tuple(setup(*weights)) + (w_proj, w_expand)
     done = None
     for odd in range(2):
         got = exchange(made[odd], odd)

time: 100 us -> 96.3 us (0.963)
  Pallas kernels: 51.1 us -> 44.9 us
  waiting for transfers between devices: 12.6 us -> 13.8 us
  local copies, waits for them, and re-layouts: 0.6 us -> 1.6 us
    pallas_call x2, Pallas kernels: 38.2 us -> 34.5 us  [layer(): pl.pallas_call(main_kernel, out_shape=jax.ShapeDtypeStruct((GROUP, ROWS,...]
    pallas_call x1, Pallas kernels: 2.74 us -> 0.74 us  [setup(): pl.pallas_call(setup_kernel, out_shape=(jax.ShapeDtypeStruct((3 * C, C),...]
    unnamed x24 -> x46, local copies, waits for them, and re-layouts: 0.05 us -> 1.59 us
    all_to_all x4, waiting for transfers between devices: 10.9 us -> 12.1 us  [exchange(): lax.all_to_all(blocks, ('tile', 'lev'), 0, 0, axis_index_groups=pair_grou...]
  transfers between devices with their start and end apart: 6 -> 6, of which waited for: 3 -> 3; matrix products, arithmetic and copies ran while one was open for 1% -> 0% of each run, Pallas kernels for 45% -> 41%
where the time goes in v4:
time: 96.3 us; the launch traced here: 95.7 us
  Pallas kernels  44.9 us (47%)
  starting transfers between devices  34.2 us (36%)
  waiting for transfers between devices  13.8 us (14%)
  local copies, waits for them, and re-layouts  1.6 us (2%)
  between operations  1.13 us (1%)
    pallas_call x2, Pallas kernels, layer(): pl.pallas_call(main_kernel, out_shape=jax.ShapeDtypeStruct((GROUP, ROWS,...  34.5 us
    all_to_all x4, starting transfers between devices, exchange(): lax.all_to_all(blocks, ('tile', 'lev'), 0, 0, axis_index_groups=pair_grou...  30.9 us
    all_to_all x4, waiting for transfers between devices, exchange(): lax.all_to_all(blocks, ('tile', 'lev'), 0, 0, axis_index_groups=pair_grou...  12.1 us
    pallas_call x2, Pallas kernels, prep(): pl.pallas_call(prep_kernel, out_shape=jax.ShapeDtypeStruct((GROUP, ROWS,...  4.7 us
    ppermute x2, starting transfers between devices, block_step(): return lax.ppermute(value, 'tile', pairs)  3.24 us
    pallas_call x2, Pallas kernels, post(): pl.pallas_call(post_kernel, out_shape=(jax.ShapeDtypeStruct((2, 12, 1, LO...  2.92 us
    pallas_call x1, Pallas kernels, rim(): pl.pallas_call(rim_kernel, out_shape=(edge, edge), grid=(1,), in_specs=[s...  2.08 us
  transfers between devices with their start and end apart: 6, of which 3 were waited for; matrix products, arithmetic and copies ran while one was open for 0% of the time, Pallas kernels for 41%

profile of v4, /device:TPU:1, one launch (start us, length us, event | category | flops | bytes accessed | tf_op | source)
XLA Modules:
  0.0 95.7 jit_solution(3159227293890445023)
XLA Ops:
  0.7 0.0 copy-start.16
  0.7 2.1 %rim.1 = (bf16[96,256]{1,0:T(8,128)(2,1)}, bf16[96,256]{1,0:T(8,128)(2,1)}) custom-call(s32[4,15]{1,0:T(4,128)} %ids_ref.5, bf16[12,90,2,192]{3,2,1,0:T(2,128)(2,1)} %bitcast.14, bf16[12,90,2,192]{3,2,1,0:T(2,128)(2,1)} %bitcast.15, f32[2,12,1,90]{3,2,1,0:T(1,128)} %bitcast.18, f32[12,1,90]{2,1,0:T(1,128)} %bitcast.21), custom_call_target="tpu_custom_call" | custom-call | tf_op jit(solution)/shard_map/rim/pallas_call | solution.py:175
  2.8 3.2 %collective-permute-start = (bf16[96,256]{1,0:T(8,128)(2,1)}, bf16[96,256]{1,0:T(8,128)(2,1)S(1)}, u32[]{:S(2)}, u32[]{:S(2)}) collective-permute-start(bf16[96,256]{1,0:T(8,128)(2,1)} %get-tuple-element.22), channel_id=1, source_target_pairs={{0,12},{4,0},{8,4},{12,8},{16,28},{20,16},{24,20},{28,24},{32,44},... | collective-permute-start | bytes 147464 | tf_op jit(solution)/shard_map/ppermute | solution.py:754
  6.0 0.0 collective-permute-start.1
  6.0 1.8 %collective-permute-done.next_ref = bf16[96,256]{1,0:T(8,128)(2,1)S(1)} collective-permute-done((bf16[96,256]{1,0:T(8,128)(2,1)}, bf16[96,256]{1,0:T(8,128)(2,1)S(1)}, u32[]{:S(2)}, u32[]{:S(2)}) %collective-permute-start) | collective-permute-done | bytes 49184 | tf_op jit(solution)/shard_map/ppermute | solution.py:754
  7.8 0.0 collective-permute-done.1.prev_ref
  7.8 0.0 copy-done.1
  7.9 0.0 copy-start.22
  7.9 0.0 copy-start.4
  7.9 0.0 copy-start.5
  7.9 0.0 copy-start.7
  7.9 0.0 copy-start.9
  7.9 0.0 copy-start.10
  7.9 0.0 copy-start.11
  8.0 2.3 %prep.3 = bf16[8,240,128]{2,1,0:T(8,128)(2,1)} custom-call(s32[1]{0:T(128)} %bitcast.7.half_ref, s32[4,15]{1,0:T(4,128)S(1)} %copy-done.3, f32[2]{0:T(128)S(1)} %copy-done.12, f32[2]{0:T(128)S(1)} %copy-done.13, f32[2]{0:T(128)S(1)} %copy-done.14, bf16[12,90,2,192]{3,2,1,0:T(2,128)(2,1)S(1)} %bitcast.16, bf16[96,256]{1,0:T(8,128)(2,1)S(1)} %collective-permute-done.next_ref, ...), custom_call_target="tpu_custom_call" | custom-call | flops 1000000000 | bytes 2500000 | tf_op jit(solution)/shard_map/prep/pallas_call | solution.py:258
  10.3 12.4 %all-to-all-start.2 = ((bf16[8,240,128]{2,1,0:T(8,128)(2,1)}), bf16[8,240,128]{2,1,0:T(8,128)(2,1)S(1)}, u32[]{:S(2)}, u32[]{:S(2)}) async-start(bf16[8,240,128]{2,1,0:T(8,128)(2,1)} %prep.3), calls=%async_computation.2 | async-start | bytes 983040 | tf_op jit(solution)/shard_map/all_to_all | solution.py:745
  22.8 0.7 setup.1
  23.5 0.0 copy-start.18
  23.5 0.8 copy-done.18
  24.3 0.7 copy-done.20
  25.1 2.4 %prep.2 = bf16[8,240,128]{2,1,0:T(8,128)(2,1)} custom-call(s32[1]{0:T(128)} %bitcast.half_ref, s32[4,15]{1,0:T(4,128)S(1)} %copy-done.3, f32[2]{0:T(128)S(1)} %copy-done.12, f32[2]{0:T(128)S(1)} %copy-done.13, f32[2]{0:T(128)S(1)} %copy-done.14, bf16[12,90,2,192]{3,2,1,0:T(2,128)(2,1)S(1)} %bitcast.17, bf16[96,256]{1,0:T(8,128)(2,1)S(1)} %collective-permute-done.next_ref, ...), custom_call_target="tpu_custom_call" | custom-call | flops 1000000000 | bytes 2500000 | tf_op jit(solution)/shard_map/prep/pallas_call | solution.py:258
  27.4 2.8 %all-to-all-done.2.x_ref = bf16[8,240,128]{2,1,0:T(8,128)(2,1)S(1)} async-done(((bf16[8,240,128]{2,1,0:T(8,128)(2,1)}), bf16[8,240,128]{2,1,0:T(8,128)(2,1)S(1)}, u32[]{:S(2)}, u32[]{:S(2)}) %all-to-all-start.2) | async-done | bytes 491552 | tf_op jit(solution)/shard_map/all_to_all | solution.py:745
  30.2 4.9 %all-to-all-start = ((bf16[8,240,128]{2,1,0:T(8,128)(2,1)}), bf16[8,240,128]{2,1,0:T(8,128)(2,1)S(1)}, u32[]{:S(2)}, u32[]{:S(2)}) async-start(bf16[8,240,128]{2,1,0:T(8,128)(2,1)} %prep.2), calls=%async_computation | async-start | bytes 983040 | tf_op jit(solution)/shard_map/all_to_all | solution.py:745
  35.1 17.2 %layer.3 = bf16[8,240,128]{2,1,0:T(8,128)(2,1)} custom-call(bf16[8,240,128]{2,1,0:T(8,128)(2,1)S(1)} %all-to-all-done.2.x_ref, bf16[144,144]{1,0:T(8,128)(2,1)S(1)} %copy-done.17, bf16[144,144]{1,0:T(8,128)(2,1)S(1)} %copy-done.17, bf16[576,192]{1,0:T(8,128)(2,1)S(1)} %copy-done.21, f32[144,896]{1,0:T(8,128)S(1)} %copy-done.19, ...), custom_call_target="tpu_custom_call" | custom-call | flops 20000000000 | bytes 4000000 | tf_op jit(solution)/shard_map/layer/pallas_call | solution.py:713
  52.4 0.0 all-to-all-done.x_ref
  52.4 9.6 %all-to-all-start.3 = ((bf16[8,240,128]{2,1,0:T(8,128)(2,1)}), bf16[8,240,128]{2,1,0:T(8,128)(2,1)S(1)}, u32[]{:S(2)}, u32[]{:S(2)}) async-start(bf16[8,240,128]{2,1,0:T(8,128)(2,1)} %layer.3), calls=%async_computation.3 | async-start | bytes 983040 | tf_op jit(solution)/shard_map/all_to_all | solution.py:745
  62.0 17.2 %layer.2 = bf16[8,240,128]{2,1,0:T(8,128)(2,1)} custom-call(bf16[8,240,128]{2,1,0:T(8,128)(2,1)S(1)} %all-to-all-done.x_ref, bf16[144,144]{1,0:T(8,128)(2,1)S(1)} %copy-done.17, bf16[144,144]{1,0:T(8,128)(2,1)S(1)} %copy-done.17, bf16[576,192]{1,0:T(8,128)(2,1)S(1)} %copy-done.21, f32[144,896]{1,0:T(8,128)S(1)} %copy-done.19, ...), custom_call_target="tpu_custom_call" | custom-call | flops 20000000000 | bytes 4000000 | tf_op jit(solution)/shard_map/layer/pallas_call | solution.py:713
  79.3 0.0 all-to-all-done.3.x_ref
  79.3 4.0 %all-to-all-start.1 = ((bf16[8,240,128]{2,1,0:T(8,128)(2,1)}), bf16[8,240,128]{2,1,0:T(8,128)(2,1)S(1)}, u32[]{:S(2)}, u32[]{:S(2)}) async-start(bf16[8,240,128]{2,1,0:T(8,128)(2,1)} %layer.2), calls=%async_computation.1 | async-start | bytes 983040 | tf_op jit(solution)/shard_map/all_to_all | solution.py:745
  83.3 1.5 %post.2 = (f32[2,12,1,90]{3,2,1,0:T(1,128)}, bf16[12,90,2,192]{3,2,1,0:T(2,128)(2,1)}) custom-call(s32[1]{0:T(128)} %bitcast.7.half_ref, bf16[8,240,128]{2,1,0:T(8,128)(2,1)S(1)} %all-to-all-done.3.x_ref, bf16[288,432]{1,0:T(8,128)(2,1)S(1)} %copy-done.15), custom_call_target="tpu_custom_call" | custom-call | flops 1000000000 | bytes 2500000 | tf_op jit(solution)/shard_map/post/pallas_call | solution.py:316
  84.8 9.3 %all-to-all-done.1.x_ref = bf16[8,240,128]{2,1,0:T(8,128)(2,1)S(1)} async-done(((bf16[8,240,128]{2,1,0:T(8,128)(2,1)}), bf16[8,240,128]{2,1,0:T(8,128)(2,1)S(1)}, u32[]{:S(2)}, u32[]{:S(2)}) %all-to-all-start.1) | async-done | bytes 491552 | tf_op jit(solution)/shard_map/all_to_all | solution.py:745
  94.0 1.5 %post.3 = (f32[2,12,1,90]{3,2,1,0:T(1,128)}, bf16[12,90,2,192]{3,2,1,0:T(2,128)(2,1)}) custom-call(s32[1]{0:T(128)} %bitcast.half_ref, bf16[8,240,128]{2,1,0:T(8,128)(2,1)S(1)} %all-to-all-done.1.x_ref, bf16[288,432]{1,0:T(8,128)(2,1)S(1)} %copy-done.15, f32[2,12,1,90]{3,2,1,0:T(1,128)} %get-tuple-element.38.refs_0_, ...), custom_call_target="tpu_custom_call", output_to_operand_aliasing={{0}: (3, {}), {1}: (4, {})} | custom-call | flops 1000000000 | bytes 2500000 | tf_op jit(solution)/shard_map/post/pallas_call | solution.py:316
  (35 shorter events, 0.1 us)
Async XLA Ops:
  0.6 7.2 %copy-start = (bf16[2,1,12,90,192]{4,0,3,2,1:T(2,128)(2,1)S(1)}, bf16[2,1,12,90,192]{4,0,3,2,1:T(2,128)(2,1)}, u32[]{:S(2)}) copy-start(bf16[2,1,12,90,192]{4,0,3,2,1:T(2,128)(2,1)} %param.20) | copy-start | bytes 2488324
  0.6 7.2 %copy-start.1 = (f32[2,1,12,90]{3,1,2,0:T(1,128)S(1)}, f32[2,1,12,90]{3,1,2,0:T(1,128)}, u32[]{:S(2)}) copy-start(f32[2,1,12,90]{3,1,2,0:T(1,128)} %param.35) | copy-start | bytes 25924
  0.7 7.2 %copy-start.2 = (f32[1,12,90]{2,0,1:T(1,128)S(1)}, f32[1,12,90]{2,0,1:T(1,128)}, u32[]{:S(2)}) copy-start(f32[1,12,90]{2,0,1:T(1,128)} %param.34) | copy-start | bytes 12964
  0.7 7.2 %copy-start.3 = (s32[4,15]{1,0:T(4,128)S(1)}, s32[4,15]{1,0:T(4,128)}, u32[]{:S(2)}) copy-start(s32[4,15]{1,0:T(4,128)} %ids_ref.5) | copy-start | bytes 724
  0.7 7.2 %copy-start.12 = (f32[2]{0:T(128)S(1)}, f32[2]{0:T(128)}, u32[]{:S(2)}) copy-start(f32[2]{0:T(128)} %thick_ref.3) | copy-start | bytes 28
  0.7 7.2 %copy-start.13 = (f32[2]{0:T(128)S(1)}, f32[2]{0:T(128)}, u32[]{:S(2)}) copy-start(f32[2]{0:T(128)} %weight_ref.3) | copy-start | bytes 28
  0.7 7.2 %copy-start.14 = (f32[2]{0:T(128)S(1)}, f32[2]{0:T(128)}, u32[]{:S(2)}) copy-start(f32[2]{0:T(128)} %base_ref.3) | copy-start | bytes 28
  0.7 7.2 %copy-start.16 = (bf16[288,384]{1,0:T(8,128)(2,1)S(1)}, bf16[288,384]{1,0:T(8,128)(2,1)}, u32[]{:S(2)}) copy-start(bf16[288,384]{1,0:T(8,128)(2,1)} %constant.48.clone.perm_ref) | copy-start | bytes 663556
  2.8 5.0 %collective-permute-start = (bf16[96,256]{1,0:T(8,128)(2,1)}, bf16[96,256]{1,0:T(8,128)(2,1)S(1)}, u32[]{:S(2)}, u32[]{:S(2)}) collective-permute-start(bf16[96,256]{1,0:T(8,128)(2,1)} %get-tuple-element.22), channel_id=1, source_target_pairs={{0,12},{4,0},{8,4},{12,8},{16,28},{20,16},{24,20},{28,24},{32,44},... | collective-permute-start | bytes 147464 | tf_op jit(solution)/shard_map/ppermute | solution.py:754
  6.0 1.8 %collective-permute-start.1 = (bf16[96,256]{1,0:T(8,128)(2,1)}, bf16[96,256]{1,0:T(8,128)(2,1)S(1)}, u32[]{:S(2)}, u32[]{:S(2)}) collective-permute-start(bf16[96,256]{1,0:T(8,128)(2,1)} %get-tuple-element.23), channel_id=1, source_target_pairs={{0,4},{4,8},{8,12},{12,0},{16,20},{20,24},{24,28},{28,16},{32,36},... | collective-permute-start | bytes 147464 | tf_op jit(solution)/shard_map/ppermute | solution.py:754
  7.9 14.8 %copy-start.22 = (bf16[192]{0:T(256)(128)(2,1)S(1)}, bf16[192]{0:T(256)(128)(2,1)}, u32[]{:S(2)}) copy-start(bf16[192]{0:T(256)(128)(2,1)} %param.30) | copy-start | bytes 1156
  7.9 14.8 %copy-start.4 = (f32[6,144,144]{2,1,0:T(8,128)S(1)}, f32[6,144,144]{2,1,0:T(8,128)}, u32[]{:S(2)}) copy-start(f32[6,144,144]{2,1,0:T(8,128)} %bias_ref) | copy-start | bytes 1492996
  7.9 14.8 %copy-start.5 = (bf16[768,192]{0,1:T(8,128)(2,1)S(1)}, bf16[768,192]{0,1:T(8,128)(2,1)}, u32[]{:S(2)}) copy-start(bf16[768,192]{0,1:T(8,128)(2,1)} %param.29) | copy-start | bytes 884740
  7.9 14.8 %copy-start.7 = (bf16[192,576]{1,0:T(8,128)(2,1)S(1)}, bf16[192,576]{1,0:T(8,128)(2,1)}, u32[]{:S(2)}) copy-start(bf16[192,576]{1,0:T(8,128)(2,1)} %w_ref) | copy-start | bytes 663556
  7.9 14.8 %copy-start.9 = (s32[8,144]{1,0:T(8,128)S(1)}, s32[8,144]{1,0:T(8,128)}, u32[]{:S(2)}) copy-start(s32[8,144]{1,0:T(8,128)} %pat_ref) | copy-start | bytes 13828
  7.9 14.8 %copy-start.10 = (f32[192]{0:T(256)S(1)}, f32[192]{0:T(256)}, u32[]{:S(2)}) copy-start(f32[192]{0:T(256)} %param.21) | copy-start | bytes 2308
  7.9 14.8 %copy-start.11 = (f32[192]{0:T(256)S(1)}, f32[192]{0:T(256)}, u32[]{:S(2)}) copy-start(f32[192]{0:T(256)} %param.27) | copy-start | bytes 2308
  10.3 19.9 %all-to-all-start.2 = ((bf16[8,240,128]{2,1,0:T(8,128)(2,1)}), bf16[8,240,128]{2,1,0:T(8,128)(2,1)S(1)}, u32[]{:S(2)}, u32[]{:S(2)}) async-start(bf16[8,240,128]{2,1,0:T(8,128)(2,1)} %prep.3), calls=%async_computation.2 | async-start | bytes 983040 | tf_op jit(solution)/shard_map/all_to_all | solution.py:745
  23.5 0.8 copy-start.18
  24.3 0.7 copy-start.20
  25.0 10.1 %copy-start.6 = (bf16[192,768]{1,0:T(8,128)(2,1)S(1)}, bf16[192,768]{1,0:T(8,128)(2,1)}, u32[]{:S(2)}) copy-start(bf16[192,768]{1,0:T(8,128)(2,1)} %expand_ref.3) | copy-start | bytes 884740
  25.0 10.1 %copy-start.8 = (bf16[192,192]{1,0:T(8,128)(2,1)S(1)}, bf16[192,192]{1,0:T(8,128)(2,1)}, u32[]{:S(2)}) copy-start(bf16[192,192]{1,0:T(8,128)(2,1)} %proj_ref.3) | copy-start | bytes 221188
  25.0 10.1 %copy-start.17 = (bf16[144,144]{1,0:T(8,128)(2,1)S(1)}, bf16[144,144]{1,0:T(8,128)(2,1)}, u32[]{:S(2)}) copy-start(bf16[144,144]{1,0:T(8,128)(2,1)} %constant.50.clone.order_ref.back_ref) | copy-start | bytes 124420
  25.0 10.1 %copy-start.19 = (f32[144,896]{1,0:T(8,128)S(1)}, f32[144,896]{1,0:T(8,128)}, u32[]{:S(2)}) copy-start(f32[144,896]{1,0:T(8,128)} %copy-done.18) | copy-start | bytes 1548292
  25.0 10.1 %copy-start.21 = (bf16[576,192]{1,0:T(8,128)(2,1)S(1)}, bf16[576,192]{1,0:T(8,128)(2,1)}, u32[]{:S(2)}) copy-start(bf16[576,192]{1,0:T(8,128)(2,1)} %copy-done.20) | copy-start | bytes 663556
  30.2 22.2 %all-to-all-start = ((bf16[8,240,128]{2,1,0:T(8,128)(2,1)}), bf16[8,240,128]{2,1,0:T(8,128)(2,1)S(1)}, u32[]{:S(2)}, u32[]{:S(2)}) async-start(bf16[8,240,128]{2,1,0:T(8,128)(2,1)} %prep.2), calls=%async_computation | async-start | bytes 983040 | tf_op jit(solution)/shard_map/all_to_all | solution.py:745
  52.4 26.9 %all-to-all-start.3 = ((bf16[8,240,128]{2,1,0:T(8,128)(2,1)}), bf16[8,240,128]{2,1,0:T(8,128)(2,1)S(1)}, u32[]{:S(2)}, u32[]{:S(2)}) async-start(bf16[8,240,128]{2,1,0:T(8,128)(2,1)} %layer.3), calls=%async_computation.3 | async-start | bytes 983040 | tf_op jit(solution)/shard_map/all_to_all | solution.py:745
  62.0 21.3 %copy-start.15 = (bf16[288,432]{1,0:T(8,128)(2,1)S(1)}, bf16[288,432]{1,0:T(8,128)(2,1)}, u32[]{:S(2)}) copy-start(bf16[288,432]{1,0:T(8,128)(2,1)} %constant.49.clone.perm_ref) | copy-start | bytes 746500
  79.3 14.7 %all-to-all-start.1 = ((bf16[8,240,128]{2,1,0:T(8,128)(2,1)}), bf16[8,240,128]{2,1,0:T(8,128)(2,1)S(1)}, u32[]{:S(2)}, u32[]{:S(2)}) async-start(bf16[8,240,128]{2,1,0:T(8,128)(2,1)} %layer.2), calls=%async_computation.1 | async-start | bytes 983040 | tf_op jit(solution)/shard_map/all_to_all | solution.py:745

commit v5 on v4

--- a/solution.py
+++ b/solution.py
@@ -192,12 +192,7 @@
     )(ids, feats, feats, target, surface)
 
 
-def prep_kernel(
-    half_ref, ids_ref, thick_ref, weight_ref, base_ref,
-    f_ref, next_ref, prev_ref, target_ref, surface_ref, perm_ref,
-    out_ref, rows_ref, packed, sems,
-):
-    upper = half_ref[0] == 1
+def fill_rows(half_ref, f_ref, target_ref, surface_ref, rows_ref, after, before):
     start = 6 * half_ref[0]
     targets = [
         jnp.concatenate([target_ref[lev, start + r] for r in range(6)], axis=0)
@@ -205,10 +200,6 @@
     ]
     ground = jnp.concatenate([surface_ref[start + r] for r in range(6)], axis=0)
     values = dot_nt(lon_pick(2 * LONS, 0), field_rows(targets, ground, 6, 8))
-    after, before = (
-        jnp.where(upper, ref[48:96].astype(F32), ref[0:48].astype(F32))
-        for ref in (next_ref, prev_ref)
-    )
     lane = lanes((2 * LONS, 128))
     for r in range(6):
         tokens = f_ref[start + r].reshape(2 * LONS, C).astype(F32)
@@ -218,26 +209,35 @@
         for at, part in ((0, tokens[:, 0:128]), (128, second)):
             cut = slice(at, at + 128)
             rows_ref[208 * r : 208 * r + 176, cut] = part[0:176].astype(BF16)
-            tail = [
-                part[176:180],
-                after[8 * r : 8 * r + 6, cut],
-                before[8 * r + 2 : 8 * r + 8, cut],
-                part[0:6],
-                jnp.zeros((10, 128), F32),
-            ]
+            if after is None:
+                rim_part = [jnp.zeros((12, 128), F32)]
+            else:
+                rim_part = [after[8 * r : 8 * r + 6, cut], before[8 * r + 2 : 8 * r + 8, cut]]
+            tail = [part[176:180]] + rim_part + [part[0:6], jnp.zeros((10, 128), F32)]
             tail = jnp.concatenate(tail, axis=0).astype(BF16)
             rows_ref[208 * r + 176 : 208 * r + 208, cut] = tail
+
+
+def rims(half_ref, next_ref, prev_ref):
+    upper = half_ref[0] == 1
+    return [
+        jnp.where(upper, ref[48:96].astype(F32), ref[0:48].astype(F32))
+        for ref in (next_ref, prev_ref)
+    ]
+
+
+def send_blocks(pairs, ids_ref, level_refs, source, before, perm_ref, packed, out_ref, sems):
     lane16 = lanes((16, 128))
     row16 = lax.broadcasted_iota(jnp.int32, (16, 128), 0)
     scalars = jnp.zeros((16, 128), F32)
     for lev in range(2):
-        for k, ref in enumerate((thick_ref, weight_ref, base_ref)):
+        for k, ref in enumerate(level_refs):
             scalars = jnp.where((row16 == lev) & (lane16 == 72 + k), ref[lev], scalars)
     top, middle, low = split3(scalars)
     scalars = top + roll(middle, 3) + roll(low, 6)
-    for m in range(4):
-        source = [rows_ref[208 * r + 48 * m : 208 * r + 48 * m + 64, :] for r in range(6)]
-        made = dot(perm_ref[...], jnp.concatenate(source, axis=0))
+    copies = []
+    for m in pairs:
+        made = dot(perm_ref[...], jnp.concatenate([source(r, m) for r in range(6)], axis=0))
         for q in range(2):
             d = 2 * m + q
             spare = scalars
@@ -248,29 +248,104 @@
                     else:
                         ident = before[0:1, 200 + p : 201 + p]
                     spare = jnp.where((row16 == 2 + p) & (lane16 == 81 + col), ident, spare)
-            pack_block(packed, d, made[WIN * q : WIN * q + WIN], spare)
-            pltpu.make_async_copy(packed.at[d], out_ref.at[d], sems.at[d]).start()
-    for d in range(GROUP):
-        pltpu.make_async_copy(packed.at[d], out_ref.at[d], sems.at[d]).wait()
-
-
-def prep(half, ids, thick, weight, base, feats, after, before, target, surface, perm):
+            at = d - 2 * pairs[0]
+            pack_block(packed, at, made[WIN * q : WIN * q + WIN], spare)
+            copies.append(pltpu.make_async_copy(packed.at[at], out_ref.at[d], sems.at[at]))
+            copies[-1].start()
+    for copy in copies:
+        copy.wait()
+
+
+def prep_kernel(
+    half_ref, ids_ref, thick_ref, weight_ref, base_ref,
+    f_ref, next_ref, prev_ref, target_ref, surface_ref, perm_ref,
+    out_ref, rows_ref, packed, sems,
+):
+    after, before = rims(half_ref, next_ref, prev_ref)
+    fill_rows(half_ref, f_ref, target_ref, surface_ref, rows_ref, after, before)
+    send_blocks(
+        range(4), ids_ref, (thick_ref, weight_ref, base_ref),
+        lambda r, m: rows_ref[208 * r + 48 * m : 208 * r + 48 * m + 64, :],
+        before, perm_ref, packed, out_ref, sems,
+    )
+
+
+def inner_kernel(
+    half_ref, ids_ref, thick_ref, weight_ref, base_ref,
+    f_ref, target_ref, surface_ref, perm_ref,
+    out_ref, rows_ref, packed, sems,
+):
+    fill_rows(half_ref, f_ref, target_ref, surface_ref, rows_ref, None, None)
+    send_blocks(
+        range(3), ids_ref, (thick_ref, weight_ref, base_ref),
+        lambda r, m: rows_ref[208 * r + 48 * m : 208 * r + 48 * m + 64, :],
+        None, perm_ref, packed, out_ref, sems,
+    )
+
+
+def outer_kernel(
+    half_ref, ids_ref, thick_ref, weight_ref, base_ref,
+    next_ref, prev_ref, rows_ref, perm_ref, _,
+    out_ref, packed, sems,
+):
+    after, before = rims(half_ref, next_ref, prev_ref)
+
+    def source(r, m):
+        own = rows_ref[208 * r + 176 : 208 * r + 208, :].astype(F32)
+        more = [
+            jnp.zeros((4, 256), F32), after[8 * r : 8 * r + 6], before[8 * r + 2 : 8 * r + 8],
+            jnp.zeros((16, 256), F32),
+        ]
+        tail = (own + jnp.concatenate(more, axis=0)).astype(BF16)
+        return jnp.concatenate([rows_ref[208 * r + 144 : 208 * r + 176, :], tail], axis=0)
+
+    send_blocks(
+        range(3, 4), ids_ref, (thick_ref, weight_ref, base_ref),
+        source, before, perm_ref, packed, out_ref, sems,
+    )
+
+
+def prep_call(kernel, name, count, outs, out_specs, scratch, aliases, args):
     return pl.pallas_call(
-        prep_kernel,
-        out_shape=jax.ShapeDtypeStruct((GROUP, ROWS, 128), BF16),
-        in_specs=[smem()] * 5 + [vmem()] * 6,
-        out_specs=pl.BlockSpec(memory_space=pl.ANY),
-        scratch_shapes=[
-            pltpu.VMEM((6 * 208, 256), BF16),
-            pltpu.VMEM((GROUP, ROWS, 128), BF16),
-            pltpu.SemaphoreType.DMA((GROUP,)),
-        ],
+        kernel,
+        out_shape=outs,
+        in_specs=[smem()] * 5
+        + [vmem()] * (len(args) - 5 - len(aliases))
+        + [pl.BlockSpec(memory_space=pl.ANY)] * len(aliases),
+        out_specs=out_specs,
+        scratch_shapes=scratch
+        + [pltpu.VMEM((count, ROWS, 128), BF16), pltpu.SemaphoreType.DMA((count,))],
+        input_output_aliases=aliases,
         compiler_params=pltpu.CompilerParams(vmem_limit_bytes=SMALL_VMEM),
         cost_estimate=pl.CostEstimate(
             flops=1_000_000_000, bytes_accessed=2_500_000, transcendentals=0
         ),
-        name="prep",
-    )(half, ids, thick, weight, base, feats, after, before, target, surface, perm)
+        name=name,
+    )(*args)
+
+
+BLOCKS_OUT = jax.ShapeDtypeStruct((GROUP, ROWS, 128), BF16)
+
+
+def prep(half, ids, thick, weight, base, feats, after, before, target, surface, perm):
+    return prep_call(
+        prep_kernel, "prep", GROUP, BLOCKS_OUT, pl.BlockSpec(memory_space=pl.ANY),
+        [pltpu.VMEM((6 * 208, 256), BF16)], {},
+        (half, ids, thick, weight, base, feats, after, before, target, surface, perm),
+    )
+
+
+def prep_early(half, ids, thick, weight, base, feats, after, before, target, surface, perm):
+    blocks, rows = prep_call(
+        inner_kernel, "inner", 6,
+        (BLOCKS_OUT, jax.ShapeDtypeStruct((6 * 208, 256), BF16)),
+        (pl.BlockSpec(memory_space=pl.ANY), vmem()), [], {},
+        (half, ids, thick, weight, base, feats, target, surface, perm),
+    )
+    return prep_call(
+        outer_kernel, "outer", 2, BLOCKS_OUT, pl.BlockSpec(memory_space=pl.ANY), [], {9: 0},
+        (half, ids, thick, weight, base, after, before, rows, perm, blocks),
+    )
 
 
 def post_kernel(half_ref, x_ref, perm_ref, *refs):
@@ -590,11 +665,12 @@
         back = jnp.zeros((WIN, C), F32)
         c0 = 0.7978845608028654
         c1 = c0 * 0.044715
+        c2, c3 = -2.0 * LOG2E * c0, -2.0 * LOG2E * c1
         for f in range(3):
             at = slice(256 * f, 256 * f + 256)
             pre = dot(normed_two, expand_ref[:, at])
             u = u_row[:, at]
-            gate = 0.5 + 0.5 * jnp.tanh(pre * (c0 + c1 * (pre * pre)))
+            gate = 1.0 / (1.0 + jnp.exp2(pre * (c2 + c3 * (pre * pre))))
             unit = pre * gate
             acc = acc + unit * u
             pre, gate, unit = pre.astype(BF16), gate.astype(BF16), unit.astype(BF16)
@@ -775,11 +851,11 @@
     order_back = jnp.asarray(window_rows().T, BF16)
 
     made = [
-        prep(
+        step(
             half, window_pattern, thickness, level_weight, temp_base,
             feats, after, before, goal, ground, perm,
         )
-        for half in halves
+        for step, half in zip((prep_early, prep), halves)
     ]
     weights = (w_qkv, window_bias, patterns, attn_gain, mlp_gain, temp_head, w_reduce.T)
     weights, made[0] = lax.optimization_barrier((weights, made[0]))

time: 96.3 us -> 95.4 us (level)
  waiting for transfers between devices: 13.8 us -> 12.1 us
  Pallas kernels: 44.9 us -> 46.3 us
    ppermute x2, waiting for transfers between devices: 1.77 us -> 0.01 us  [block_step(): return lax.ppermute(value, 'tile', pairs)]
    pallas_call x2 -> x3, Pallas kernels: 4.7 us -> 6.09 us  [prep_call(): pl.pallas_call(kernel, out_shape=outs, in_specs=[smem()] * 5 + [vmem()] *...]
  transfers between devices with their start and end apart: 6 -> 6, of which waited for: 3 -> 2; matrix products, arithmetic and copies ran while one was open for 0% -> 0% of each run, Pallas kernels for 41% -> 44%
where the time goes in v5:
time: 95.4 us; the launch traced here: 94.8 us
  Pallas kernels  46.3 us (49%)
  starting transfers between devices  33.6 us (35%)
  waiting for transfers between devices  12.1 us (13%)
  local copies, waits for them, and re-layouts  1.61 us (2%)
  between operations  1.16 us (1%)
    pallas_call x2, Pallas kernels, layer(): pl.pallas_call(main_kernel, out_shape=jax.ShapeDtypeStruct((GROUP, ROWS,...  34.5 us
    all_to_all x4, starting transfers between devices, exchange(): lax.all_to_all(blocks, ('tile', 'lev'), 0, 0, axis_index_groups=pair_grou...  30.3 us
    all_to_all x4, waiting for transfers between devices, exchange(): lax.all_to_all(blocks, ('tile', 'lev'), 0, 0, axis_index_groups=pair_grou...  12.1 us
    pallas_call x3, Pallas kernels, prep_call(): pl.pallas_call(kernel, out_shape=outs, in_specs=[smem()] * 5 + [vmem()] *...  6.09 us
    ppermute x2, starting transfers between devices, block_step(): return lax.ppermute(value, 'tile', pairs)  3.24 us
    pallas_call x2, Pallas kernels, post(): pl.pallas_call(post_kernel, out_shape=(jax.ShapeDtypeStruct((2, 12, 1, LO...  2.92 us
    pallas_call x1, Pallas kernels, rim(): pl.pallas_call(rim_kernel, out_shape=(edge, edge), grid=(1,), in_specs=[s...  2.08 us
  transfers between devices with their start and end apart: 6, of which 2 were waited for; matrix products, arithmetic and copies ran while one was open for 0% of the time, Pallas kernels for 44%

profile of v5, /device:TPU:1, one launch (start us, length us, event | category | flops | bytes accessed | tf_op | source)
XLA Modules:
  0.0 94.8 jit_solution(6521831038861902877)
XLA Ops:
  0.7 0.0 copy-start.16
  0.7 2.1 %rim.1 = (bf16[96,256]{1,0:T(8,128)(2,1)}, bf16[96,256]{1,0:T(8,128)(2,1)}) custom-call(s32[4,15]{1,0:T(4,128)} %ids_ref.7, bf16[12,90,2,192]{3,2,1,0:T(2,128)(2,1)} %bitcast.14, bf16[12,90,2,192]{3,2,1,0:T(2,128)(2,1)} %bitcast.15, f32[2,12,1,90]{3,2,1,0:T(1,128)} %bitcast.18, f32[12,1,90]{2,1,0:T(1,128)} %bitcast.21), custom_call_target="tpu_custom_call" | custom-call | tf_op jit(solution)/shard_map/rim/pallas_call | solution.py:175
  2.8 3.2 %collective-permute-start = (bf16[96,256]{1,0:T(8,128)(2,1)}, bf16[96,256]{1,0:T(8,128)(2,1)S(1)}, u32[]{:S(2)}, u32[]{:S(2)}) collective-permute-start(bf16[96,256]{1,0:T(8,128)(2,1)} %get-tuple-element.24), channel_id=1, source_target_pairs={{0,12},{4,0},{8,4},{12,8},{16,28},{20,16},{24,20},{28,24},{32,44},... | collective-permute-start | bytes 147464 | tf_op jit(solution)/shard_map/ppermute | solution.py:830
  6.0 0.0 collective-permute-start.1
  6.1 2.2 %inner.1 = (bf16[8,240,128]{2,1,0:T(8,128)(2,1)}, bf16[1248,256]{1,0:T(8,128)(2,1)S(1)}) custom-call(s32[1]{0:T(128)} %bitcast.7.half_ref, s32[4,15]{1,0:T(4,128)S(1)} %copy-done.3, f32[2]{0:T(128)S(1)} %copy-done.12, f32[2]{0:T(128)S(1)} %copy-done.13, f32[2]{0:T(128)S(1)} %copy-done.14, bf16[12,90,2,192]{3,2,1,0:T(2,128)(2,1)S(1)} %bitcast.16, ...), custom_call_target="tpu_custom_call" | custom-call | flops 1000000000 | bytes 2500000 | tf_op jit(solution)/shard_map/inner/pallas_call | solution.py:309
  8.3 0.0 collective-permute-done.next_ref
  8.3 0.0 collective-permute-done.1.prev_ref
  8.3 0.0 copy-start.22
  8.4 0.0 copy-start.4
  8.4 0.0 copy-start.5
  8.4 0.0 copy-start.7
  8.4 0.0 copy-start.9
  8.4 0.0 copy-start.10
  8.4 0.0 copy-start.11
  8.4 1.5 %outer.1 = bf16[8,240,128]{2,1,0:T(8,128)(2,1)} custom-call(s32[1]{0:T(128)} %bitcast.7.half_ref, s32[4,15]{1,0:T(4,128)S(1)} %copy-done.3, f32[2]{0:T(128)S(1)} %copy-done.12, f32[2]{0:T(128)S(1)} %copy-done.13, f32[2]{0:T(128)S(1)} %copy-done.14, bf16[96,256]{1,0:T(8,128)(2,1)S(1)} %collective-permute-done.next_ref, ...), custom_call_target="tpu_custom_call", output_to_operand_aliasing={{}: (9, {})} | custom-call | flops 1000000000 | bytes 2500000 | tf_op jit(solution)/shard_map/outer/pallas_call | solution.py:309
  10.0 11.8 %all-to-all-start.2 = ((bf16[8,240,128]{2,1,0:T(8,128)(2,1)}), bf16[8,240,128]{2,1,0:T(8,128)(2,1)S(1)}, u32[]{:S(2)}, u32[]{:S(2)}) async-start(bf16[8,240,128]{2,1,0:T(8,128)(2,1)} %outer.1), calls=%async_computation.2 | async-start | bytes 983040 | tf_op jit(solution)/shard_map/all_to_all | solution.py:821
  21.9 0.7 setup.1
  22.6 0.0 copy-start.18
  22.7 0.8 copy-done.18
  23.4 0.7 copy-done.20
  24.2 2.3 %prep.1 = bf16[8,240,128]{2,1,0:T(8,128)(2,1)} custom-call(s32[1]{0:T(128)} %bitcast.half_ref, s32[4,15]{1,0:T(4,128)S(1)} %copy-done.3, f32[2]{0:T(128)S(1)} %copy-done.12, f32[2]{0:T(128)S(1)} %copy-done.13, f32[2]{0:T(128)S(1)} %copy-done.14, bf16[12,90,2,192]{3,2,1,0:T(2,128)(2,1)S(1)} %bitcast.17, bf16[96,256]{1,0:T(8,128)(2,1)S(1)} %collective-permute-done.next_ref, ...), custom_call_target="tpu_custom_call" | custom-call | flops 1000000000 | bytes 2500000 | tf_op jit(solution)/shard_map/prep/pallas_call | solution.py:309
  26.5 2.8 %all-to-all-done.2.x_ref = bf16[8,240,128]{2,1,0:T(8,128)(2,1)S(1)} async-done(((bf16[8,240,128]{2,1,0:T(8,128)(2,1)}), bf16[8,240,128]{2,1,0:T(8,128)(2,1)S(1)}, u32[]{:S(2)}, u32[]{:S(2)}) %all-to-all-start.2) | async-done | bytes 491552 | tf_op jit(solution)/shard_map/all_to_all | solution.py:821
  29.3 4.9 %all-to-all-start = ((bf16[8,240,128]{2,1,0:T(8,128)(2,1)}), bf16[8,240,128]{2,1,0:T(8,128)(2,1)S(1)}, u32[]{:S(2)}, u32[]{:S(2)}) async-start(bf16[8,240,128]{2,1,0:T(8,128)(2,1)} %prep.1), calls=%async_computation | async-start | bytes 983040 | tf_op jit(solution)/shard_map/all_to_all | solution.py:821
  34.2 17.3 %layer.3 = bf16[8,240,128]{2,1,0:T(8,128)(2,1)} custom-call(bf16[8,240,128]{2,1,0:T(8,128)(2,1)S(1)} %all-to-all-done.2.x_ref, bf16[144,144]{1,0:T(8,128)(2,1)S(1)} %copy-done.17, bf16[144,144]{1,0:T(8,128)(2,1)S(1)} %copy-done.17, bf16[576,192]{1,0:T(8,128)(2,1)S(1)} %copy-done.21, f32[144,896]{1,0:T(8,128)S(1)} %copy-done.19, ...), custom_call_target="tpu_custom_call" | custom-call | flops 20000000000 | bytes 4000000 | tf_op jit(solution)/shard_map/layer/pallas_call | solution.py:789
  51.5 0.0 all-to-all-done.x_ref
  51.5 9.6 %all-to-all-start.3 = ((bf16[8,240,128]{2,1,0:T(8,128)(2,1)}), bf16[8,240,128]{2,1,0:T(8,128)(2,1)S(1)}, u32[]{:S(2)}, u32[]{:S(2)}) async-start(bf16[8,240,128]{2,1,0:T(8,128)(2,1)} %layer.3), calls=%async_computation.3 | async-start | bytes 983040 | tf_op jit(solution)/shard_map/all_to_all | solution.py:821
  61.2 17.3 %layer.2 = bf16[8,240,128]{2,1,0:T(8,128)(2,1)} custom-call(bf16[8,240,128]{2,1,0:T(8,128)(2,1)S(1)} %all-to-all-done.x_ref, bf16[144,144]{1,0:T(8,128)(2,1)S(1)} %copy-done.17, bf16[144,144]{1,0:T(8,128)(2,1)S(1)} %copy-done.17, bf16[576,192]{1,0:T(8,128)(2,1)S(1)} %copy-done.21, f32[144,896]{1,0:T(8,128)S(1)} %copy-done.19, ...), custom_call_target="tpu_custom_call" | custom-call | flops 20000000000 | bytes 4000000 | tf_op jit(solution)/shard_map/layer/pallas_call | solution.py:789
  78.4 0.0 all-to-all-done.3.x_ref
  78.4 4.0 %all-to-all-start.1 = ((bf16[8,240,128]{2,1,0:T(8,128)(2,1)}), bf16[8,240,128]{2,1,0:T(8,128)(2,1)S(1)}, u32[]{:S(2)}, u32[]{:S(2)}) async-start(bf16[8,240,128]{2,1,0:T(8,128)(2,1)} %layer.2), calls=%async_computation.1 | async-start | bytes 983040 | tf_op jit(solution)/shard_map/all_to_all | solution.py:821
  82.4 1.5 %post.2 = (f32[2,12,1,90]{3,2,1,0:T(1,128)}, bf16[12,90,2,192]{3,2,1,0:T(2,128)(2,1)}) custom-call(s32[1]{0:T(128)} %bitcast.7.half_ref, bf16[8,240,128]{2,1,0:T(8,128)(2,1)S(1)} %all-to-all-done.3.x_ref, bf16[288,432]{1,0:T(8,128)(2,1)S(1)} %copy-done.15), custom_call_target="tpu_custom_call" | custom-call | flops 1000000000 | bytes 2500000 | tf_op jit(solution)/shard_map/post/pallas_call | solution.py:391
  83.9 9.3 %all-to-all-done.1.x_ref = bf16[8,240,128]{2,1,0:T(8,128)(2,1)S(1)} async-done(((bf16[8,240,128]{2,1,0:T(8,128)(2,1)}), bf16[8,240,128]{2,1,0:T(8,128)(2,1)S(1)}, u32[]{:S(2)}, u32[]{:S(2)}) %all-to-all-start.1) | async-done | bytes 491552 | tf_op jit(solution)/shard_map/all_to_all | solution.py:821
  93.2 1.5 %post.3 = (f32[2,12,1,90]{3,2,1,0:T(1,128)}, bf16[12,90,2,192]{3,2,1,0:T(2,128)(2,1)}) custom-call(s32[1]{0:T(128)} %bitcast.half_ref, bf16[8,240,128]{2,1,0:T(8,128)(2,1)S(1)} %all-to-all-done.1.x_ref, bf16[288,432]{1,0:T(8,128)(2,1)S(1)} %copy-done.15, f32[2,12,1,90]{3,2,1,0:T(1,128)} %get-tuple-element.42.refs_0_, ...), custom_call_target="tpu_custom_call", output_to_operand_aliasing={{0}: (3, {}), {1}: (4, {})} | custom-call | flops 1000000000 | bytes 2500000 | tf_op jit(solution)/shard_map/post/pallas_call | solution.py:391
  (36 shorter events, 0.1 us)
Async XLA Ops:
  0.6 5.4 %copy-start = (bf16[2,1,12,90,192]{4,0,3,2,1:T(2,128)(2,1)S(1)}, bf16[2,1,12,90,192]{4,0,3,2,1:T(2,128)(2,1)}, u32[]{:S(2)}) copy-start(bf16[2,1,12,90,192]{4,0,3,2,1:T(2,128)(2,1)} %param.20) | copy-start | bytes 2488324
  0.6 5.4 %copy-start.1 = (f32[2,1,12,90]{3,1,2,0:T(1,128)S(1)}, f32[2,1,12,90]{3,1,2,0:T(1,128)}, u32[]{:S(2)}) copy-start(f32[2,1,12,90]{3,1,2,0:T(1,128)} %param.35) | copy-start | bytes 25924
  0.7 5.4 %copy-start.2 = (f32[1,12,90]{2,0,1:T(1,128)S(1)}, f32[1,12,90]{2,0,1:T(1,128)}, u32[]{:S(2)}) copy-start(f32[1,12,90]{2,0,1:T(1,128)} %param.34) | copy-start | bytes 12964
  0.7 5.4 %copy-start.3 = (s32[4,15]{1,0:T(4,128)S(1)}, s32[4,15]{1,0:T(4,128)}, u32[]{:S(2)}) copy-start(s32[4,15]{1,0:T(4,128)} %ids_ref.7) | copy-start | bytes 724
  0.7 5.4 %copy-start.12 = (f32[2]{0:T(128)S(1)}, f32[2]{0:T(128)}, u32[]{:S(2)}) copy-start(f32[2]{0:T(128)} %thick_ref.5) | copy-start | bytes 28
  0.7 5.4 %copy-start.13 = (f32[2]{0:T(128)S(1)}, f32[2]{0:T(128)}, u32[]{:S(2)}) copy-start(f32[2]{0:T(128)} %weight_ref.5) | copy-start | bytes 28
  0.7 5.4 %copy-start.14 = (f32[2]{0:T(128)S(1)}, f32[2]{0:T(128)}, u32[]{:S(2)}) copy-start(f32[2]{0:T(128)} %base_ref.5) | copy-start | bytes 28
  0.7 5.4 %copy-start.16 = (bf16[288,384]{1,0:T(8,128)(2,1)S(1)}, bf16[288,384]{1,0:T(8,128)(2,1)}, u32[]{:S(2)}) copy-start(bf16[288,384]{1,0:T(8,128)(2,1)} %constant.48.clone.perm_ref) | copy-start | bytes 663556
  2.8 5.5 %collective-permute-start = (bf16[96,256]{1,0:T(8,128)(2,1)}, bf16[96,256]{1,0:T(8,128)(2,1)S(1)}, u32[]{:S(2)}, u32[]{:S(2)}) collective-permute-start(bf16[96,256]{1,0:T(8,128)(2,1)} %get-tuple-element.24), channel_id=1, source_target_pairs={{0,12},{4,0},{8,4},{12,8},{16,28},{20,16},{24,20},{28,24},{32,44},... | collective-permute-start | bytes 147464 | tf_op jit(solution)/shard_map/ppermute | solution.py:830
  6.0 2.3 %collective-permute-start.1 = (bf16[96,256]{1,0:T(8,128)(2,1)}, bf16[96,256]{1,0:T(8,128)(2,1)S(1)}, u32[]{:S(2)}, u32[]{:S(2)}) collective-permute-start(bf16[96,256]{1,0:T(8,128)(2,1)} %get-tuple-element.25), channel_id=1, source_target_pairs={{0,4},{4,8},{8,12},{12,0},{16,20},{20,24},{24,28},{28,16},{32,36},... | collective-permute-start | bytes 147464 | tf_op jit(solution)/shard_map/ppermute | solution.py:830
  8.3 13.5 %copy-start.22 = (bf16[192]{0:T(256)(128)(2,1)S(1)}, bf16[192]{0:T(256)(128)(2,1)}, u32[]{:S(2)}) copy-start(bf16[192]{0:T(256)(128)(2,1)} %param.30) | copy-start | bytes 1156
  8.4 13.5 %copy-start.4 = (f32[6,144,144]{2,1,0:T(8,128)S(1)}, f32[6,144,144]{2,1,0:T(8,128)}, u32[]{:S(2)}) copy-start(f32[6,144,144]{2,1,0:T(8,128)} %bias_ref) | copy-start | bytes 1492996
  8.4 13.5 %copy-start.5 = (bf16[768,192]{0,1:T(8,128)(2,1)S(1)}, bf16[768,192]{0,1:T(8,128)(2,1)}, u32[]{:S(2)}) copy-start(bf16[768,192]{0,1:T(8,128)(2,1)} %param.29) | copy-start | bytes 884740
  8.4 13.5 %copy-start.7 = (bf16[192,576]{1,0:T(8,128)(2,1)S(1)}, bf16[192,576]{1,0:T(8,128)(2,1)}, u32[]{:S(2)}) copy-start(bf16[192,576]{1,0:T(8,128)(2,1)} %w_ref) | copy-start | bytes 663556
  8.4 13.5 %copy-start.9 = (s32[8,144]{1,0:T(8,128)S(1)}, s32[8,144]{1,0:T(8,128)}, u32[]{:S(2)}) copy-start(s32[8,144]{1,0:T(8,128)} %pat_ref) | copy-start | bytes 13828
  8.4 13.5 %copy-start.10 = (f32[192]{0:T(256)S(1)}, f32[192]{0:T(256)}, u32[]{:S(2)}) copy-start(f32[192]{0:T(256)} %param.21) | copy-start | bytes 2308
  8.4 13.5 %copy-start.11 = (f32[192]{0:T(256)S(1)}, f32[192]{0:T(256)}, u32[]{:S(2)}) copy-start(f32[192]{0:T(256)} %param.27) | copy-start | bytes 2308
  10.0 19.4 %all-to-all-start.2 = ((bf16[8,240,128]{2,1,0:T(8,128)(2,1)}), bf16[8,240,128]{2,1,0:T(8,128)(2,1)S(1)}, u32[]{:S(2)}, u32[]{:S(2)}) async-start(bf16[8,240,128]{2,1,0:T(8,128)(2,1)} %outer.1), calls=%async_computation.2 | async-start | bytes 983040 | tf_op jit(solution)/shard_map/all_to_all | solution.py:821
  22.6 0.8 copy-start.18
  23.4 0.7 copy-start.20
  24.1 10.1 %copy-start.6 = (bf16[192,768]{1,0:T(8,128)(2,1)S(1)}, bf16[192,768]{1,0:T(8,128)(2,1)}, u32[]{:S(2)}) copy-start(bf16[192,768]{1,0:T(8,128)(2,1)} %expand_ref.3) | copy-start | bytes 884740
  24.2 10.1 %copy-start.8 = (bf16[192,192]{1,0:T(8,128)(2,1)S(1)}, bf16[192,192]{1,0:T(8,128)(2,1)}, u32[]{:S(2)}) copy-start(bf16[192,192]{1,0:T(8,128)(2,1)} %proj_ref.3) | copy-start | bytes 221188
  24.2 10.1 %copy-start.17 = (bf16[144,144]{1,0:T(8,128)(2,1)S(1)}, bf16[144,144]{1,0:T(8,128)(2,1)}, u32[]{:S(2)}) copy-start(bf16[144,144]{1,0:T(8,128)(2,1)} %constant.50.clone.order_ref.back_ref) | copy-start | bytes 124420
  24.2 10.1 %copy-start.19 = (f32[144,896]{1,0:T(8,128)S(1)}, f32[144,896]{1,0:T(8,128)}, u32[]{:S(2)}) copy-start(f32[144,896]{1,0:T(8,128)} %copy-done.18) | copy-start | bytes 1548292
  24.2 10.1 %copy-start.21 = (bf16[576,192]{1,0:T(8,128)(2,1)S(1)}, bf16[576,192]{1,0:T(8,128)(2,1)}, u32[]{:S(2)}) copy-start(bf16[576,192]{1,0:T(8,128)(2,1)} %copy-done.20) | copy-start | bytes 663556
  29.3 22.2 %all-to-all-start = ((bf16[8,240,128]{2,1,0:T(8,128)(2,1)}), bf16[8,240,128]{2,1,0:T(8,128)(2,1)S(1)}, u32[]{:S(2)}, u32[]{:S(2)}) async-start(bf16[8,240,128]{2,1,0:T(8,128)(2,1)} %prep.1), calls=%async_computation | async-start | bytes 983040 | tf_op jit(solution)/shard_map/all_to_all | solution.py:821
  51.5 26.9 %all-to-all-start.3 = ((bf16[8,240,128]{2,1,0:T(8,128)(2,1)}), bf16[8,240,128]{2,1,0:T(8,128)(2,1)S(1)}, u32[]{:S(2)}, u32[]{:S(2)}) async-start(bf16[8,240,128]{2,1,0:T(8,128)(2,1)} %layer.3), calls=%async_computation.3 | async-start | bytes 983040 | tf_op jit(solution)/shard_map/all_to_all | solution.py:821
  61.2 21.3 %copy-start.15 = (bf16[288,432]{1,0:T(8,128)(2,1)S(1)}, bf16[288,432]{1,0:T(8,128)(2,1)}, u32[]{:S(2)}) copy-start(bf16[288,432]{1,0:T(8,128)(2,1)} %constant.49.clone.perm_ref) | copy-start | bytes 746500
  78.4 14.7 %all-to-all-start.1 = ((bf16[8,240,128]{2,1,0:T(8,128)(2,1)}), bf16[8,240,128]{2,1,0:T(8,128)(2,1)S(1)}, u32[]{:S(2)}, u32[]{:S(2)}) async-start(bf16[8,240,128]{2,1,0:T(8,128)(2,1)} %layer.2), calls=%async_computation.1 | async-start | bytes 983040 | tf_op jit(solution)/shard_map/all_to_all | solution.py:821

commit v6 on v5

--- a/solution.py
+++ b/solution.py
@@ -713,7 +713,8 @@
         interleave(forward(p, 0), forward(p, 1))
         return carry
 
-    lax.fori_loop(0, 4, forward_step, 0)
+    for step in range(4):
+        forward_step(step, 0)
 
     def scalar(l, k):
         return levels_ref[l // 2, l % 2 : l % 2 + 1, 72 + k : 73 + k]
@@ -767,7 +768,8 @@
         interleave(backward(p, 0), backward(p, 1))
         return carry
 
-    lax.fori_loop(0, 4, backward_step, 0)
+    for step in range(4):
+        backward_step(step, 0)
 
     for p in range(4):
         for a in range(2):

time: 95.4 us -> 90 us (0.943)
  Pallas kernels: 46.3 us -> 40.9 us
    pallas_call x2, Pallas kernels: 34.5 us -> 29.1 us  [layer(): pl.pallas_call(main_kernel, out_shape=jax.ShapeDtypeStruct((GROUP, ROWS,...]
  transfers between devices with their start and end apart: 6 -> 6, of which waited for: 2 -> 2; matrix products, arithmetic and copies ran while one was open for 0% -> 0% of each run, Pallas kernels for 44% -> 40%
where the time goes in v6:
time: 90 us; the launch traced here: 89.4 us
  Pallas kernels  40.9 us (45%)
  starting transfers between devices  33.6 us (37%)
  waiting for transfers between devices  12.1 us (13%)
  local copies, waits for them, and re-layouts  1.61 us (2%)
  between operations  1.18 us (1%)
    all_to_all x4, starting transfers between devices, exchange(): lax.all_to_all(blocks, ('tile', 'lev'), 0, 0, axis_index_groups=pair_grou...  30.3 us
    pallas_call x2, Pallas kernels, layer(): pl.pallas_call(main_kernel, out_shape=jax.ShapeDtypeStruct((GROUP, ROWS,...  29.1 us
    all_to_all x4, waiting for transfers between devices, exchange(): lax.all_to_all(blocks, ('tile', 'lev'), 0, 0, axis_index_groups=pair_grou...  12.1 us
    pallas_call x3, Pallas kernels, prep_call(): pl.pallas_call(kernel, out_shape=outs, in_specs=[smem()] * 5 + [vmem()] *...  6.09 us
    ppermute x2, starting transfers between devices, block_step(): return lax.ppermute(value, 'tile', pairs)  3.24 us
    pallas_call x2, Pallas kernels, post(): pl.pallas_call(post_kernel, out_shape=(jax.ShapeDtypeStruct((2, 12, 1, LO...  2.92 us
    pallas_call x1, Pallas kernels, rim(): pl.pallas_call(rim_kernel, out_shape=(edge, edge), grid=(1,), in_specs=[s...  2.08 us
  transfers between devices with their start and end apart: 6, of which 2 were waited for; matrix products, arithmetic and copies ran while one was open for 0% of the time, Pallas kernels for 40%

profile of v6, /device:TPU:1, one launch (start us, length us, event | category | flops | bytes accessed | tf_op | source)
XLA Modules:
  0.0 89.4 jit_solution(18405389846981164818)
XLA Ops:
  0.7 0.0 copy-start.16
  0.7 2.1 %rim.1 = (bf16[96,256]{1,0:T(8,128)(2,1)}, bf16[96,256]{1,0:T(8,128)(2,1)}) custom-call(s32[4,15]{1,0:T(4,128)} %ids_ref.7, bf16[12,90,2,192]{3,2,1,0:T(2,128)(2,1)} %bitcast.14, bf16[12,90,2,192]{3,2,1,0:T(2,128)(2,1)} %bitcast.15, f32[2,12,1,90]{3,2,1,0:T(1,128)} %bitcast.18, f32[12,1,90]{2,1,0:T(1,128)} %bitcast.21), custom_call_target="tpu_custom_call" | custom-call | tf_op jit(solution)/shard_map/rim/pallas_call | solution.py:175
  2.8 3.2 %collective-permute-start = (bf16[96,256]{1,0:T(8,128)(2,1)}, bf16[96,256]{1,0:T(8,128)(2,1)S(1)}, u32[]{:S(2)}, u32[]{:S(2)}) collective-permute-start(bf16[96,256]{1,0:T(8,128)(2,1)} %get-tuple-element.24), channel_id=1, source_target_pairs={{0,12},{4,0},{8,4},{12,8},{16,28},{20,16},{24,20},{28,24},{32,44},... | collective-permute-start | bytes 147464 | tf_op jit(solution)/shard_map/ppermute | solution.py:832
  6.0 0.0 collective-permute-start.1
  6.1 2.2 %inner.1 = (bf16[8,240,128]{2,1,0:T(8,128)(2,1)}, bf16[1248,256]{1,0:T(8,128)(2,1)S(1)}) custom-call(s32[1]{0:T(128)} %bitcast.7.half_ref, s32[4,15]{1,0:T(4,128)S(1)} %copy-done.3, f32[2]{0:T(128)S(1)} %copy-done.12, f32[2]{0:T(128)S(1)} %copy-done.13, f32[2]{0:T(128)S(1)} %copy-done.14, bf16[12,90,2,192]{3,2,1,0:T(2,128)(2,1)S(1)} %bitcast.16, ...), custom_call_target="tpu_custom_call" | custom-call | flops 1000000000 | bytes 2500000 | tf_op jit(solution)/shard_map/inner/pallas_call | solution.py:309
  8.3 0.0 collective-permute-done.next_ref
  8.3 0.0 collective-permute-done.1.prev_ref
  8.3 0.0 copy-start.22
  8.4 0.0 copy-start.4
  8.4 0.0 copy-start.5
  8.4 0.0 copy-start.7
  8.4 0.0 copy-start.9
  8.4 0.0 copy-start.10
  8.4 0.0 copy-start.11
  8.4 1.5 %outer.1 = bf16[8,240,128]{2,1,0:T(8,128)(2,1)} custom-call(s32[1]{0:T(128)} %bitcast.7.half_ref, s32[4,15]{1,0:T(4,128)S(1)} %copy-done.3, f32[2]{0:T(128)S(1)} %copy-done.12, f32[2]{0:T(128)S(1)} %copy-done.13, f32[2]{0:T(128)S(1)} %copy-done.14, bf16[96,256]{1,0:T(8,128)(2,1)S(1)} %collective-permute-done.next_ref, ...), custom_call_target="tpu_custom_call", output_to_operand_aliasing={{}: (9, {})} | custom-call | flops 1000000000 | bytes 2500000 | tf_op jit(solution)/shard_map/outer/pallas_call | solution.py:309
  10.0 11.8 %all-to-all-start.2 = ((bf16[8,240,128]{2,1,0:T(8,128)(2,1)}), bf16[8,240,128]{2,1,0:T(8,128)(2,1)S(1)}, u32[]{:S(2)}, u32[]{:S(2)}) async-start(bf16[8,240,128]{2,1,0:T(8,128)(2,1)} %outer.1), calls=%async_computation.2 | async-start | bytes 983040 | tf_op jit(solution)/shard_map/all_to_all | solution.py:823
  21.9 0.7 setup.1
  22.6 0.0 copy-start.18
  22.7 0.8 copy-done.18
  23.4 0.7 copy-done.20
  24.2 2.3 %prep.1 = bf16[8,240,128]{2,1,0:T(8,128)(2,1)} custom-call(s32[1]{0:T(128)} %bitcast.half_ref, s32[4,15]{1,0:T(4,128)S(1)} %copy-done.3, f32[2]{0:T(128)S(1)} %copy-done.12, f32[2]{0:T(128)S(1)} %copy-done.13, f32[2]{0:T(128)S(1)} %copy-done.14, bf16[12,90,2,192]{3,2,1,0:T(2,128)(2,1)S(1)} %bitcast.17, bf16[96,256]{1,0:T(8,128)(2,1)S(1)} %collective-permute-done.next_ref, ...), custom_call_target="tpu_custom_call" | custom-call | flops 1000000000 | bytes 2500000 | tf_op jit(solution)/shard_map/prep/pallas_call | solution.py:309
  26.5 2.8 %all-to-all-done.2.x_ref = bf16[8,240,128]{2,1,0:T(8,128)(2,1)S(1)} async-done(((bf16[8,240,128]{2,1,0:T(8,128)(2,1)}), bf16[8,240,128]{2,1,0:T(8,128)(2,1)S(1)}, u32[]{:S(2)}, u32[]{:S(2)}) %all-to-all-start.2) | async-done | bytes 491552 | tf_op jit(solution)/shard_map/all_to_all | solution.py:823
  29.3 4.9 %all-to-all-start = ((bf16[8,240,128]{2,1,0:T(8,128)(2,1)}), bf16[8,240,128]{2,1,0:T(8,128)(2,1)S(1)}, u32[]{:S(2)}, u32[]{:S(2)}) async-start(bf16[8,240,128]{2,1,0:T(8,128)(2,1)} %prep.1), calls=%async_computation | async-start | bytes 983040 | tf_op jit(solution)/shard_map/all_to_all | solution.py:823
  34.2 14.6 %layer.3 = bf16[8,240,128]{2,1,0:T(8,128)(2,1)} custom-call(bf16[8,240,128]{2,1,0:T(8,128)(2,1)S(1)} %all-to-all-done.2.x_ref, bf16[144,144]{1,0:T(8,128)(2,1)S(1)} %copy-done.17, bf16[144,144]{1,0:T(8,128)(2,1)S(1)} %copy-done.17, bf16[576,192]{1,0:T(8,128)(2,1)S(1)} %copy-done.21, f32[144,896]{1,0:T(8,128)S(1)} %copy-done.19, ...), custom_call_target="tpu_custom_call" | custom-call | flops 20000000000 | bytes 4000000 | tf_op jit(solution)/shard_map/layer/pallas_call | solution.py:791
  48.9 0.0 all-to-all-done.x_ref
  48.9 9.6 %all-to-all-start.3 = ((bf16[8,240,128]{2,1,0:T(8,128)(2,1)}), bf16[8,240,128]{2,1,0:T(8,128)(2,1)S(1)}, u32[]{:S(2)}, u32[]{:S(2)}) async-start(bf16[8,240,128]{2,1,0:T(8,128)(2,1)} %layer.3), calls=%async_computation.3 | async-start | bytes 983040 | tf_op jit(solution)/shard_map/all_to_all | solution.py:823
  58.5 14.5 %layer.2 = bf16[8,240,128]{2,1,0:T(8,128)(2,1)} custom-call(bf16[8,240,128]{2,1,0:T(8,128)(2,1)S(1)} %all-to-all-done.x_ref, bf16[144,144]{1,0:T(8,128)(2,1)S(1)} %copy-done.17, bf16[144,144]{1,0:T(8,128)(2,1)S(1)} %copy-done.17, bf16[576,192]{1,0:T(8,128)(2,1)S(1)} %copy-done.21, f32[144,896]{1,0:T(8,128)S(1)} %copy-done.19, ...), custom_call_target="tpu_custom_call" | custom-call | flops 20000000000 | bytes 4000000 | tf_op jit(solution)/shard_map/layer/pallas_call | solution.py:791
  73.0 0.0 all-to-all-done.3.x_ref
  73.0 4.0 %all-to-all-start.1 = ((bf16[8,240,128]{2,1,0:T(8,128)(2,1)}), bf16[8,240,128]{2,1,0:T(8,128)(2,1)S(1)}, u32[]{:S(2)}, u32[]{:S(2)}) async-start(bf16[8,240,128]{2,1,0:T(8,128)(2,1)} %layer.2), calls=%async_computation.1 | async-start | bytes 983040 | tf_op jit(solution)/shard_map/all_to_all | solution.py:823
  77.0 1.5 %post.2 = (f32[2,12,1,90]{3,2,1,0:T(1,128)}, bf16[12,90,2,192]{3,2,1,0:T(2,128)(2,1)}) custom-call(s32[1]{0:T(128)} %bitcast.7.half_ref, bf16[8,240,128]{2,1,0:T(8,128)(2,1)S(1)} %all-to-all-done.3.x_ref, bf16[288,432]{1,0:T(8,128)(2,1)S(1)} %copy-done.15), custom_call_target="tpu_custom_call" | custom-call | flops 1000000000 | bytes 2500000 | tf_op jit(solution)/shard_map/post/pallas_call | solution.py:391
  78.5 9.3 %all-to-all-done.1.x_ref = bf16[8,240,128]{2,1,0:T(8,128)(2,1)S(1)} async-done(((bf16[8,240,128]{2,1,0:T(8,128)(2,1)}), bf16[8,240,128]{2,1,0:T(8,128)(2,1)S(1)}, u32[]{:S(2)}, u32[]{:S(2)}) %all-to-all-start.1) | async-done | bytes 491552 | tf_op jit(solution)/shard_map/all_to_all | solution.py:823
  87.7 1.5 %post.3 = (f32[2,12,1,90]{3,2,1,0:T(1,128)}, bf16[12,90,2,192]{3,2,1,0:T(2,128)(2,1)}) custom-call(s32[1]{0:T(128)} %bitcast.half_ref, bf16[8,240,128]{2,1,0:T(8,128)(2,1)S(1)} %all-to-all-done.1.x_ref, bf16[288,432]{1,0:T(8,128)(2,1)S(1)} %copy-done.15, f32[2,12,1,90]{3,2,1,0:T(1,128)} %get-tuple-element.42.refs_0_, ...), custom_call_target="tpu_custom_call", output_to_operand_aliasing={{0}: (3, {}), {1}: (4, {})} | custom-call | flops 1000000000 | bytes 2500000 | tf_op jit(solution)/shard_map/post/pallas_call | solution.py:391
  (36 shorter events, 0.1 us)
Async XLA Ops:
  0.6 5.4 %copy-start = (bf16[2,1,12,90,192]{4,0,3,2,1:T(2,128)(2,1)S(1)}, bf16[2,1,12,90,192]{4,0,3,2,1:T(2,128)(2,1)}, u32[]{:S(2)}) copy-start(bf16[2,1,12,90,192]{4,0,3,2,1:T(2,128)(2,1)} %param.20) | copy-start | bytes 2488324
  0.6 5.4 %copy-start.1 = (f32[2,1,12,90]{3,1,2,0:T(1,128)S(1)}, f32[2,1,12,90]{3,1,2,0:T(1,128)}, u32[]{:S(2)}) copy-start(f32[2,1,12,90]{3,1,2,0:T(1,128)} %param.35) | copy-start | bytes 25924
  0.7 5.4 %copy-start.2 = (f32[1,12,90]{2,0,1:T(1,128)S(1)}, f32[1,12,90]{2,0,1:T(1,128)}, u32[]{:S(2)}) copy-start(f32[1,12,90]{2,0,1:T(1,128)} %param.34) | copy-start | bytes 12964
  0.7 5.4 %copy-start.3 = (s32[4,15]{1,0:T(4,128)S(1)}, s32[4,15]{1,0:T(4,128)}, u32[]{:S(2)}) copy-start(s32[4,15]{1,0:T(4,128)} %ids_ref.7) | copy-start | bytes 724
  0.7 5.4 %copy-start.12 = (f32[2]{0:T(128)S(1)}, f32[2]{0:T(128)}, u32[]{:S(2)}) copy-start(f32[2]{0:T(128)} %thick_ref.5) | copy-start | bytes 28
  0.7 5.4 %copy-start.13 = (f32[2]{0:T(128)S(1)}, f32[2]{0:T(128)}, u32[]{:S(2)}) copy-start(f32[2]{0:T(128)} %weight_ref.5) | copy-start | bytes 28
  0.7 5.4 %copy-start.14 = (f32[2]{0:T(128)S(1)}, f32[2]{0:T(128)}, u32[]{:S(2)}) copy-start(f32[2]{0:T(128)} %base_ref.5) | copy-start | bytes 28
  0.7 5.4 %copy-start.16 = (bf16[288,384]{1,0:T(8,128)(2,1)S(1)}, bf16[288,384]{1,0:T(8,128)(2,1)}, u32[]{:S(2)}) copy-start(bf16[288,384]{1,0:T(8,128)(2,1)} %constant.48.clone.perm_ref) | copy-start | bytes 663556
  2.8 5.5 %collective-permute-start = (bf16[96,256]{1,0:T(8,128)(2,1)}, bf16[96,256]{1,0:T(8,128)(2,1)S(1)}, u32[]{:S(2)}, u32[]{:S(2)}) collective-permute-start(bf16[96,256]{1,0:T(8,128)(2,1)} %get-tuple-element.24), channel_id=1, source_target_pairs={{0,12},{4,0},{8,4},{12,8},{16,28},{20,16},{24,20},{28,24},{32,44},... | collective-permute-start | bytes 147464 | tf_op jit(solution)/shard_map/ppermute | solution.py:832
  6.0 2.3 %collective-permute-start.1 = (bf16[96,256]{1,0:T(8,128)(2,1)}, bf16[96,256]{1,0:T(8,128)(2,1)S(1)}, u32[]{:S(2)}, u32[]{:S(2)}) collective-permute-start(bf16[96,256]{1,0:T(8,128)(2,1)} %get-tuple-element.25), channel_id=1, source_target_pairs={{0,4},{4,8},{8,12},{12,0},{16,20},{20,24},{24,28},{28,16},{32,36},... | collective-permute-start | bytes 147464 | tf_op jit(solution)/shard_map/ppermute | solution.py:832
  8.3 13.5 %copy-start.22 = (bf16[192]{0:T(256)(128)(2,1)S(1)}, bf16[192]{0:T(256)(128)(2,1)}, u32[]{:S(2)}) copy-start(bf16[192]{0:T(256)(128)(2,1)} %param.30) | copy-start | bytes 1156
  8.4 13.5 %copy-start.4 = (f32[6,144,144]{2,1,0:T(8,128)S(1)}, f32[6,144,144]{2,1,0:T(8,128)}, u32[]{:S(2)}) copy-start(f32[6,144,144]{2,1,0:T(8,128)} %bias_ref) | copy-start | bytes 1492996
  8.4 13.5 %copy-start.5 = (bf16[768,192]{0,1:T(8,128)(2,1)S(1)}, bf16[768,192]{0,1:T(8,128)(2,1)}, u32[]{:S(2)}) copy-start(bf16[768,192]{0,1:T(8,128)(2,1)} %param.29) | copy-start | bytes 884740
  8.4 13.5 %copy-start.7 = (bf16[192,576]{1,0:T(8,128)(2,1)S(1)}, bf16[192,576]{1,0:T(8,128)(2,1)}, u32[]{:S(2)}) copy-start(bf16[192,576]{1,0:T(8,128)(2,1)} %w_ref) | copy-start | bytes 663556
  8.4 13.5 %copy-start.9 = (s32[8,144]{1,0:T(8,128)S(1)}, s32[8,144]{1,0:T(8,128)}, u32[]{:S(2)}) copy-start(s32[8,144]{1,0:T(8,128)} %pat_ref) | copy-start | bytes 13828
  8.4 13.5 %copy-start.10 = (f32[192]{0:T(256)S(1)}, f32[192]{0:T(256)}, u32[]{:S(2)}) copy-start(f32[192]{0:T(256)} %param.21) | copy-start | bytes 2308
  8.4 13.5 %copy-start.11 = (f32[192]{0:T(256)S(1)}, f32[192]{0:T(256)}, u32[]{:S(2)}) copy-start(f32[192]{0:T(256)} %param.27) | copy-start | bytes 2308
  10.0 19.4 %all-to-all-start.2 = ((bf16[8,240,128]{2,1,0:T(8,128)(2,1)}), bf16[8,240,128]{2,1,0:T(8,128)(2,1)S(1)}, u32[]{:S(2)}, u32[]{:S(2)}) async-start(bf16[8,240,128]{2,1,0:T(8,128)(2,1)} %outer.1), calls=%async_computation.2 | async-start | bytes 983040 | tf_op jit(solution)/shard_map/all_to_all | solution.py:823
  22.6 0.8 copy-start.18
  23.4 0.7 copy-start.20
  24.1 10.1 %copy-start.6 = (bf16[192,768]{1,0:T(8,128)(2,1)S(1)}, bf16[192,768]{1,0:T(8,128)(2,1)}, u32[]{:S(2)}) copy-start(bf16[192,768]{1,0:T(8,128)(2,1)} %expand_ref.3) | copy-start | bytes 884740
  24.2 10.1 %copy-start.8 = (bf16[192,192]{1,0:T(8,128)(2,1)S(1)}, bf16[192,192]{1,0:T(8,128)(2,1)}, u32[]{:S(2)}) copy-start(bf16[192,192]{1,0:T(8,128)(2,1)} %proj_ref.3) | copy-start | bytes 221188
  24.2 10.1 %copy-start.17 = (bf16[144,144]{1,0:T(8,128)(2,1)S(1)}, bf16[144,144]{1,0:T(8,128)(2,1)}, u32[]{:S(2)}) copy-start(bf16[144,144]{1,0:T(8,128)(2,1)} %constant.50.clone.order_ref.back_ref) | copy-start | bytes 124420
  24.2 10.1 %copy-start.19 = (f32[144,896]{1,0:T(8,128)S(1)}, f32[144,896]{1,0:T(8,128)}, u32[]{:S(2)}) copy-start(f32[144,896]{1,0:T(8,128)} %copy-done.18) | copy-start | bytes 1548292
  24.2 10.1 %copy-start.21 = (bf16[576,192]{1,0:T(8,128)(2,1)S(1)}, bf16[576,192]{1,0:T(8,128)(2,1)}, u32[]{:S(2)}) copy-start(bf16[576,192]{1,0:T(8,128)(2,1)} %copy-done.20) | copy-start | bytes 663556
  29.3 19.6 %all-to-all-start = ((bf16[8,240,128]{2,1,0:T(8,128)(2,1)}), bf16[8,240,128]{2,1,0:T(8,128)(2,1)S(1)}, u32[]{:S(2)}, u32[]{:S(2)}) async-start(bf16[8,240,128]{2,1,0:T(8,128)(2,1)} %prep.1), calls=%async_computation | async-start | bytes 983040 | tf_op jit(solution)/shard_map/all_to_all | solution.py:823
  48.9 24.1 %all-to-all-start.3 = ((bf16[8,240,128]{2,1,0:T(8,128)(2,1)}), bf16[8,240,128]{2,1,0:T(8,128)(2,1)S(1)}, u32[]{:S(2)}, u32[]{:S(2)}) async-start(bf16[8,240,128]{2,1,0:T(8,128)(2,1)} %layer.3), calls=%async_computation.3 | async-start | bytes 983040 | tf_op jit(solution)/shard_map/all_to_all | solution.py:823
  58.5 18.5 %copy-start.15 = (bf16[288,432]{1,0:T(8,128)(2,1)S(1)}, bf16[288,432]{1,0:T(8,128)(2,1)}, u32[]{:S(2)}) copy-start(bf16[288,432]{1,0:T(8,128)(2,1)} %constant.49.clone.perm_ref) | copy-start | bytes 746500
  73.0 14.7 %all-to-all-start.1 = ((bf16[8,240,128]{2,1,0:T(8,128)(2,1)}), bf16[8,240,128]{2,1,0:T(8,128)(2,1)S(1)}, u32[]{:S(2)}, u32[]{:S(2)}) async-start(bf16[8,240,128]{2,1,0:T(8,128)(2,1)} %layer.2), calls=%async_computation.1 | async-start | bytes 983040 | tf_op jit(solution)/shard_map/all_to_all | solution.py:823
